TPU v7x, 32 devices: a whole 2x2x4 slice. The times are simulated.
32 devices in a mesh: freq: 4 (over x, core), space: 8 (over z, y).
Axes of the slice: x: 2, y: 2, z: 4, core: 2. Of those that a mesh axis runs over, the one named last changes fastest.
Arguments:
- saved_modes: bfloat16 [4, 4, 2, 2, 3, 128, 128, 128], P('freq', None, None, None, None, 'space'), may hold values from -6 to 6
- mode_gains: float32 [4, 4], P('freq'), may hold values from 0.5 to 4
Outputs:
- smoothed_gradient: float32 [128, 128, 128], P('space', 'freq')
All inputs are finite; a program needn't handle non-finite values.
Results may differ from a plain program's by a relative error of at most 0.0003.
Values may be sent and summed in bfloat16 or wider, within the bound.
No kernel may reach another device: no remote copies, remote signals or barrier semaphores. Data moves between devices by JAX's collectives and lax.ppermute only.
A program may use at most 256 MiB of HBM per device.

v0:
```python
import jax
import jax.numpy as jnp
from jax import lax
from jax.sharding import PartitionSpec as P

AXIAL = 0.35
CROSS = 0.06


def padded_2(block, sides, width):
    for axis, dim in sides:
        count = lax.axis_size(axis)
        forward = [(i, i + 1) for i in range(count - 1)]
        backward = [(target, source) for source, target in forward]
        low = lax.ppermute(
            lax.slice_in_dim(block, block.shape[dim] - width, None, axis=dim), axis, forward
        )
        high = lax.ppermute(lax.slice_in_dim(block, 0, width, axis=dim), axis, backward)
        block = jnp.concatenate([low, block, high], axis=dim)
    return block


def shift_z(grid_values, upward):
    zero_plane = jnp.zeros(grid_values.shape[:-1] + (1,), grid_values.dtype)
    if upward:
        return jnp.concatenate([grid_values[..., 1:], zero_plane], axis=-1)
    return jnp.concatenate([zero_plane, grid_values[..., :-1]], axis=-1)


def central_diffs(padded):
    center = padded[:, :, 1:-1, 1:-1]
    along_x = (padded[:, :, 2:, 1:-1] - padded[:, :, :-2, 1:-1]) * 0.5
    along_y = (padded[:, :, 1:-1, 2:] - padded[:, :, 1:-1, :-2]) * 0.5
    along_z = (shift_z(center, True) - shift_z(center, False)) * 0.5
    return (along_x, along_y, along_z)


def strain_dot(grad_forward, grad_adjoint):
    running = jnp.zeros(grad_forward[0].shape[2:], jnp.float32)
    for row_axis in range(3):
        for col_axis in range(3):
            strain_u = 0.5 * (
                grad_forward[row_axis][:, col_axis] + grad_forward[col_axis][:, row_axis]
            )
            strain_v = 0.5 * (
                grad_adjoint[row_axis][:, col_axis] + grad_adjoint[col_axis][:, row_axis]
            )
            running = running + jnp.sum(strain_u * strain_v, axis=0)
    return running


def accumulate(padded, weights, factor):
    mode_count = padded.shape[1]
    pair_total = padded.shape[0] * mode_count
    row_total = padded.shape[6]
    grid_shape = (padded.shape[5] - 2, row_total, padded.shape[7])

    def one_pair(pair_index, running):
        freq_index = pair_index // mode_count
        mode_index = pair_index % mode_count
        mode_pair = lax.dynamic_index_in_dim(padded, freq_index, 0, False)
        mode_pair = lax.dynamic_index_in_dim(mode_pair, mode_index, 0, False).astype(jnp.float32)
        mode_pair = jnp.pad(mode_pair, ((0, 0), (0, 0), (0, 0), (0, 0), (1, 1), (0, 0)))
        weight = lax.dynamic_index_in_dim(
            lax.dynamic_index_in_dim(weights, freq_index, 0, False), mode_index, 0, False
        )
        return running + factor * weight * strain_dot(
            central_diffs(mode_pair[0]), central_diffs(mode_pair[1])
        )

    return lax.fori_loop(0, pair_total, one_pair, jnp.zeros(grid_shape, jnp.float32))


def smooth_step(padded):
    center = padded[1:-1, 1:-1]
    axial = padded[2:, 1:-1] + padded[:-2, 1:-1] - 2.0 * center
    cross = (
        padded[1:-1, 2:]
        + padded[1:-1, :-2]
        + shift_z(center, True)
        + shift_z(center, False)
        - 4.0 * center
    )
    return center + AXIAL * axial + CROSS * cross


def deep_smooth(grid_values):
    slab_rows = grid_values.shape[0]
    band_rows = grid_values.shape[1]
    first_x = lax.axis_index("space") * slab_rows - 3
    total_x = slab_rows * lax.axis_size("space")
    padded = padded_2(grid_values, (("freq", 1), ("space", 0)), 3)
    first_y = lax.axis_index("freq") * band_rows - 3
    total_y = band_rows * lax.axis_size("freq")
    for sweep in range(3):
        padded = smooth_step(padded)
        global_x = first_x + sweep + 1 + jnp.arange(padded.shape[0], dtype=jnp.int32)
        global_y = first_y + sweep + 1 + jnp.arange(padded.shape[1], dtype=jnp.int32)
        valid_x = (global_x >= 0) & (global_x < total_x)
        valid_y = (global_y >= 0) & (global_y < total_y)
        padded = jnp.where(valid_x[:, None, None] & valid_y[None, :, None], padded, 0.0)
    return padded


def smooth(grid_values):
    return deep_smooth(grid_values)


def local(saved_modes, mode_gains):
    mode_count = saved_modes.shape[1]
    freq_total = saved_modes.shape[0] * lax.axis_size("freq")
    factor = -2.0 / (freq_total * mode_count)
    padded = padded_2(saved_modes, (("space", 5),), 1)
    partial_terms = accumulate(padded, mode_gains, factor)
    summed = lax.psum(partial_terms, "freq")
    band_rows = summed.shape[1] // lax.axis_size("freq")
    sensitivity = lax.dynamic_slice_in_dim(summed, lax.axis_index("freq") * band_rows, band_rows, 1)
    return smooth(sensitivity)


def solution(mesh):
    in_specs = (P("freq", None, None, None, None, "space", None, None), P("freq", None))
    out_specs = P("space", "freq", None)
    return jax.shard_map(local, mesh=mesh, in_specs=in_specs, out_specs=out_specs, check_vma=False)
```

profile of v0, /device:TPU:0, one launch (start us, length us, event | category | flops | bytes accessed | tf_op | source)
XLA Modules:
  0.0 585.8 jit_solution(15557384201011643526)
XLA Ops:
  6.5 3.9 fusion.58
  10.5 5.0 collective-permute-start
  15.4 1.3 collective-permute-start.1
  19.5 63.5 %collective-permute-done = bf16[1,4,2,2,3,1,128,128]{7,6,5,4,3,2,1,0:T(8,128)(2,1)S(1)} collective-permute-done((bf16[1,4,2,2,3,1,128,128]{7,6,5,4,3,2,1,0:T(8,128)(2,1)}, bf16[1,4,2,2,3,1,128,128]{7,6,5,4,3,2,1,0:T(8,128)(2,1)S(1)}, u32[]{:S(2)}, u32[]{:S(2)}) %collective-permute-start) | collective-permute-done | bytes 1572896 | tf_op jit(solution)/shard_map/ppermute | solution.py:15
  83.0 18.4 %pad_maximum_fusion = bf16[1,4,2,2,3,18,128,128]{7,6,5,4,3,2,1,0:T(8,128)(2,1)} fusion(bf16[1,4,2,2,3,1,128,128]{7,6,5,4,3,2,1,0:T(8,128)(2,1)S(1)} %collective-permute-done.1, bf16[1,4,2,2,3,16,128,128]{7,6,5,4,3,2,1,0:T(8,128)(2,1)} %param.4, bf16[1,4,2,2,3,1,128,128]{7,6,5,4,3,2,1,0:T(8,128)(2,1)S(1)} %collective-permute-done), kind=kLoop, calls=%fused_computation.52 | loop fusion | flops 28311552 | bytes 56623104 | tf_op jit(solution)/shard_map/concatenate | solution.py:19
  101.5 421.1 %while.16 = (s32[]{:T(128)}, f32[16,128,128]{2,1,0:T(8,128)}, f32[1,4]{1,0:T(1,128)S(1)}, bf16[1,4,2,2,3,18,128,128]{7,6,5,4,3,2,1,0:T(8,128)(2,1)}, s32[]{:T(128)}, /*index=5*/s32[]{:T(128)}, s32[]{:T(128)}, s32[]{:T(128)}) while((s32[]{:T(128)}, f32[16,128,128]{2,1,0:T(8,128)}, f32[1,4]{1,0:T(1,128)S(1)}, ...), condition=%wide.region_7.8_spmd.clone, body=%wide.region_0.7_spmd.clone.sunk | while | flops 42653704 | bytes 329720032 | solution.py:71
  101.5 4.6 dynamic-slice_bitcast_fusion.2
  106.1 8.9 %pad_convert_fusion.2 = f32[2,2,3,18,130,128]{5,4,3,2,1,0:T(8,128)} fusion(bf16[2,2,3,18,128,128]{5,4,3,2,1,0:T(8,128)(2,1)S(1)} %dynamic-slice_bitcast_fusion.2), kind=kLoop, calls=%fused_computation.2.clone.1 | loop fusion | flops 3594240 | bytes 21454848 | tf_op jit(solution)/shard_map/while/body/eval_jaxpr/jit(_pad)/pad | solution.py:63
  115.0 11.5 %slice_bitcast_fusion.3 = (f32[2,3,18,130,128]{4,3,2,1,0:T(8,128)}, f32[2,3,18,130,128]{4,3,2,1,0:T(8,128)}) fusion(f32[2,2,3,18,130,128]{5,4,3,2,1,0:T(8,128)} %pad_convert_fusion.2), kind=kLoop, calls=%fused_computation.1.clone.1 | loop fusion | bytes 28753920 | tf_op jit(solution)/shard_map/while/body/eval_jaxpr/squeeze | solution.py:68
  126.5 17.1 %fusion.67 = (f32[2,3,16,128,127]{4,3,2,1,0:T(8,128)}, f32[2,3,16,128,127]{4,3,2,1,0:T(8,128)}, f32[2,3,16,128,127]{4,3,2,1,0:T(8,128)}, f32[2,3,16,128,127]{4,3,2,1,0:T(8,128)}) fusion(f32[2,3,18,130,128]{4,3,2,1,0:T(8,128)} %get-tuple-element.215, f32[2,3,18,130,128]{4,3,2,1,0:T(8,128)} %get-tuple-element.214), kind=kLoop, calls=%fused_computation.102.clone.1 | loop fusion | bytes 49938432 | tf_op jit(solution)/shard_map/while/body/eval_jaxpr/slice | solution.py:26
  143.6 9.4 %subtract_multiply_fusion.5 = f32[2,3,16,128,128]{4,3,2,1,0:T(8,128)} fusion(f32[2,3,16,128,127]{4,3,2,1,0:T(8,128)} %get-tuple-element.220, f32[2,3,16,128,127]{4,3,2,1,0:T(8,128)} %get-tuple-element.221), kind=kLoop, calls=%fused_computation.13.clone.1 | loop fusion | flops 3145728 | bytes 18776064 | tf_op jit(solution)/shard_map/while/body/eval_jaxpr/mul | solution.py:34
  153.4 4.4 subtract_multiply_fusion.4
  157.8 27.4 %fusion.66 = (f32[2,3,16,128,128]{4,3,2,1,0:T(8,128)}, f32[2,3,16,128,128]{4,3,2,1,0:T(8,128)}, f32[2,3,16,128,128]{4,3,2,1,0:T(8,128)}, f32[2,3,16,128,128]{4,3,2,1,0:T(8,128)}) fusion(f32[2,3,18,130,128]{4,3,2,1,0:T(8,128)} %get-tuple-element.214, f32[2,3,18,130,128]{4,3,2,1,0:T(8,128)} %get-tuple-element.215), kind=kLoop, calls=%fused_computation.5.clone.1 | loop fusion | flops 12582912 | bytes 75497472 | tf_op jit(solution)/shard_map/while/body/eval_jaxpr/mul | solution.py:33
  185.2 16.5 %fusion.68 = (f32[16,128,128]{2,1,0:T(8,128)S(1)}, f32[16,128,128]{2,1,0:T(8,128)S(1)}, f32[16,128,128]{2,1,0:T(8,128)S(1)}, f32[16,128,128]{2,1,0:T(8,128)}, f3...) fusion(f32[2,3,16,128,128]{4,3,2,1,0:T(8,128)} %get-tuple-element.216, ...), kind=kLoop, calls=%fused_computation.47.clone.1 | loop fusion | flops 17301504 | bytes 44040192 | tf_op jit(solution)/shard_map/while/body/eval_jaxpr/reduce_sum | solution.py:48
  202.3 4.2 select_add_fusion.2
  206.5 4.6 dynamic-slice_bitcast_fusion.2
  211.1 8.9 %pad_convert_fusion.2 = f32[2,2,3,18,130,128]{5,4,3,2,1,0:T(8,128)} fusion(bf16[2,2,3,18,128,128]{5,4,3,2,1,0:T(8,128)(2,1)S(1)} %dynamic-slice_bitcast_fusion.2), kind=kLoop, calls=%fused_computation.2.clone.1 | loop fusion | flops 3594240 | bytes 21454848 | tf_op jit(solution)/shard_map/while/body/eval_jaxpr/jit(_pad)/pad | solution.py:63
  220.0 11.5 %slice_bitcast_fusion.3 = (f32[2,3,18,130,128]{4,3,2,1,0:T(8,128)}, f32[2,3,18,130,128]{4,3,2,1,0:T(8,128)}) fusion(f32[2,2,3,18,130,128]{5,4,3,2,1,0:T(8,128)} %pad_convert_fusion.2), kind=kLoop, calls=%fused_computation.1.clone.1 | loop fusion | bytes 28753920 | tf_op jit(solution)/shard_map/while/body/eval_jaxpr/squeeze | solution.py:68
  231.5 17.1 %fusion.67 = (f32[2,3,16,128,127]{4,3,2,1,0:T(8,128)}, f32[2,3,16,128,127]{4,3,2,1,0:T(8,128)}, f32[2,3,16,128,127]{4,3,2,1,0:T(8,128)}, f32[2,3,16,128,127]{4,3,2,1,0:T(8,128)}) fusion(f32[2,3,18,130,128]{4,3,2,1,0:T(8,128)} %get-tuple-element.215, f32[2,3,18,130,128]{4,3,2,1,0:T(8,128)} %get-tuple-element.214), kind=kLoop, calls=%fused_computation.102.clone.1 | loop fusion | bytes 49938432 | tf_op jit(solution)/shard_map/while/body/eval_jaxpr/slice | solution.py:26
  248.6 9.4 %subtract_multiply_fusion.5 = f32[2,3,16,128,128]{4,3,2,1,0:T(8,128)} fusion(f32[2,3,16,128,127]{4,3,2,1,0:T(8,128)} %get-tuple-element.220, f32[2,3,16,128,127]{4,3,2,1,0:T(8,128)} %get-tuple-element.221), kind=kLoop, calls=%fused_computation.13.clone.1 | loop fusion | flops 3145728 | bytes 18776064 | tf_op jit(solution)/shard_map/while/body/eval_jaxpr/mul | solution.py:34
  258.4 4.4 subtract_multiply_fusion.4
  262.8 27.4 %fusion.66 = (f32[2,3,16,128,128]{4,3,2,1,0:T(8,128)}, f32[2,3,16,128,128]{4,3,2,1,0:T(8,128)}, f32[2,3,16,128,128]{4,3,2,1,0:T(8,128)}, f32[2,3,16,128,128]{4,3,2,1,0:T(8,128)}) fusion(f32[2,3,18,130,128]{4,3,2,1,0:T(8,128)} %get-tuple-element.214, f32[2,3,18,130,128]{4,3,2,1,0:T(8,128)} %get-tuple-element.215), kind=kLoop, calls=%fused_computation.5.clone.1 | loop fusion | flops 12582912 | bytes 75497472 | tf_op jit(solution)/shard_map/while/body/eval_jaxpr/mul | solution.py:33
  290.2 16.5 %fusion.68 = (f32[16,128,128]{2,1,0:T(8,128)S(1)}, f32[16,128,128]{2,1,0:T(8,128)S(1)}, f32[16,128,128]{2,1,0:T(8,128)S(1)}, f32[16,128,128]{2,1,0:T(8,128)}, f3...) fusion(f32[2,3,16,128,128]{4,3,2,1,0:T(8,128)} %get-tuple-element.216, ...), kind=kLoop, calls=%fused_computation.47.clone.1 | loop fusion | flops 17301504 | bytes 44040192 | tf_op jit(solution)/shard_map/while/body/eval_jaxpr/reduce_sum | solution.py:48
  307.3 4.5 select_add_fusion.2
  311.8 4.6 dynamic-slice_bitcast_fusion.2
  316.4 8.9 %pad_convert_fusion.2 = f32[2,2,3,18,130,128]{5,4,3,2,1,0:T(8,128)} fusion(bf16[2,2,3,18,128,128]{5,4,3,2,1,0:T(8,128)(2,1)S(1)} %dynamic-slice_bitcast_fusion.2), kind=kLoop, calls=%fused_computation.2.clone.1 | loop fusion | flops 3594240 | bytes 21454848 | tf_op jit(solution)/shard_map/while/body/eval_jaxpr/jit(_pad)/pad | solution.py:63
  325.3 11.5 %slice_bitcast_fusion.3 = (f32[2,3,18,130,128]{4,3,2,1,0:T(8,128)}, f32[2,3,18,130,128]{4,3,2,1,0:T(8,128)}) fusion(f32[2,2,3,18,130,128]{5,4,3,2,1,0:T(8,128)} %pad_convert_fusion.2), kind=kLoop, calls=%fused_computation.1.clone.1 | loop fusion | bytes 28753920 | tf_op jit(solution)/shard_map/while/body/eval_jaxpr/squeeze | solution.py:68
  336.9 17.1 %fusion.67 = (f32[2,3,16,128,127]{4,3,2,1,0:T(8,128)}, f32[2,3,16,128,127]{4,3,2,1,0:T(8,128)}, f32[2,3,16,128,127]{4,3,2,1,0:T(8,128)}, f32[2,3,16,128,127]{4,3,2,1,0:T(8,128)}) fusion(f32[2,3,18,130,128]{4,3,2,1,0:T(8,128)} %get-tuple-element.215, f32[2,3,18,130,128]{4,3,2,1,0:T(8,128)} %get-tuple-element.214), kind=kLoop, calls=%fused_computation.102.clone.1 | loop fusion | bytes 49938432 | tf_op jit(solution)/shard_map/while/body/eval_jaxpr/slice | solution.py:26
  354.0 9.4 %subtract_multiply_fusion.5 = f32[2,3,16,128,128]{4,3,2,1,0:T(8,128)} fusion(f32[2,3,16,128,127]{4,3,2,1,0:T(8,128)} %get-tuple-element.220, f32[2,3,16,128,127]{4,3,2,1,0:T(8,128)} %get-tuple-element.221), kind=kLoop, calls=%fused_computation.13.clone.1 | loop fusion | flops 3145728 | bytes 18776064 | tf_op jit(solution)/shard_map/while/body/eval_jaxpr/mul | solution.py:34
  363.7 4.4 subtract_multiply_fusion.4
  368.1 27.4 %fusion.66 = (f32[2,3,16,128,128]{4,3,2,1,0:T(8,128)}, f32[2,3,16,128,128]{4,3,2,1,0:T(8,128)}, f32[2,3,16,128,128]{4,3,2,1,0:T(8,128)}, f32[2,3,16,128,128]{4,3,2,1,0:T(8,128)}) fusion(f32[2,3,18,130,128]{4,3,2,1,0:T(8,128)} %get-tuple-element.214, f32[2,3,18,130,128]{4,3,2,1,0:T(8,128)} %get-tuple-element.215), kind=kLoop, calls=%fused_computation.5.clone.1 | loop fusion | flops 12582912 | bytes 75497472 | tf_op jit(solution)/shard_map/while/body/eval_jaxpr/mul | solution.py:33
  395.6 16.5 %fusion.68 = (f32[16,128,128]{2,1,0:T(8,128)S(1)}, f32[16,128,128]{2,1,0:T(8,128)S(1)}, f32[16,128,128]{2,1,0:T(8,128)S(1)}, f32[16,128,128]{2,1,0:T(8,128)}, f3...) fusion(f32[2,3,16,128,128]{4,3,2,1,0:T(8,128)} %get-tuple-element.216, ...), kind=kLoop, calls=%fused_computation.47.clone.1 | loop fusion | flops 17301504 | bytes 44040192 | tf_op jit(solution)/shard_map/while/body/eval_jaxpr/reduce_sum | solution.py:48
  412.7 4.5 select_add_fusion.2
  417.2 4.6 dynamic-slice_bitcast_fusion.2
  421.8 8.9 %pad_convert_fusion.2 = f32[2,2,3,18,130,128]{5,4,3,2,1,0:T(8,128)} fusion(bf16[2,2,3,18,128,128]{5,4,3,2,1,0:T(8,128)(2,1)S(1)} %dynamic-slice_bitcast_fusion.2), kind=kLoop, calls=%fused_computation.2.clone.1 | loop fusion | flops 3594240 | bytes 21454848 | tf_op jit(solution)/shard_map/while/body/eval_jaxpr/jit(_pad)/pad | solution.py:63
  430.7 11.5 %slice_bitcast_fusion.3 = (f32[2,3,18,130,128]{4,3,2,1,0:T(8,128)}, f32[2,3,18,130,128]{4,3,2,1,0:T(8,128)}) fusion(f32[2,2,3,18,130,128]{5,4,3,2,1,0:T(8,128)} %pad_convert_fusion.2), kind=kLoop, calls=%fused_computation.1.clone.1 | loop fusion | bytes 28753920 | tf_op jit(solution)/shard_map/while/body/eval_jaxpr/squeeze | solution.py:68
  442.2 17.1 %fusion.67 = (f32[2,3,16,128,127]{4,3,2,1,0:T(8,128)}, f32[2,3,16,128,127]{4,3,2,1,0:T(8,128)}, f32[2,3,16,128,127]{4,3,2,1,0:T(8,128)}, f32[2,3,16,128,127]{4,3,2,1,0:T(8,128)}) fusion(f32[2,3,18,130,128]{4,3,2,1,0:T(8,128)} %get-tuple-element.215, f32[2,3,18,130,128]{4,3,2,1,0:T(8,128)} %get-tuple-element.214), kind=kLoop, calls=%fused_computation.102.clone.1 | loop fusion | bytes 49938432 | tf_op jit(solution)/shard_map/while/body/eval_jaxpr/slice | solution.py:26
  459.3 9.4 %subtract_multiply_fusion.5 = f32[2,3,16,128,128]{4,3,2,1,0:T(8,128)} fusion(f32[2,3,16,128,127]{4,3,2,1,0:T(8,128)} %get-tuple-element.220, f32[2,3,16,128,127]{4,3,2,1,0:T(8,128)} %get-tuple-element.221), kind=kLoop, calls=%fused_computation.13.clone.1 | loop fusion | flops 3145728 | bytes 18776064 | tf_op jit(solution)/shard_map/while/body/eval_jaxpr/mul | solution.py:34
  469.0 4.4 subtract_multiply_fusion.4
  473.5 27.4 %fusion.66 = (f32[2,3,16,128,128]{4,3,2,1,0:T(8,128)}, f32[2,3,16,128,128]{4,3,2,1,0:T(8,128)}, f32[2,3,16,128,128]{4,3,2,1,0:T(8,128)}, f32[2,3,16,128,128]{4,3,2,1,0:T(8,128)}) fusion(f32[2,3,18,130,128]{4,3,2,1,0:T(8,128)} %get-tuple-element.214, f32[2,3,18,130,128]{4,3,2,1,0:T(8,128)} %get-tuple-element.215), kind=kLoop, calls=%fused_computation.5.clone.1 | loop fusion | flops 12582912 | bytes 75497472 | tf_op jit(solution)/shard_map/while/body/eval_jaxpr/mul | solution.py:33
  500.9 16.5 %fusion.68 = (f32[16,128,128]{2,1,0:T(8,128)S(1)}, f32[16,128,128]{2,1,0:T(8,128)S(1)}, f32[16,128,128]{2,1,0:T(8,128)S(1)}, f32[16,128,128]{2,1,0:T(8,128)}, f3...) fusion(f32[2,3,16,128,128]{4,3,2,1,0:T(8,128)} %get-tuple-element.216, ...), kind=kLoop, calls=%fused_computation.47.clone.1 | loop fusion | flops 17301504 | bytes 44040192 | tf_op jit(solution)/shard_map/while/body/eval_jaxpr/reduce_sum | solution.py:48
  518.0 4.5 select_add_fusion.2
  522.7 38.1 %all-reduce.13.cloned.1.call-done = f32[16,128,128]{2,1,0:T(8,128)} async-done(((f32[16,128,128]{2,1,0:T(8,128)}), f32[16,128,128]{2,1,0:T(8,128)}) %all-reduce.13.cloned.1.call-update) | async-done | bytes 1048592 | tf_op jit(solution)/shard_map/psum | solution.py:115
  561.7 1.5 collective-permute-start.2
  563.2 1.3 collective-permute-start.3
  565.5 1.7 collective-permute-done.3
  567.3 3.4 collective-permute-start.4
  572.5 4.3 collective-permute-done.5
  (58 shorter events, 12.5 us)
Async XLA Ops:
  6.5 554.3 %all-reduce.13.cloned.1.call-start = ((), (), s32[]{:S(2)}) async-start(), calls=%async_computation | async-start | bytes 2097152 | tf_op jit(solution)/shard_map/psum | solution.py:115
  10.5 72.5 %collective-permute-start = (bf16[1,4,2,2,3,1,128,128]{7,6,5,4,3,2,1,0:T(8,128)(2,1)}, bf16[1,4,2,2,3,1,128,128]{7,6,5,4,3,2,1,0:T(8,128)(2,1)S(1)}, u32[]{:S(2)}, u32[]{:S(2)}) collective-permute-start(bf16[1,4,2,2,3,1,128,128]{7,6,5,4,3,2,1,0:T(8,128)(2,1)} %get-tuple-element.161), channel_id=1, source_target_pairs={{0,1},{1,2},{2,3},{3,4},{4,5},{5,6},{6,7},{8,9},{9,10},{10,11},{11... | collective-permute-start | bytes 4718600 | tf_op jit(solution)/shard_map/ppermute | solution.py:15
  15.4 67.6 %collective-permute-start.1 = (bf16[1,4,2,2,3,1,128,128]{7,6,5,4,3,2,1,0:T(8,128)(2,1)}, bf16[1,4,2,2,3,1,128,128]{7,6,5,4,3,2,1,0:T(8,128)(2,1)S(1)}, u32[]{:S(2)}, u32[]{:S(2)}) collective-permute-start(bf16[1,4,2,2,3,1,128,128]{7,6,5,4,3,2,1,0:T(8,128)(2,1)} %get-tuple-element.162), channel_id=1, source_target_pairs={{1,0},{2,1},{3,2},{4,3},{5,4},{6,5},{7,6},{9,8},{10,9},{11,10},{12... | collective-permute-start | bytes 4718600 | tf_op jit(solution)/shard_map/ppermute | solution.py:18
  19.5 82.0 %copy-start.7 = (f32[1,4]{1,0:T(1,128)S(1)}, f32[1,4]{1,0:T(1,128)}, u32[]{:S(2)}) copy-start(f32[1,4]{1,0:T(1,128)} %param.5) | copy-start | bytes 52
  101.4 421.1 %copy-start.4 = (pred[36]{0:T(512)(128)(4,1)S(1)}, pred[36]{0:T(512)(128)(4,1)}, u32[]{:S(2)}) copy-start(pred[36]{0:T(512)(128)(4,1)} %compare_and_fusion) | copy-start | bytes 112
  101.4 421.1 %copy-start.5 = (pred[20]{0:T(512)(128)(4,1)S(1)}, pred[20]{0:T(512)(128)(4,1)}, u32[]{:S(2)}) copy-start(pred[20]{0:T(512)(128)(4,1)} %compare_and_fusion.1) | copy-start | bytes 64
  101.4 421.2 %copy-start.6 = (pred[34]{0:T(512)(128)(4,1)S(1)}, pred[34]{0:T(512)(128)(4,1)}, u32[]{:S(2)}) copy-start(pred[34]{0:T(512)(128)(4,1)} %compare_and_fusion.2) | copy-start | bytes 106
  101.4 470.6 %copy-start.2 = (pred[32]{0:T(512)(128)(4,1)S(1)}, pred[32]{0:T(512)(128)(4,1)}, u32[]{:S(2)}) copy-start(pred[32]{0:T(512)(128)(4,1)} %compare_and_fusion.4) | copy-start | bytes 100
  101.5 470.6 %copy-start.3 = (pred[16]{0:T(512)(128)(4,1)S(1)}, pred[16]{0:T(512)(128)(4,1)}, u32[]{:S(2)}) copy-start(pred[16]{0:T(512)(128)(4,1)} %compare_and_fusion.5) | copy-start | bytes 52
  143.6 9.4 %copy-start = (f32[2,3,16,128,127]{4,3,2,1,0:T(8,128)S(1)}, f32[2,3,16,128,127]{4,3,2,1,0:T(8,128)}, u32[]{:S(2)}) copy-start(f32[2,3,16,128,127]{4,3,2,1,0:T(8,128)} %get-tuple-element.218) | copy-start | bytes 18726916 | tf_op jit(solution)/shard_map/while
  143.6 9.8 %copy-start.1 = (f32[2,3,16,128,127]{4,3,2,1,0:T(8,128)S(1)}, f32[2,3,16,128,127]{4,3,2,1,0:T(8,128)}, u32[]{:S(2)}) copy-start(f32[2,3,16,128,127]{4,3,2,1,0:T(8,128)} %get-tuple-element.219) | copy-start | bytes 18726916 | tf_op jit(solution)/shard_map/while
  248.6 9.4 %copy-start = (f32[2,3,16,128,127]{4,3,2,1,0:T(8,128)S(1)}, f32[2,3,16,128,127]{4,3,2,1,0:T(8,128)}, u32[]{:S(2)}) copy-start(f32[2,3,16,128,127]{4,3,2,1,0:T(8,128)} %get-tuple-element.218) | copy-start | bytes 18726916 | tf_op jit(solution)/shard_map/while
  248.6 9.8 %copy-start.1 = (f32[2,3,16,128,127]{4,3,2,1,0:T(8,128)S(1)}, f32[2,3,16,128,127]{4,3,2,1,0:T(8,128)}, u32[]{:S(2)}) copy-start(f32[2,3,16,128,127]{4,3,2,1,0:T(8,128)} %get-tuple-element.219) | copy-start | bytes 18726916 | tf_op jit(solution)/shard_map/while
  353.9 9.4 %copy-start = (f32[2,3,16,128,127]{4,3,2,1,0:T(8,128)S(1)}, f32[2,3,16,128,127]{4,3,2,1,0:T(8,128)}, u32[]{:S(2)}) copy-start(f32[2,3,16,128,127]{4,3,2,1,0:T(8,128)} %get-tuple-element.218) | copy-start | bytes 18726916 | tf_op jit(solution)/shard_map/while
  353.9 9.8 %copy-start.1 = (f32[2,3,16,128,127]{4,3,2,1,0:T(8,128)S(1)}, f32[2,3,16,128,127]{4,3,2,1,0:T(8,128)}, u32[]{:S(2)}) copy-start(f32[2,3,16,128,127]{4,3,2,1,0:T(8,128)} %get-tuple-element.219) | copy-start | bytes 18726916 | tf_op jit(solution)/shard_map/while
  459.3 9.4 %copy-start = (f32[2,3,16,128,127]{4,3,2,1,0:T(8,128)S(1)}, f32[2,3,16,128,127]{4,3,2,1,0:T(8,128)}, u32[]{:S(2)}) copy-start(f32[2,3,16,128,127]{4,3,2,1,0:T(8,128)} %get-tuple-element.218) | copy-start | bytes 18726916 | tf_op jit(solution)/shard_map/while
  459.3 9.8 %copy-start.1 = (f32[2,3,16,128,127]{4,3,2,1,0:T(8,128)S(1)}, f32[2,3,16,128,127]{4,3,2,1,0:T(8,128)}, u32[]{:S(2)}) copy-start(f32[2,3,16,128,127]{4,3,2,1,0:T(8,128)} %get-tuple-element.219) | copy-start | bytes 18726916 | tf_op jit(solution)/shard_map/while
  561.7 3.8 collective-permute-start.2
  563.2 4.0 collective-permute-start.3
  567.3 5.2 collective-permute-start.4
  570.7 6.1 %collective-permute-start.5 = (f32[3,38,128]{2,1,0:T(8,128)S(1)}, f32[3,38,128]{2,1,0:T(8,128)S(1)}, u32[]{:S(2)}, u32[]{:S(2)}) collective-permute-start(f32[3,38,128]{2,1,0:T(8,128)S(1)} %get-tuple-element.172), channel_id=1, source_target_pairs={{1,0},{2,1},{3,2},{4,3},{5,4},{6,5},{7,6},{9,8},{10,9},{11,10},{12... | collective-permute-start | bytes 175112 | tf_op jit(solution)/shard_map/ppermute | solution.py:18
Sparse Core Ops, SparseCore 0:
  522.7 38.1 all-reduce.12
where the time goes:
time: 587 us; the launch traced here: 586 us
  other arithmetic  310 us (53%)
  local copies, waits for them, and re-layouts  140 us (24%)
  waiting for transfers between devices  108 us (18%)
  starting transfers between devices  13.7 us (2%)
  between operations  13.6 us (2%)
    mul x4, other arithmetic, central_diffs(): along_y = (padded[:, :, 1:-1, 2:] - padded[:, :, 1:-1, :-2]) * 0.5  110 us
    slice x7, local copies, waits for them, and re-layouts, shift_z(): return jnp.concatenate([grid_values[..., 1:], zero_plane], axis=-1)  68.8 us
    reduce_sum x4, other arithmetic, strain_dot(): running = running + jnp.sum(strain_u * strain_v, axis=0)  66.1 us
    ppermute x3, waiting for transfers between devices, padded_2(): lax.ppermute(lax.slice_in_dim(block, block.shape[dim] - width, None, axis...  64 us
    mul x8, other arithmetic, central_diffs(): along_z = (shift_z(center, True) - shift_z(center, False)) * 0.5  55.3 us
    squeeze x4, local copies, waits for them, and re-layouts, one_pair(): mode_pair[0]  46.2 us
    psum x1, waiting for transfers between devices, local(): summed = lax.psum(partial_terms, 'freq')  38.1 us
    pad x4, other arithmetic, one_pair(): jnp.pad(mode_pair, ((0, 0), (0, 0), (0, 0), (0, 0), (1, 1), (0, 0)))  35.6 us
  transfers between devices with their start and end apart: 7, of which 5 were waited for; matrix products, arithmetic and copies ran while one was open for 1% of the time, Pallas kernels for 0%

commit v1 on v0

v1 whole, which is shorter than its diff:
```python
import functools

import jax
import jax.numpy as jnp
from jax import lax
from jax.experimental import pallas as pl
from jax.experimental.pallas import tpu as pltpu
from jax.sharding import PartitionSpec as P

AXIAL = 0.35
CROSS = 0.06
MARGIN = 8
VMEM_LIMIT = 48 * 1024 * 1024


def strain_terms(field, row_grad, lane_grad, axial_grad):
    normal = (
        axial_grad(0),
        axial_grad(1) + row_grad(0),
        axial_grad(2) + lane_grad(0),
    )
    inner = (row_grad(1), lane_grad(2), row_grad(2) + lane_grad(1))
    return normal, inner


def interior_kernel(side_ref, weight_ref, modes_ref, sens_ref, edge_ref, wide_ref, lane_ref):
    slab, rows, lanes = modes_ref.shape[2:]
    first = (pl.program_id(0) == 0) & (pl.program_id(1) == 0)

    @pl.when(first)
    def _():
        sens_ref[...] = jnp.zeros_like(sens_ref)
        wide_ref[...] = jnp.zeros_like(wide_ref)

    source = lax.broadcasted_iota(jnp.int32, (lanes, lanes), 0)
    target = lax.broadcasted_iota(jnp.int32, (lanes, lanes), 1)
    difference = jnp.where(source == target + 1, 1.0, 0.0) - jnp.where(source == target - 1, 1.0, 0.0)
    difference = difference.astype(jnp.bfloat16)
    scale = weight_ref[0, pl.program_id(0)]

    def load_plane(plane, carry):
        for kind in range(2):
            for part in range(3):
                values = modes_ref[kind, part, plane]
                field = kind * 3 + part
                wide_ref[field, plane + 1, MARGIN : MARGIN + rows] = values.astype(jnp.float32)
                lane_ref[field, plane] = jnp.dot(
                    values, difference, preferred_element_type=jnp.float32
                )
        return carry

    lax.fori_loop(0, slab, load_plane, 0)

    step = 16

    def terms(plane, start):
        sides = []
        for kind in range(2):
            def axial(part):
                field = kind * 3 + part
                return (
                    wide_ref[field, plane + 2, pl.ds(MARGIN + start, step)]
                    - wide_ref[field, plane, pl.ds(MARGIN + start, step)]
                )

            def by_row(part):
                field = kind * 3 + part
                return (
                    wide_ref[field, plane + 1, pl.ds(MARGIN + start + 1, step)]
                    - wide_ref[field, plane + 1, pl.ds(MARGIN + start - 1, step)]
                )

            def by_lane(part):
                return lane_ref[kind * 3 + part, plane, pl.ds(start, step)]

            sides.append(strain_terms(None, by_row, by_lane, axial))
        return sides

    def inner_plane(plane, carry):
        for start in range(0, rows, step):
            (nu, iu), (nv, iv) = terms(plane, start)
            diagonal = nu[0] * nv[0] + iu[0] * iv[0] + iu[1] * iv[1]
            mixed = nu[1] * nv[1] + nu[2] * nv[2] + iu[2] * iv[2]
            sens_ref[plane, pl.ds(MARGIN + start, step)] += scale * (2.0 * diagonal + mixed)
        return carry

    lax.fori_loop(1, slab - 1, inner_plane, 0)

    for plane, sign in ((0, -1.0), (slab - 1, 1.0)):
        side = 1 - side_ref[0] if plane == 0 else side_ref[0]
        for start in range(0, rows, step):
            (nu, iu), (nv, iv) = terms(plane, start)
            diagonal = iu[0] * iv[0] + iu[1] * iv[1]
            mixed = iu[2] * iv[2]
            sens_ref[plane, pl.ds(MARGIN + start, step)] += scale * (2.0 * diagonal + mixed)
            for part in range(3):
                edge_ref[side, 0, part, pl.ds(start, step)] = sign * nu[part]
                edge_ref[side, 1, part, pl.ds(start, step)] = sign * nv[part]


def interior(saved_modes, weights, odd):
    _, modes, kinds, halves, parts, slab, rows, lanes = saved_modes.shape
    return pl.pallas_call(
        interior_kernel,
        grid=(modes, halves),
        in_specs=[
            pl.BlockSpec(memory_space=pltpu.SMEM),
            pl.BlockSpec(memory_space=pltpu.SMEM),
            pl.BlockSpec(
                (None, None, kinds, None, parts, slab, rows, lanes),
                lambda m, c: (0, m, 0, c, 0, 0, 0, 0),
            ),
        ],
        out_specs=[
            pl.BlockSpec((slab, rows + 2 * MARGIN, lanes), lambda m, c: (0, 0, 0)),
            pl.BlockSpec(
                (2, None, None, kinds, parts, rows, lanes),
                lambda m, c: (0, m, c, 0, 0, 0, 0),
            ),
        ],
        out_shape=[
            jax.ShapeDtypeStruct((slab, rows + 2 * MARGIN, lanes), jnp.float32),
            jax.ShapeDtypeStruct((2, modes, halves, kinds, parts, rows, lanes), jnp.float32),
        ],
        scratch_shapes=[
            pltpu.VMEM((kinds * parts, slab + 2, rows + 2 * MARGIN, lanes), jnp.float32),
            pltpu.VMEM((kinds * parts, slab, rows, lanes), jnp.float32),
        ],
        compiler_params=pltpu.CompilerParams(vmem_limit_bytes=VMEM_LIMIT),
        cost_estimate=pl.CostEstimate(
            flops=saved_modes.size * 16, bytes_accessed=saved_modes.size * 2, transcendentals=0
        ),
    )(odd, weights, saved_modes)


def late_kernel(weight_ref, edge_ref, halo_ref, out_ref):
    mode = pl.program_id(0)
    halves = edge_ref.shape[0]
    total = None
    for half in range(halves):
        diagonal, mixed = None, None
        for part in range(3):
            u = edge_ref[half, 0, part] + halo_ref[0, half, part].astype(jnp.float32)
            v = edge_ref[half, 1, part] + halo_ref[1, half, part].astype(jnp.float32)
            term = u * v
            if part == 0:
                term = 2.0 * term
            total = term if total is None else total + term
    total = weight_ref[0, mode] * total

    @pl.when(mode == 0)
    def _():
        out_ref[...] = jnp.zeros_like(out_ref)

    rows = total.shape[0]
    out_ref[pl.ds(MARGIN, rows)] += total


def late(weights, edges, halo, side):
    _, modes, halves, kinds, parts, rows, lanes = edges.shape
    return pl.pallas_call(
        late_kernel,
        grid=(modes,),
        in_specs=[
            pl.BlockSpec(memory_space=pltpu.SMEM),
            pl.BlockSpec(
                (None, None, halves, kinds, parts, rows, lanes),
                lambda m: (side, m, 0, 0, 0, 0, 0),
            ),
            pl.BlockSpec(
                (None, kinds, halves, parts, rows, lanes), lambda m: (m, 0, 0, 0, 0, 0)
            ),
        ],
        out_specs=pl.BlockSpec((rows + 2 * MARGIN, lanes), lambda m: (0, 0)),
        out_shape=jax.ShapeDtypeStruct((rows + 2 * MARGIN, lanes), jnp.float32),
        compiler_params=pltpu.CompilerParams(vmem_limit_bytes=VMEM_LIMIT),
    )(weights, edges, halo)


def smooth_kernel(total_x, total_y, place_ref, base_ref, *refs):
    near_ref, far_ref = refs[:2]
    late_refs = refs[2:-3]
    out_ref, one_ref, two_ref = refs[-3:]
    slab, tall, lanes = base_ref.shape
    odd, first_x, first_y = place_ref[0], place_ref[1], place_ref[2]
    even = odd == 0
    one_ref[pl.ds(3, slab)] = base_ref[...]
    near = near_ref[...]
    far = far_ref[...]
    one_ref[pl.ds(0, 3)] = jnp.where(even, far, near)
    one_ref[pl.ds(slab + 3, 3)] = jnp.where(even, near, far)
    late = late_refs[0][...]
    for ref in late_refs[1:]:
        late = late + ref[...]
    low, high = 3, slab + 2
    one_ref[high] += jnp.where(even, late[0], late[1])
    one_ref[low] += jnp.where(even, late[1], late[0])
    one_ref[high + 1] += jnp.where(even, late[2], late[3])
    one_ref[low - 1] += jnp.where(even, late[3], late[2])

    lane = lax.broadcasted_iota(jnp.int32, (tall, lanes), 1)
    row = lax.broadcasted_iota(jnp.int32, (tall, lanes), 0) + (first_y - MARGIN)
    first_lane, last_lane = lane == 0, lane == lanes - 1
    inside_y = (row >= 0) & (row < total_y)

    def passed(source, plane):
        center = source[plane]
        axial = source[plane + 1] + source[plane - 1] - 2.0 * center
        cross = (
            pltpu.roll(center, tall - 1, 0)
            + pltpu.roll(center, 1, 0)
            + jnp.where(last_lane, 0.0, pltpu.roll(center, lanes - 1, 1))
            + jnp.where(first_lane, 0.0, pltpu.roll(center, 1, 1))
            - 4.0 * center
        )
        x = first_x + (plane - 3)
        inside = inside_y & (x >= 0) & (x < total_x)
        return jnp.where(inside, center + AXIAL * axial + CROSS * cross, 0.0)

    for plane in range(1, slab + 5):
        two_ref[plane] = passed(one_ref, plane)
    for plane in range(2, slab + 4):
        one_ref[plane] = passed(two_ref, plane)
    for plane in range(3, slab + 3):
        out_ref[plane - 3] = passed(one_ref, plane)[MARGIN : tall - MARGIN]


def smooth(place, base, near, far, lates, total_x, total_y):
    slab, tall, lanes = base.shape
    return pl.pallas_call(
        functools.partial(smooth_kernel, total_x, total_y),
        in_specs=[pl.BlockSpec(memory_space=pltpu.SMEM)]
        + [pl.BlockSpec(memory_space=pltpu.VMEM)] * (3 + len(lates)),
        out_specs=pl.BlockSpec(memory_space=pltpu.VMEM),
        out_shape=jax.ShapeDtypeStruct((slab, tall - 2 * MARGIN, lanes), jnp.float32),
        scratch_shapes=[pltpu.VMEM((slab + 6, tall, lanes), jnp.float32)] * 2,
        compiler_params=pltpu.CompilerParams(vmem_limit_bytes=VMEM_LIMIT),
    )(place, base, near, far, *lates)


def swap(block, axis, pairs):
    return lax.ppermute(block, axis, [p for a, b in pairs for p in ((a, b), (b, a))])


def band(block, index, band_rows):
    start = pl.multiple_of(index * band_rows, 8)
    return lax.dynamic_slice_in_dim(block, start, band_rows + 2 * MARGIN, axis=1)


def shares(block, band_rows):
    count = lax.axis_size("freq")
    mine = lax.axis_index("freq")
    found = [band(block, mine, band_rows)]
    for turn in range(1, count):
        part = band(block, (mine + turn) % count, band_rows)
        found.append(lax.ppermute(part, "freq", [(i, (i + turn) % count) for i in range(count)]))
    return found


def local(saved_modes, mode_gains):
    _, modes, kinds, halves, parts, slab, rows, lanes = saved_modes.shape
    freqs = lax.axis_size("freq")
    slabs = lax.axis_size("space")
    factor = -2.0 / (saved_modes.shape[0] * freqs * modes)
    weights = (factor / 8.0) * mode_gains
    place = lax.axis_index("space")
    odd = place % 2
    band_rows = rows // freqs
    near_pairs = [(i, i + 1) for i in range(0, slabs - 1, 2)]
    far_pairs = [(i, i + 1) for i in range(1, slabs - 1, 2)]

    near_plane = jnp.where(odd == 0, slab - 1, 0)
    far_plane = slab - 1 - near_plane
    near_halo = swap(lax.dynamic_index_in_dim(saved_modes[0], near_plane, 4, False), "space", near_pairs)
    far_halo = swap(lax.dynamic_index_in_dim(saved_modes[0], far_plane, 4, False), "space", far_pairs)

    early, edges = interior(saved_modes, weights, odd.reshape(1).astype(jnp.int32))
    base = functools.reduce(jnp.add, shares(early, band_rows))
    near_start = jnp.where(odd == 0, slab - 3, 0)
    near = swap(lax.dynamic_slice_in_dim(base, near_start, 3, 0), "space", near_pairs)
    far = swap(lax.dynamic_slice_in_dim(base, slab - 3 - near_start, 3, 0), "space", far_pairs)

    near_late = late(weights, edges, near_halo, 0)
    far_late = late(weights, edges, far_halo, 1)
    others = [swap(near_late, "space", near_pairs), swap(far_late, "space", far_pairs)]
    lates = shares(jnp.stack([near_late, far_late] + others), band_rows)
    where = jnp.stack([odd, place * slab, lax.axis_index("freq") * band_rows]).astype(jnp.int32)
    return smooth(where, base, near, far, lates, slab * slabs, rows)


def solution(mesh):
    in_specs = (P("freq", None, None, None, None, "space", None, None), P("freq", None))
    out_specs = P("space", "freq", None)
    return jax.shard_map(local, mesh=mesh, in_specs=in_specs, out_specs=out_specs, check_vma=False)
```

time: 587 us -> 101 us (0.17)
  other arithmetic: 310 us -> 1.43 us
  local copies, waits for them, and re-layouts: 140 us -> 4.85 us
  waiting for transfers between devices: 108 us -> 22.6 us
  Pallas kernels: 0 us -> 52.4 us
  between operations: 13.6 us -> 0.14 us
  starting transfers between devices: 13.7 us -> 19.7 us
    mul x16 -> x1, other arithmetic: 167 us -> 0.01 us  [local(): weights = factor / 8.0 * mode_gains]
    slice x9 -> x0, local copies, waits for them, and re-layouts: 73.6 us -> none  [the longest x7 68.8 us: shift_z(): return jnp.concatenate([grid_values[..., 1:], zero_plane], axis=-1)]
    reduce_sum x4 -> x0, other arithmetic: 66.1 us -> none  [strain_dot(): running = running + jnp.sum(strain_u * strain_v, axis=0)]
    pallas_call x0 -> x4, Pallas kernels: none -> 52.4 us  [the longest x1 44.4 us: interior(): pl.pallas_call(interior_kernel, grid=(modes, halves), in_specs=[pl.BlockS...]
    ppermute x6 -> x12, waiting for transfers between devices: 70 us -> 22.6 us  [the longest x6 22 us: shares(): lax.ppermute(part, 'freq', [(i, (i + turn) % count) for i in range(count)])]
    squeeze x4 -> x1, local copies, waits for them, and re-layouts: 46.2 us -> 3.97 us  [local(): lax.dynamic_index_in_dim(saved_modes[0], near_plane, 4, False)]
    psum x1 -> x0, waiting for transfers between devices: 38.1 us -> none  [local(): summed = lax.psum(partial_terms, 'freq')]
    pad x4 -> x0, other arithmetic: 35.6 us -> none  [one_pair(): jnp.pad(mode_pair, ((0, 0), (0, 0), (0, 0), (0, 0), (1, 1), (0, 0)))]
  transfers between devices with their start and end apart: 7 -> 12, of which waited for: 5 -> 7; matrix products, arithmetic and copies ran while one was open for 1% -> 2% of each run, Pallas kernels for 0% -> 50%
where the time goes in v1:
time: 101 us
  Pallas kernels  52.4 us (52%)
  waiting for transfers between devices  22.6 us (22%)
  starting transfers between devices  19.7 us (20%)
  local copies, waits for them, and re-layouts  4.85 us (5%)
  other arithmetic  1.43 us (1%)
    pallas_call x1, Pallas kernels, interior(): pl.pallas_call(interior_kernel, grid=(modes, halves), in_specs=[pl.BlockS...  44.4 us
    ppermute x6, waiting for transfers between devices, shares(): lax.ppermute(part, 'freq', [(i, (i + turn) % count) for i in range(count)])  22 us
    ppermute x6, starting transfers between devices, swap(): lax.ppermute(block, axis, [p for a, b in pairs for p in ((a, b), (b, a))])  14.7 us
    pallas_call x2, Pallas kernels, late(): pl.pallas_call(late_kernel, grid=(modes,), in_specs=[pl.BlockSpec(memory_...  5.93 us
    ppermute x6, starting transfers between devices, shares(): lax.ppermute(part, 'freq', [(i, (i + turn) % count) for i in range(count)])  5.01 us
    squeeze x1, local copies, waits for them, and re-layouts, local(): lax.dynamic_index_in_dim(saved_modes[0], near_plane, 4, False)  3.97 us
    pallas_call x1, Pallas kernels, smooth(): pl.pallas_call(functools.partial(smooth_kernel, total_x, total_y), in_spe...  2.13 us
  transfers between devices with their start and end apart: 12, of which 7 were waited for; matrix products, arithmetic and copies ran while one was open for 2% of the time, Pallas kernels for 50%

profile of v1, /device:TPU:0, one launch (start us, length us, event | category | flops | bytes accessed | tf_op | source)
XLA Modules:
  0.0 101.1 jit_solution(14724932746565470929)
XLA Ops:
  0.0 0.0 copy-start
  0.0 4.0 %dynamic-slice_bitcast_fusion.1 = (bf16[4,2,2,3,128,128]{5,4,3,2,1,0:T(8,128)(2,1)}, bf16[4,2,2,3,128,128]{5,4,3,2,1,0:T(8,128)(2,1)}) fusion(bf16[1,4,2,2,3,16,128,128]{7,6,5,4,3,2,1,0:T(8,128)(2,1)} %modes_ref.1, s32[]{:T(128)S(6)} %select_n.67, s32[]{:T(128)S(6)} %select_n.68), kind=kLoop, calls=%fused_computation.1 | loop fusion | bytes 6291464 | tf_op jit(solution)/shard_map/jit(dynamic_index_in_dim)/squeeze | solution.py:274
  4.0 3.0 %collective-permute-start.5 = (bf16[4,2,2,3,128,128]{5,4,3,2,1,0:T(8,128)(2,1)}, bf16[4,2,2,3,128,128]{5,4,3,2,1,0:T(8,128)(2,1)}, u32[]{:S(2)}, u32[]{:S(2)}) collective-permute-start(bf16[4,2,2,3,128,128]{5,4,3,2,1,0:T(8,128)(2,1)} %get-tuple-element.9), channel_id=1, source_target_pairs={{0,1},{1,0},{2,3},{3,2},{4,5},{5,4},{6,7},{7,6},{8,9},{9,8},{10,11... | collective-permute-start | bytes 4718600 | tf_op jit(solution)/shard_map/ppermute | solution.py:242
  6.9 0.7 collective-permute-start.6
  7.7 0.0 copy-done
  7.8 44.4 %shard_map.28 = (f32[16,144,128]{2,1,0:T(8,128)S(1)}, f32[2,4,2,2,3,128,128]{6,5,4,3,2,1,0:T(8,128)}) custom-call(s32[1]{0:T(128)} %bitcast.side_ref, f32[1,4]{1,0:T(1,128)S(1)} %broadcast_multiply_fusion.weight_ref, bf16[1,4,2,2,3,16,128,128]{7,6,5,4,3,2,1,0:T(8,128)(2,1)} %modes_ref.1), custom_call_target="tpu_custom_call" | custom-call | flops 201326592 | bytes 25165824 | tf_op jit(solution)/shard_map/pallas_call | solution.py:103
  52.1 0.8 constant_dynamic-slice_fusion.8
  52.9 0.0 collective-permute-start
  52.9 1.7 %collective-permute-start.2 = (f32[16,48,128]{2,1,0:T(8,128)S(1)}, f32[16,48,128]{2,1,0:T(8,128)}, u32[]{:S(2)}, u32[]{:S(2)}) collective-permute-start(f32[16,48,128]{2,1,0:T(8,128)S(1)} %get-tuple-element.12), channel_id=1, source_target_pairs={{0,24},{8,0},{16,8},{24,16},{1,25},{9,1},{17,9},{25,17},{2,26},{10... | collective-permute-start | bytes 1179656 | tf_op jit(solution)/shard_map/ppermute | solution.py:256
  54.7 1.5 %collective-permute-start.1 = (f32[16,48,128]{2,1,0:T(8,128)S(1)}, f32[16,48,128]{2,1,0:T(8,128)}, u32[]{:S(2)}, u32[]{:S(2)}) collective-permute-start(f32[16,48,128]{2,1,0:T(8,128)S(1)} %get-tuple-element.13), channel_id=1, source_target_pairs={{0,16},{8,24},{16,0},{24,8},{1,17},{9,25},{17,1},{25,9},{2,18},{10... | collective-permute-start | bytes 1179656 | tf_op jit(solution)/shard_map/ppermute | solution.py:256
  56.2 6.9 %collective-permute-done = f32[16,48,128]{2,1,0:T(8,128)} collective-permute-done((f32[16,48,128]{2,1,0:T(8,128)}, f32[16,48,128]{2,1,0:T(8,128)}, u32[]{:S(2)}, u32[]{:S(2)}) %collective-permute-start) | collective-permute-done | bytes 393248 | tf_op jit(solution)/shard_map/ppermute | solution.py:256
  63.0 1.1 %collective-permute-done.2 = f32[16,48,128]{2,1,0:T(8,128)} collective-permute-done((f32[16,48,128]{2,1,0:T(8,128)S(1)}, f32[16,48,128]{2,1,0:T(8,128)}, u32[]{:S(2)}, u32[]{:S(2)}) %collective-permute-start.2) | collective-permute-done | bytes 393248 | tf_op jit(solution)/shard_map/ppermute | solution.py:256
  64.1 9.0 %collective-permute-done.1 = f32[16,48,128]{2,1,0:T(8,128)} collective-permute-done((f32[16,48,128]{2,1,0:T(8,128)S(1)}, f32[16,48,128]{2,1,0:T(8,128)}, u32[]{:S(2)}, u32[]{:S(2)}) %collective-permute-start.1) | collective-permute-done | bytes 393248 | tf_op jit(solution)/shard_map/ppermute | solution.py:256
  73.1 1.3 %add_add_fusion.base_ref = f32[16,48,128]{2,1,0:T(8,128)S(1)} fusion(f32[16,48,128]{2,1,0:T(8,128)} %collective-permute-done.2, f32[16,48,128]{2,1,0:T(8,128)} %collective-permute-done.1, f32[16,48,128]{2,1,0:T(8,128)} %collective-permute-done, f32[16,144,128]{2,1,0:T(8,128)S(1)} %get-tuple-element.7, s32[]{:T(128)S(6)} %select_n.58), kind=kLoop, calls=%fused_computation.2 | loop fusion | flops 294912 | bytes 1966084 | tf_op jit(solution)/shard_map/add | solution.py:278
  74.4 0.2 collective-permute-done.5.halo_ref
  74.6 3.1 %shard_map.29 = f32[144,128]{1,0:T(8,128)S(1)} custom-call(f32[1,4]{1,0:T(1,128)S(1)} %broadcast_multiply_fusion.weight_ref, f32[2,4,2,2,3,128,128]{6,5,4,3,2,1,0:T(8,128)} %get-tuple-element.8.edge_ref, bf16[4,2,2,3,128,128]{5,4,3,2,1,0:T(8,128)(2,1)} %collective-permute-done.5.halo_ref), custom_call_target="tpu_custom_call" | custom-call | tf_op jit(solution)/shard_map/pallas_call | solution.py:161
  77.8 4.1 %collective-permute-start.7 = (f32[144,128]{1,0:T(8,128)S(1)}, f32[144,128]{1,0:T(8,128)S(1)}, u32[]{:S(2)}, u32[]{:S(2)}) collective-permute-start(f32[144,128]{1,0:T(8,128)S(1)} %shard_map.29), channel_id=1, source_target_pairs={{0,1},{1,0},{2,3},{3,2},{4,5},{5,4},{6,7},{7,6},{8,9},{9,8},{10,11... | collective-permute-start | bytes 221192 | tf_op jit(solution)/shard_map/ppermute | solution.py:242
  81.8 0.0 collective-permute-done.6.halo_ref
  81.8 2.8 %shard_map.30 = f32[144,128]{1,0:T(8,128)S(1)} custom-call(f32[1,4]{1,0:T(1,128)S(1)} %broadcast_multiply_fusion.weight_ref, f32[2,4,2,2,3,128,128]{6,5,4,3,2,1,0:T(8,128)} %get-tuple-element.8.edge_ref, bf16[4,2,2,3,128,128]{5,4,3,2,1,0:T(8,128)(2,1)S(1)} %collective-permute-done.6.halo_ref), custom_call_target="tpu_custom_call" | custom-call | tf_op jit(solution)/shard_map/pallas_call | solution.py:161
  84.7 0.7 collective-permute-start.8
  85.4 0.7 collective-permute-start.4
  86.0 5.6 %collective-permute-start.3 = (f32[3,48,128]{2,1,0:T(8,128)S(1)}, f32[3,48,128]{2,1,0:T(8,128)S(1)}, u32[]{:S(2)}, u32[]{:S(2)}) collective-permute-start(f32[3,48,128]{2,1,0:T(8,128)S(1)} %get-tuple-element.15), channel_id=1, source_target_pairs={{0,1},{1,0},{2,3},{3,2},{4,5},{5,4},{6,7},{7,6},{8,9},{9,8},{10,11... | collective-permute-start | bytes 221192 | tf_op jit(solution)/shard_map/ppermute | solution.py:242
  91.6 0.0 collective-permute-done.7
  91.6 0.0 collective-permute-done.8
  91.7 0.1 collective-permute-start.11
  91.8 1.6 %collective-permute-start.10 = (f32[4,48,128]{2,1,0:T(8,128)S(1)}, f32[4,48,128]{2,1,0:T(8,128)S(1)}, u32[]{:S(2)}, u32[]{:S(2)}) collective-permute-start(f32[4,48,128]{2,1,0:T(8,128)S(1)} %get-tuple-element.17), channel_id=1, source_target_pairs={{0,16},{8,24},{16,0},{24,8},{1,17},{9,25},{17,1},{25,9},{2,18},{10... | collective-permute-start | bytes 294920 | tf_op jit(solution)/shard_map/ppermute | solution.py:256
  93.3 0.2 collective-permute-start.9
  93.5 0.1 pad_add_fusion.place_ref
  93.6 0.0 collective-permute-done.4.refs_1_
  93.6 0.4 collective-permute-done.3.refs_0_
  94.0 0.0 collective-permute-done.11.refs_5_
  94.0 4.9 %collective-permute-done.10.refs_4_ = f32[4,48,128]{2,1,0:T(8,128)S(1)} collective-permute-done((f32[4,48,128]{2,1,0:T(8,128)S(1)}, f32[4,48,128]{2,1,0:T(8,128)S(1)}, u32[]{:S(2)}, u32[]{:S(2)}) %collective-permute-start.10) | collective-permute-done | bytes 98336 | tf_op jit(solution)/shard_map/ppermute | solution.py:256
  98.9 0.1 collective-permute-done.9.refs_3_
  99.0 2.1 %shard_map.31 = f32[16,32,128]{2,1,0:T(8,128)} custom-call(s32[3]{0:T(128)S(1)} %pad_add_fusion.place_ref, f32[16,48,128]{2,1,0:T(8,128)S(1)} %add_add_fusion.base_ref, f32[3,48,128]{2,1,0:T(8,128)S(1)} %collective-permute-done.3.refs_0_, f32[3,48,128]{2,1,0:T(8,128)S(1)} %collective-permute-done.4.refs_1_, f32[4,48,128]{2,1,0:T(8,128)S(1)} %get-tuple-element.19.refs_2_, ...), custom_call_target="tpu_custom_call" | custom-call | tf_op jit(solution)/shard_map/pallas_call | solution.py:230
  (4 shorter events, 0.1 us)
Async XLA Ops:
  0.0 7.7 %copy-start = (f32[1,4]{1,0:T(1,128)S(1)}, f32[1,4]{1,0:T(1,128)}, u32[]{:S(2)}) copy-start(f32[1,4]{1,0:T(1,128)} %param.3) | copy-start | bytes 52
  4.0 70.6 %collective-permute-start.5 = (bf16[4,2,2,3,128,128]{5,4,3,2,1,0:T(8,128)(2,1)}, bf16[4,2,2,3,128,128]{5,4,3,2,1,0:T(8,128)(2,1)}, u32[]{:S(2)}, u32[]{:S(2)}) collective-permute-start(bf16[4,2,2,3,128,128]{5,4,3,2,1,0:T(8,128)(2,1)} %get-tuple-element.9), channel_id=1, source_target_pairs={{0,1},{1,0},{2,3},{3,2},{4,5},{5,4},{6,7},{7,6},{8,9},{9,8},{10,11... | collective-permute-start | bytes 4718600 | tf_op jit(solution)/shard_map/ppermute | solution.py:242
  6.9 74.9 %collective-permute-start.6 = (bf16[4,2,2,3,128,128]{5,4,3,2,1,0:T(8,128)(2,1)}, bf16[4,2,2,3,128,128]{5,4,3,2,1,0:T(8,128)(2,1)S(1)}, u32[]{:S(2)}, u32[]{:S(2)}) collective-permute-start(bf16[4,2,2,3,128,128]{5,4,3,2,1,0:T(8,128)(2,1)} %get-tuple-element.10), channel_id=1, source_target_pairs={{1,2},{2,1},{3,4},{4,3},{5,6},{6,5},{9,10},{10,9},{11,12},{12,11},... | collective-permute-start | bytes 4718600 | tf_op jit(solution)/shard_map/ppermute | solution.py:242
  52.9 10.1 %collective-permute-start = (f32[16,48,128]{2,1,0:T(8,128)}, f32[16,48,128]{2,1,0:T(8,128)}, u32[]{:S(2)}, u32[]{:S(2)}) collective-permute-start(f32[16,48,128]{2,1,0:T(8,128)} %get-tuple-element.11), channel_id=1, source_target_pairs={{0,8},{8,16},{16,24},{24,0},{1,9},{9,17},{17,25},{25,1},{2,10},{10... | collective-permute-start | bytes 1179656 | tf_op jit(solution)/shard_map/ppermute | solution.py:256
  52.9 11.2 %collective-permute-start.2 = (f32[16,48,128]{2,1,0:T(8,128)S(1)}, f32[16,48,128]{2,1,0:T(8,128)}, u32[]{:S(2)}, u32[]{:S(2)}) collective-permute-start(f32[16,48,128]{2,1,0:T(8,128)S(1)} %get-tuple-element.12), channel_id=1, source_target_pairs={{0,24},{8,0},{16,8},{24,16},{1,25},{9,1},{17,9},{25,17},{2,26},{10... | collective-permute-start | bytes 1179656 | tf_op jit(solution)/shard_map/ppermute | solution.py:256
  54.7 18.4 %collective-permute-start.1 = (f32[16,48,128]{2,1,0:T(8,128)S(1)}, f32[16,48,128]{2,1,0:T(8,128)}, u32[]{:S(2)}, u32[]{:S(2)}) collective-permute-start(f32[16,48,128]{2,1,0:T(8,128)S(1)} %get-tuple-element.13), channel_id=1, source_target_pairs={{0,16},{8,24},{16,0},{24,8},{1,17},{9,25},{17,1},{25,9},{2,18},{10... | collective-permute-start | bytes 1179656 | tf_op jit(solution)/shard_map/ppermute | solution.py:256
  77.8 13.9 %collective-permute-start.7 = (f32[144,128]{1,0:T(8,128)S(1)}, f32[144,128]{1,0:T(8,128)S(1)}, u32[]{:S(2)}, u32[]{:S(2)}) collective-permute-start(f32[144,128]{1,0:T(8,128)S(1)} %shard_map.29), channel_id=1, source_target_pairs={{0,1},{1,0},{2,3},{3,2},{4,5},{5,4},{6,7},{7,6},{8,9},{9,8},{10,11... | collective-permute-start | bytes 221192 | tf_op jit(solution)/shard_map/ppermute | solution.py:242
  84.7 7.0 %collective-permute-start.8 = (f32[144,128]{1,0:T(8,128)S(1)}, f32[144,128]{1,0:T(8,128)S(1)}, u32[]{:S(2)}, u32[]{:S(2)}) collective-permute-start(f32[144,128]{1,0:T(8,128)S(1)} %shard_map.30), channel_id=1, source_target_pairs={{1,2},{2,1},{3,4},{4,3},{5,6},{6,5},{9,10},{10,9},{11,12},{12,11},... | collective-permute-start | bytes 221192 | tf_op jit(solution)/shard_map/ppermute | solution.py:242
  85.4 8.2 %collective-permute-start.4 = (f32[3,48,128]{2,1,0:T(8,128)S(1)}, f32[3,48,128]{2,1,0:T(8,128)S(1)}, u32[]{:S(2)}, u32[]{:S(2)}) collective-permute-start(f32[3,48,128]{2,1,0:T(8,128)S(1)} %get-tuple-element.14), channel_id=1, source_target_pairs={{1,2},{2,1},{3,4},{4,3},{5,6},{6,5},{9,10},{10,9},{11,12},{12,11},... | collective-permute-start | bytes 221192 | tf_op jit(solution)/shard_map/ppermute | solution.py:242
  86.0 7.9 %collective-permute-start.3 = (f32[3,48,128]{2,1,0:T(8,128)S(1)}, f32[3,48,128]{2,1,0:T(8,128)S(1)}, u32[]{:S(2)}, u32[]{:S(2)}) collective-permute-start(f32[3,48,128]{2,1,0:T(8,128)S(1)} %get-tuple-element.15), channel_id=1, source_target_pairs={{0,1},{1,0},{2,3},{3,2},{4,5},{5,4},{6,7},{7,6},{8,9},{9,8},{10,11... | collective-permute-start | bytes 221192 | tf_op jit(solution)/shard_map/ppermute | solution.py:242
  91.7 2.3 %collective-permute-start.11 = (f32[4,48,128]{2,1,0:T(8,128)S(1)}, f32[4,48,128]{2,1,0:T(8,128)S(1)}, u32[]{:S(2)}, u32[]{:S(2)}) collective-permute-start(f32[4,48,128]{2,1,0:T(8,128)S(1)} %get-tuple-element.16), channel_id=1, source_target_pairs={{0,24},{8,0},{16,8},{24,16},{1,25},{9,1},{17,9},{25,17},{2,26},{10... | collective-permute-start | bytes 294920 | tf_op jit(solution)/shard_map/ppermute | solution.py:256
  91.8 7.1 %collective-permute-start.10 = (f32[4,48,128]{2,1,0:T(8,128)S(1)}, f32[4,48,128]{2,1,0:T(8,128)S(1)}, u32[]{:S(2)}, u32[]{:S(2)}) collective-permute-start(f32[4,48,128]{2,1,0:T(8,128)S(1)} %get-tuple-element.17), channel_id=1, source_target_pairs={{0,16},{8,24},{16,0},{24,8},{1,17},{9,25},{17,1},{25,9},{2,18},{10... | collective-permute-start | bytes 294920 | tf_op jit(solution)/shard_map/ppermute | solution.py:256
  93.3 5.7 %collective-permute-start.9 = (f32[4,48,128]{2,1,0:T(8,128)S(1)}, f32[4,48,128]{2,1,0:T(8,128)S(1)}, u32[]{:S(2)}, u32[]{:S(2)}) collective-permute-start(f32[4,48,128]{2,1,0:T(8,128)S(1)} %get-tuple-element.18), channel_id=1, source_target_pairs={{0,8},{8,16},{16,24},{24,0},{1,9},{9,17},{17,25},{25,1},{2,10},{10... | collective-permute-start | bytes 294920 | tf_op jit(solution)/shard_map/ppermute | solution.py:256

commit v2 on v1

v2 whole, which is shorter than its diff:
```python
import functools

import jax
import jax.numpy as jnp
from jax import lax
from jax.experimental import pallas as pl
from jax.experimental.pallas import tpu as pltpu
from jax.sharding import PartitionSpec as P

AXIAL = 0.35
CROSS = 0.06
MARGIN = 8
STEP = 16
INTERIOR_VMEM = 36 * 1024 * 1024
QUICK = pl.CostEstimate(flops=1024, bytes_accessed=1024, transcendentals=0)
INTERIOR_FLOPS = 8 * 10**9
SMOOTH_FLOPS = 10**10
SMALL_VMEM = 16 * 1024 * 1024


def plane_kernel(begin, plane_ref, modes_ref, *refs):
    out_refs, sems = refs[-1 - len(begin) : -1], refs[-1]
    copies = []
    for at, (first, out_ref) in enumerate(zip(begin, out_refs, strict=True)):
        source = modes_ref.at[0, pl.ds(first, out_ref.shape[0]), :, :, :, plane_ref[0]]
        copies.append(pltpu.make_async_copy(source, out_ref, sems.at[at]))
        copies[-1].start()
    for copy in copies:
        copy.wait()


def planes(saved_modes, plane, groups, after):
    _, _, kinds, halves, parts, _, rows, lanes = saved_modes.shape
    return pl.pallas_call(
        functools.partial(plane_kernel, [first for first, _ in groups]),
        in_specs=[pl.BlockSpec(memory_space=pltpu.SMEM), pl.BlockSpec(memory_space=pl.ANY)]
        + [pl.BlockSpec(memory_space=pl.ANY)] * len(after),
        out_specs=[pl.BlockSpec(memory_space=pltpu.VMEM)] * len(groups),
        out_shape=[
            pltpu.VMEM((count, kinds, halves, parts, rows, lanes), saved_modes.dtype) for _, count in groups
        ],
        scratch_shapes=[pltpu.SemaphoreType.DMA((len(groups),))],
        compiler_params=pltpu.CompilerParams(vmem_limit_bytes=SMALL_VMEM),
        cost_estimate=QUICK,
    )(plane.reshape(1).astype(jnp.int32), hbm(saved_modes), *after)


def interior_kernel(after, side_ref, weight_ref, modes_ref, *refs):
    sens_ref, near_edge_ref, far_edge_ref, wide_ref, lane_ref = refs[after:]
    slab, rows, lanes = modes_ref.shape[2:]

    @pl.when((pl.program_id(0) == 0) & (pl.program_id(1) == 0))
    def _():
        sens_ref[...] = jnp.zeros_like(sens_ref)
        wide_ref[...] = jnp.zeros_like(wide_ref)

    source = lax.broadcasted_iota(jnp.int32, (lanes, lanes), 0)
    target = lax.broadcasted_iota(jnp.int32, (lanes, lanes), 1)
    difference = jnp.where(source == target + 1, 1.0, 0.0) - jnp.where(source == target - 1, 1.0, 0.0)
    difference = difference.astype(jnp.bfloat16)
    lane = lax.broadcasted_iota(jnp.int32, (STEP, lanes), 1)
    not_last = jnp.where(lane == lanes - 1, 0.0, 1.0)
    not_first = jnp.where(lane == 0, 0.0, 1.0)
    scale = weight_ref[0, pl.program_id(0)]

    def load_plane(plane):
        for kind in range(2):
            for part in range(3):
                values = modes_ref[kind, part, plane]
                field = kind * 3 + part
                wide_ref[field, plane + 1, MARGIN : MARGIN + rows] = values.astype(jnp.float32)
                if part > 0:
                    lane_ref[field, plane] = jnp.dot(
                        values, difference, preferred_element_type=jnp.float32
                    )

    def terms(plane, start):
        sides = []
        for kind in range(2):

            def axial(part):
                field = kind * 3 + part
                return (
                    wide_ref[field, plane + 2, pl.ds(MARGIN + start, STEP)]
                    - wide_ref[field, plane, pl.ds(MARGIN + start, STEP)]
                )

            def by_row(part):
                field = kind * 3 + part
                return (
                    wide_ref[field, plane + 1, pl.ds(MARGIN + start + 1, STEP)]
                    - wide_ref[field, plane + 1, pl.ds(MARGIN + start - 1, STEP)]
                )

            def by_lane(part):
                if part > 0:
                    return lane_ref[kind * 3 + part, plane, pl.ds(start, STEP)]
                values = modes_ref[kind, part, plane, pl.ds(start, STEP)]
                upper = pltpu.roll(values, lanes - 1, 1).astype(jnp.float32)
                lower = pltpu.roll(values, 1, 1).astype(jnp.float32)
                return upper * not_last - lower * not_first

            outer = (axial(0), axial(1) + by_row(0), axial(2) + by_lane(0))
            inner = (by_row(1), by_lane(2), by_row(2) + by_lane(1))
            sides.append((outer, inner))
        return sides

    def inner_plane(plane):
        for start in range(0, rows, STEP):
            (ou, iu), (ov, iv) = terms(plane, start)
            diagonal = ou[0] * ov[0] + iu[0] * iv[0] + iu[1] * iv[1]
            mixed = ou[1] * ov[1] + ou[2] * ov[2] + iu[2] * iv[2]
            sens_ref[plane, pl.ds(MARGIN + start, STEP)] += scale * (2.0 * diagonal + mixed)

    def both(plane, carry):
        load_plane(plane + 1)
        inner_plane(plane)
        return carry

    load_plane(0)
    load_plane(1)
    lax.fori_loop(1, slab - 1, both, 0, unroll=True)

    odd = side_ref[0]
    near = (1 - odd) * (slab - 1)
    for edge_ref, plane, sign in (
        (near_edge_ref, near, 1.0 - 2.0 * odd.astype(jnp.float32)),
        (far_edge_ref, slab - 1 - near, 2.0 * odd.astype(jnp.float32) - 1.0),
    ):
        for start in range(0, rows, STEP):
            (ou, iu), (ov, iv) = terms(plane, start)
            diagonal = iu[0] * iv[0] + iu[1] * iv[1]
            mixed = iu[2] * iv[2]
            sens_ref[plane, pl.ds(MARGIN + start, STEP)] += scale * (2.0 * diagonal + mixed)
            for part in range(3):
                edge_ref[0, part, pl.ds(start, STEP)] = sign * ou[part]
                edge_ref[1, part, pl.ds(start, STEP)] = sign * ov[part]


def interior(saved_modes, weights, sides, after):
    _, modes, kinds, halves, parts, slab, rows, lanes = saved_modes.shape
    whole = (slab, rows + 2 * MARGIN, lanes)
    edges = (modes, halves, kinds, parts, rows, lanes)
    fields = kinds * parts
    return pl.pallas_call(
        functools.partial(interior_kernel, len(after)),
        grid=(modes, halves),
        in_specs=[
            pl.BlockSpec(memory_space=pltpu.SMEM),
            pl.BlockSpec(memory_space=pltpu.SMEM),
            pl.BlockSpec(
                (None, None, kinds, None, parts, slab, rows, lanes),
                lambda m, c: (0, m, 0, c, 0, 0, 0, 0),
            ),
        ]
        + [pl.BlockSpec(memory_space=pl.ANY)] * len(after),
        out_specs=[pl.BlockSpec(whole, lambda m, c: (0, 0, 0))]
        + [pl.BlockSpec((None, None) + edges[2:], lambda m, c: (m, c, 0, 0, 0, 0))] * 2,
        out_shape=[pltpu.VMEM(whole, jnp.float32), pltpu.HBM(edges, jnp.float32), pltpu.VMEM(edges, jnp.float32)],
        scratch_shapes=[
            pltpu.VMEM((fields, slab + 2, rows + 2 * MARGIN, lanes), jnp.float32),
            pltpu.VMEM((fields, slab, rows, lanes), jnp.float32),
        ],
        compiler_params=pltpu.CompilerParams(vmem_limit_bytes=INTERIOR_VMEM),
        cost_estimate=pl.CostEstimate(flops=INTERIOR_FLOPS, bytes_accessed=1024, transcendentals=0),
    )(sides, weights, saved_modes, *after)


def outer_plane(weight_ref, edge_ref, halo_ref, begin, start):
    modes, halves, _, parts = edge_ref.shape[:4]
    total = None
    for mode in range(modes):
        found = None
        for half in range(halves):
            for part in range(parts):
                u, v = (
                    edge_ref[mode, half, kind, part, pl.ds(start, STEP)]
                    + halo_ref[mode, kind, half, part, pl.ds(start, STEP)].astype(jnp.float32)
                    for kind in range(2)
                )
                term = u * v
                if part == 0:
                    term = 2.0 * term
                found = term if found is None else found + term
        found = weight_ref[0, begin + mode] * found
        total = found if total is None else total + found
    return total


def far_kernel(side_ref, weight_ref, edge_ref, halo_ref, sens_ref, turns_ref, tall_ref):
    slab = sens_ref.shape[0]
    rows = edge_ref.shape[4]
    count, _, tall, _ = turns_ref.shape
    band = tall - 2 * MARGIN
    far = side_ref[0] * (slab - 1)
    tall_ref[...] = sens_ref[far]
    for start in range(0, rows, STEP):
        tall_ref[pl.ds(MARGIN + start, STEP)] += outer_plane(weight_ref, edge_ref, halo_ref, 0, start)
    for piece in range(count):
        index, bits = 0, 1
        while bits < count:
            index = 2 * index + (piece // bits) % 2
            bits *= 2
        turns_ref[piece] = sens_ref[:, pl.ds(index * band, tall)]
        turns_ref[piece, far] = tall_ref[pl.ds(index * band, tall)]


def finish_far(sides, weights, edges, halo, sens, freqs):
    slab, rows, lanes = sens.shape
    band = (rows - 2 * MARGIN) // freqs
    return pl.pallas_call(
        far_kernel,
        in_specs=[pl.BlockSpec(memory_space=pltpu.SMEM)] * 2 + [pl.BlockSpec(memory_space=pltpu.VMEM)] * 3,
        out_specs=pl.BlockSpec(memory_space=pltpu.VMEM),
        out_shape=jax.ShapeDtypeStruct((freqs, slab, band + 2 * MARGIN, lanes), jnp.float32),
        scratch_shapes=[pltpu.VMEM((rows, lanes), jnp.float32)],
        compiler_params=pltpu.CompilerParams(vmem_limit_bytes=SMALL_VMEM),
        cost_estimate=QUICK,
    )(sides, weights, edges, halo, sens)


def near_part_kernel(weight_ref, edge_ref, halo_ref, last_ref, *refs):
    out_ref, kept_ref, done = refs[-3:]
    copy = pltpu.make_async_copy(last_ref.at[last_ref.shape[0] - 1], kept_ref.at[0], done)
    copy.start()
    for start in range(0, out_ref.shape[0], STEP):
        out_ref[pl.ds(start, STEP)] = outer_plane(weight_ref, edge_ref, halo_ref, 0, start)
    copy.wait()


def near_part(weights, edges, halo, after):
    count = halo.shape[0]
    rows, lanes = edges.shape[4:]
    return pl.pallas_call(
        near_part_kernel,
        grid=(1,),
        in_specs=[
            pl.BlockSpec(memory_space=pltpu.SMEM),
            pl.BlockSpec((count,) + edges.shape[1:], lambda i: (0,) * 6),
            pl.BlockSpec(halo.shape, lambda i: (0,) * 6),
        ]
        + [pl.BlockSpec(memory_space=pl.ANY)] * (1 + len(after)),
        out_specs=[
            pl.BlockSpec((rows, lanes), lambda i: (0, 0)),
            pl.BlockSpec(memory_space=pltpu.VMEM),
        ],
        out_shape=[
            pltpu.VMEM((rows, lanes), jnp.float32),
            pltpu.VMEM((1,) + edges.shape[1:], jnp.float32),
        ],
        scratch_shapes=[pltpu.SemaphoreType.DMA(())],
        compiler_params=pltpu.CompilerParams(vmem_limit_bytes=SMALL_VMEM),
        cost_estimate=QUICK,
    )(weights, edges, halo, edges, *after)


def outer_kernel(begin, weight_ref, edge_ref, halo_ref, before_ref, *refs):
    out_ref, tall_ref, band_ref, done = refs[-4:]
    rows = edge_ref.shape[4]
    pieces, tall, lanes = band_ref.shape
    band = tall - 2 * MARGIN
    empty = jnp.zeros((MARGIN, lanes), jnp.float32)
    tall_ref[pl.ds(0, MARGIN)] = empty
    tall_ref[pl.ds(MARGIN + rows, MARGIN)] = empty
    for start in range(0, rows, STEP):
        found = outer_plane(weight_ref, edge_ref, halo_ref, begin, start)
        tall_ref[pl.ds(MARGIN + start, STEP)] = before_ref[pl.ds(start, STEP)] + found
    for piece in range(pieces):
        band_ref[piece] = tall_ref[pl.ds(piece // 2 * band, tall)]
    copy = pltpu.make_async_copy(band_ref, out_ref, done)
    copy.start()
    copy.wait()


def finish_near(begin, weights, edges, halo, before, pieces, after):
    rows, lanes = edges.shape[4:]
    shape = (pieces, rows // (pieces // 2) + 2 * MARGIN, lanes)
    return pl.pallas_call(
        functools.partial(outer_kernel, begin),
        in_specs=[pl.BlockSpec(memory_space=pltpu.SMEM)]
        + [pl.BlockSpec(memory_space=pltpu.VMEM)] * 3
        + [pl.BlockSpec(memory_space=pl.ANY)] * len(after),
        out_specs=pl.BlockSpec(memory_space=pltpu.HBM),
        out_shape=pltpu.HBM(shape, jnp.float32),
        scratch_shapes=[
            pltpu.VMEM((rows + 2 * MARGIN, lanes), jnp.float32),
            pltpu.VMEM(shape, jnp.float32),
            pltpu.SemaphoreType.DMA(()),
        ],
        compiler_params=pltpu.CompilerParams(vmem_limit_bytes=SMALL_VMEM),
        cost_estimate=QUICK,
    )(weights, edges, halo, before, *after)


class Pass:
    def __init__(self, tall, lanes, first_y, total_y):
        self.tall, self.lanes = tall, lanes
        self.lane = lax.broadcasted_iota(jnp.int32, (tall, lanes), 1)
        row = lax.broadcasted_iota(jnp.int32, (tall, lanes), 0) + (first_y - MARGIN)
        self.inside = (row >= 0) & (row < total_y)

    def __call__(self, below, center, above):
        axial = above + below - 2.0 * center
        cross = (
            pltpu.roll(center, self.tall - 1, 0)
            + pltpu.roll(center, 1, 0)
            + jnp.where(self.lane == self.lanes - 1, 0.0, pltpu.roll(center, self.lanes - 1, 1))
            + jnp.where(self.lane == 0, 0.0, pltpu.roll(center, 1, 1))
            - 4.0 * center
        )
        return jnp.where(self.inside, center + AXIAL * axial + CROSS * cross, 0.0)


def smooth_kernel(total_x, total_y, place_ref, base_ref, near_ref, far_ref, out_ref, one_ref, two_ref):
    slab, tall, lanes = base_ref.shape
    first_x = place_ref[1]
    even = place_ref[0] == 0
    one_ref[pl.ds(3, slab)] = base_ref[...]
    near = near_ref[...]
    far = far_ref[...]
    one_ref[pl.ds(0, 3)] = jnp.where(even, far, near)
    one_ref[pl.ds(slab + 3, 3)] = jnp.where(even, near, far)
    smoothed = Pass(tall, lanes, place_ref[2], total_y)

    def clear(ref, plane):
        x = first_x + (plane - 3)

        @pl.when((x < 0) | (x >= total_x))
        def _():
            ref[plane] = jnp.zeros_like(ref[plane])

    def passed(source, plane):
        return smoothed(source[plane - 1], source[plane], source[plane + 1])

    for plane in range(1, slab + 5):
        two_ref[plane] = passed(one_ref, plane)
    for plane in (1, 2, slab + 3, slab + 4):
        clear(two_ref, plane)
    for plane in range(2, slab + 4):
        one_ref[plane] = passed(two_ref, plane)
    for plane in (2, slab + 3):
        clear(one_ref, plane)
    for plane in range(3, slab + 3):
        out_ref[plane - 3] = passed(one_ref, plane)[MARGIN : tall - MARGIN]


def smooth(place, base, near, far, total_x, total_y):
    slab, tall, lanes = base.shape
    return pl.pallas_call(
        functools.partial(smooth_kernel, total_x, total_y),
        in_specs=[pl.BlockSpec(memory_space=pltpu.SMEM)]
        + [pl.BlockSpec(memory_space=pltpu.VMEM)] * 3,
        out_specs=pl.BlockSpec(memory_space=pltpu.VMEM),
        out_shape=pltpu.VMEM((slab, tall - 2 * MARGIN, lanes), jnp.float32),
        scratch_shapes=[pltpu.VMEM((slab + 6, tall, lanes), jnp.float32)] * 2,
        compiler_params=pltpu.CompilerParams(vmem_limit_bytes=SMALL_VMEM),
        cost_estimate=pl.CostEstimate(flops=SMOOTH_FLOPS, bytes_accessed=1024, transcendentals=0),
    )(place, base, near, far)


def add_near_kernel(total_y, place_ref, late_vmem, before_ref, out_ref):
    pieces, tall, lanes = late_vmem.shape
    slab, band = before_ref.shape[:2]
    even = place_ref[0] == 0
    first = jnp.where(even, slab - 4, 0)
    out_ref[...] = before_ref[...]
    smoothed = Pass(tall, lanes, place_ref[2], total_y)
    lower, upper = (
        functools.reduce(jnp.add, [late_vmem[i] for i in range(which, pieces, 2)]) for which in range(2)
    )
    zero = jnp.zeros_like(lower)
    planes = {-1: jnp.where(even, upper, lower), 0: jnp.where(even, lower, upper)}
    for reach in (1, 2, 3):
        low, high = max(-1 - reach, reach - 4), min(reach, 3)
        planes = {
            at: smoothed(planes.get(at - 1, zero), planes.get(at, zero), planes.get(at + 1, zero))
            for at in range(low, high + 1)
        }
    for at in range(4):
        out_ref[first + jnp.where(even, 3 - at, at)] += planes[at][MARGIN : tall - MARGIN]


def add_near(place, late, before, total_y):
    slab, band, lanes = before.shape
    return pl.pallas_call(
        functools.partial(add_near_kernel, total_y),
        in_specs=[pl.BlockSpec(memory_space=pltpu.SMEM)] + [pl.BlockSpec(memory_space=pltpu.VMEM)] * 2,
        out_specs=pl.BlockSpec(memory_space=pltpu.VMEM),
        out_shape=jax.ShapeDtypeStruct(before.shape, jnp.float32),
        compiler_params=pltpu.CompilerParams(vmem_limit_bytes=SMALL_VMEM),
        cost_estimate=QUICK,
    )(place, late, before)


def swap(block, axis, pairs):
    return lax.ppermute(block, axis, [p for a, b in pairs for p in ((a, b), (b, a))])


def trade(pieces, pairs):
    slabs = lax.axis_size("space")
    groups = [[f * slabs + s for f in range(lax.axis_size("freq")) for s in pair] for pair in pairs]
    return lax.all_to_all(pieces, ("freq", "space"), 0, 0, axis_index_groups=groups, tiled=True)


def hbm(block):
    return pltpu.with_memory_space_constraint(block, pltpu.HBM)


def split_kernel(side_ref, found_ref, send_ref, keep_ref):
    half = keep_ref.shape[0]
    which = side_ref[1] // 2 % 2
    for ref, side in ((keep_ref, which), (send_ref, 1 - which)):
        for piece in range(half):
            at = side * half + piece
            ref[piece] = found_ref[at] + found_ref[2 * half + at]


def split(sides, found):
    shape = (found.shape[0] // 4,) + found.shape[1:]
    return pl.pallas_call(
        split_kernel,
        in_specs=[pl.BlockSpec(memory_space=pltpu.SMEM), pl.BlockSpec(memory_space=pltpu.VMEM)],
        out_specs=[pl.BlockSpec(memory_space=pltpu.VMEM)] * 2,
        out_shape=[jax.ShapeDtypeStruct(shape, jnp.float32)] * 2,
        compiler_params=pltpu.CompilerParams(vmem_limit_bytes=SMALL_VMEM),
        cost_estimate=QUICK,
    )(sides, found)


def base_kernel(side_ref, keep_ref, found_ref, *refs):
    base_ref, near_ref, far_ref = refs[-3:]
    slab, depth = base_ref.shape[0], near_ref.shape[0]
    base_ref[...] = keep_ref[0] + found_ref[0]
    start = (1 - side_ref[0]) * (slab - depth)
    near_ref[...] = base_ref[pl.ds(start, depth)]
    far_ref[...] = base_ref[pl.ds(slab - depth - start, depth)]


def finish_base(sides, keep, found, after):
    _, slab, tall, lanes = keep.shape
    return pl.pallas_call(
        base_kernel,
        in_specs=[pl.BlockSpec(memory_space=pltpu.SMEM)]
        + [pl.BlockSpec(memory_space=pltpu.VMEM)] * 2
        + [pl.BlockSpec(memory_space=pl.ANY)] * len(after),
        out_specs=[pl.BlockSpec(memory_space=pltpu.VMEM)] * 3,
        out_shape=[jax.ShapeDtypeStruct((count, tall, lanes), jnp.float32) for count in (slab, 3, 3)],
        compiler_params=pltpu.CompilerParams(vmem_limit_bytes=SMALL_VMEM),
        cost_estimate=QUICK,
    )(sides, keep, found, *after)


def band_sum(sides, turns):
    count = lax.axis_size("freq")
    groups = [[i, i + 1] for i in range(0, count, 2)]
    send, keep = split(sides, lax.all_to_all(turns, "freq", 0, 0, axis_index_groups=groups, tiled=True))
    found = lax.ppermute(send, "freq", [(i, i ^ 2) for i in range(count)])
    return finish_base(sides, keep, found, [])


def local(saved_modes, mode_gains):
    _, modes, kinds, halves, parts, slab, rows, lanes = saved_modes.shape
    freqs = lax.axis_size("freq")
    slabs = lax.axis_size("space")
    factor = -2.0 / (saved_modes.shape[0] * freqs * modes)
    weights = (factor / 8.0) * mode_gains
    place = lax.axis_index("space")
    odd = place % 2
    near_pairs = [(i, i + 1) for i in range(0, slabs - 1, 2)]
    far_pairs = [(i, i + 1) for i in range(1, slabs - 1, 2)]

    def outer(plane, begin, count):
        start = (0, begin, 0, 0, 0, plane, 0, 0)
        found = lax.dynamic_slice(saved_modes, start, (1, count, kinds, halves, parts, 1, rows, lanes))
        return found.reshape((count, kinds, halves, parts, rows, lanes))

    last = modes - 1
    near_plane = jnp.where(odd == 0, slab - 1, 0)
    (far_out,) = planes(saved_modes, slab - 1 - near_plane, [(0, modes)], [])
    far_halo = swap(far_out, "space", far_pairs)
    near_out, last_out = planes(saved_modes, near_plane, [(0, last), (last, 1)], [far_out])
    near_halo = swap(near_out, "space", near_pairs)

    sides = jnp.stack([odd, lax.axis_index("freq")]).astype(jnp.int32)
    sens, near_edges, far_edges = interior(saved_modes, weights, sides, [near_out])
    base, near, far = band_sum(sides, finish_far(sides, weights, far_edges, far_halo, sens, freqs))
    near, far = swap(near, "space", near_pairs), swap(far, "space", far_pairs)
    where = jnp.stack([odd, place * slab, lax.axis_index("freq") * (rows // freqs)]).astype(jnp.int32)
    smoothed = smooth(where, base, near, far, slab * slabs, rows)

    last_halo = swap(last_out, "space", near_pairs)
    near_late, last_edges = near_part(weights, hbm(near_edges), hbm(near_halo), [base])
    near_late = finish_near(last, weights, last_edges, last_halo, near_late, 2 * freqs, [])
    return add_near(where, trade(near_late, near_pairs), smoothed, rows)


def solution(mesh):
    in_specs = (P("freq", None, None, None, None, "space", None, None), P("freq", None))
    out_specs = P("space", "freq", None)
    return jax.shard_map(local, mesh=mesh, in_specs=in_specs, out_specs=out_specs, check_vma=False)
```

time: 101 us -> 89.5 us (0.89)
  Pallas kernels: 52.4 us -> 34.3 us
  starting transfers between devices: 19.7 us -> 35.3 us
  waiting for transfers between devices: 22.6 us -> 14.2 us
  blocking collectives: 0 us -> 5 us
  local copies, waits for them, and re-layouts: 4.85 us -> 0.01 us
  other arithmetic: 1.43 us -> 0.16 us
    ppermute x6 -> x1, waiting for transfers between devices: 22 us -> 0.01 us  [band_sum(): found = lax.ppermute(send, 'freq', [(i, i ^ 2) for i in range(count)])]
    pallas_call x3 -> x9, Pallas kernels: 50.3 us -> 32.9 us  [the longest x1 20.8 us: interior(): pl.pallas_call(functools.partial(interior_kernel, len(after)), grid=(mode...]
    ppermute x6 -> x5, starting transfers between devices: 14.7 us -> 29 us  [swap(): lax.ppermute(block, axis, [p for a, b in pairs for p in ((a, b), (b, a))])]
    ppermute x6 -> x5, waiting for transfers between devices: 0.59 us -> 10.3 us  [swap(): lax.ppermute(block, axis, [p for a, b in pairs for p in ((a, b), (b, a))])]
    all_to_all x0 -> x1, blocking collectives: none -> 5 us  [band_sum(): lax.all_to_all(turns, 'freq', 0, 0, axis_index_groups=groups, tiled=True)]
    all_to_all x0 -> x1, starting transfers between devices: none -> 4.7 us  [trade(): lax.all_to_all(pieces, ('freq', 'space'), 0, 0, axis_index_groups=groups,...]
    squeeze x1 -> x0, local copies, waits for them, and re-layouts: 3.97 us -> none  [local(): lax.dynamic_index_in_dim(saved_modes[0], near_plane, 4, False)]
    all_to_all x0 -> x1, waiting for transfers between devices: none -> 3.89 us  [trade(): lax.all_to_all(pieces, ('freq', 'space'), 0, 0, axis_index_groups=groups,...]
  transfers between devices with their start and end apart: 12 -> 7, of which waited for: 7 -> 3; matrix products, arithmetic and copies ran while one was open for 2% -> 0% of each run, Pallas kernels for 50% -> 35%
where the time goes in v2:
time: 89.5 us; the launch traced here: 89.1 us
  starting transfers between devices  35.3 us (39%)
  Pallas kernels  34.3 us (38%)
  waiting for transfers between devices  14.2 us (16%)
  blocking collectives  5 us (6%)
    ppermute x5, starting transfers between devices, swap(): lax.ppermute(block, axis, [p for a, b in pairs for p in ((a, b), (b, a))])  29 us
    pallas_call x1, Pallas kernels, interior(): pl.pallas_call(functools.partial(interior_kernel, len(after)), grid=(mode...  20.8 us
    ppermute x5, waiting for transfers between devices, swap(): lax.ppermute(block, axis, [p for a, b in pairs for p in ((a, b), (b, a))])  10.3 us
    all_to_all x1, blocking collectives, band_sum(): lax.all_to_all(turns, 'freq', 0, 0, axis_index_groups=groups, tiled=True)  5 us
    all_to_all x1, starting transfers between devices, trade(): lax.all_to_all(pieces, ('freq', 'space'), 0, 0, axis_index_groups=groups,...  4.7 us
    all_to_all x1, waiting for transfers between devices, trade(): lax.all_to_all(pieces, ('freq', 'space'), 0, 0, axis_index_groups=groups,...  3.89 us
    pallas_call x2, Pallas kernels, planes(): pl.pallas_call(functools.partial(plane_kernel, [first for first, _ in gro...  3.82 us
    pallas_call x1, Pallas kernels, near_part(): pl.pallas_call(near_part_kernel, grid=(1,), in_specs=[pl.BlockSpec(memory...  3.13 us
  transfers between devices with their start and end apart: 7, of which 3 were waited for; matrix products, arithmetic and copies ran while one was open for 0% of the time, Pallas kernels for 35%

profile of v2, /device:TPU:0, one launch (start us, length us, event | category | flops | bytes accessed | tf_op | source)
XLA Modules:
  0.0 89.1 jit_solution(10285360156487624302)
XLA Ops:
  0.0 1.4 %shard_map.28.refs_0_ = bf16[4,2,2,3,128,128]{5,4,3,2,1,0:T(8,128)(2,1)S(1)} custom-call(s32[1]{0:T(128)} %bitcast.5.plane_ref, bf16[1,4,2,2,3,16,128,128]{7,6,5,4,3,2,1,0:T(8,128)(2,1)} %modes_ref.5), custom_call_target="tpu_custom_call" | custom-call | flops 1024 | bytes 1024 | tf_op jit(solution)/shard_map/pallas_call | solution.py:34
  1.4 0.8 collective-permute-start.1
  2.2 0.0 copy-start
  2.2 2.4 %shard_map.29 = (bf16[3,2,2,3,128,128]{5,4,3,2,1,0:T(8,128)(2,1)}, bf16[1,2,2,3,128,128]{5,4,3,2,1,0:T(8,128)(2,1)S(1)}) custom-call(s32[1]{0:T(128)} %bitcast.4.plane_ref, bf16[1,4,2,2,3,16,128,128]{7,6,5,4,3,2,1,0:T(8,128)(2,1)} %modes_ref.5, bf16[4,2,2,3,128,128]{5,4,3,2,1,0:T(8,128)(2,1)S(1)} %shard_map.28.refs_0_), custom_call_target="tpu_custom_call" | custom-call | flops 1024 | bytes 1024 | tf_op jit(solution)/shard_map/pallas_call | solution.py:34
  4.6 5.7 %collective-permute-start = (bf16[3,2,2,3,128,128]{5,4,3,2,1,0:T(8,128)(2,1)}, bf16[3,2,2,3,128,128]{5,4,3,2,1,0:T(8,128)(2,1)}, u32[]{:S(2)}, u32[]{:S(2)}) collective-permute-start(bf16[3,2,2,3,128,128]{5,4,3,2,1,0:T(8,128)(2,1)} %get-tuple-element.17.refs_0_), channel_id=1, source_target_pairs={{0,1},{1,0},{2,3},{3,2},{4,5},{5,4},{6,7},{7,6},{8,9},{9,8},{10,11... | collective-permute-start | bytes 3538952 | tf_op jit(solution)/shard_map/ppermute | solution.py:396
  10.3 0.1 pad_add_fusion.1.side_ref
  10.4 0.0 copy-done
  10.4 20.8 %shard_map.30 = (f32[16,144,128]{2,1,0:T(8,128)S(1)}, f32[4,2,2,3,128,128]{5,4,3,2,1,0:T(8,128)}, f32[4,2,2,3,128,128]{5,4,3,2,1,0:T(8,128)S(1)}) custom-call(s32[2]{0:T(128)S(1)} %pad_add_fusion.1.side_ref, f32[1,4]{1,0:T(1,128)S(1)} %broadcast_multiply_fusion.weight_ref, bf16[1,4,2,2,3,16,128,128]{7,6,5,4,3,2,1,0:T(8,128)(2,1)} %modes_ref.5, ...), custom_call_target="tpu_custom_call" | custom-call | flops 8000000000 | bytes 1024 | tf_op jit(solution)/shard_map/pallas_call | solution.py:145
  31.2 0.0 collective-permute-done.1.halo_ref
  31.2 1.1 %shard_map.31 = f32[4,16,48,128]{3,2,1,0:T(8,128)S(1)} custom-call(s32[2]{0:T(128)S(1)} %pad_add_fusion.1.side_ref, f32[1,4]{1,0:T(1,128)S(1)} %broadcast_multiply_fusion.weight_ref, f32[4,2,2,3,128,128]{5,4,3,2,1,0:T(8,128)S(1)} %get-tuple-element.19.edge_ref, bf16[4,2,2,3,128,128]{5,4,3,2,1,0:T(8,128)(2,1)S(1)} %collective-permute-done.1.halo_ref, ...), custom_call_target="tpu_custom_call" | custom-call | flops 1024 | bytes 1024 | tf_op jit(solution)/shard_map/pallas_call | solution.py:211
  32.3 5.0 %all_to_all.10.found_ref = f32[4,16,48,128]{3,2,1,0:T(8,128)S(1)} all-to-all(f32[4,16,48,128]{3,2,1,0:T(8,128)S(1)} %shard_map.31), channel_id=1, replica_groups={{0,8},{16,24},{1,9},{17,25},{2,10},{18,26},{3,11},{19,27},{4,12},{20,28..., dimensions={0} | all-to-all | bytes 3145728 | tf_op jit(solution)/shard_map/all_to_all | solution.py:456
  37.3 0.6 shard_map.32
  37.9 1.6 %collective-permute-start.2 = (f32[1,16,48,128]{3,2,1,0:T(8,128)S(1)}, f32[1,16,48,128]{3,2,1,0:T(8,128)S(1)}, u32[]{:S(2)}, u32[]{:S(2)}) collective-permute-start(f32[1,16,48,128]{3,2,1,0:T(8,128)S(1)} %get-tuple-element.22), channel_id=1, source_target_pairs={{0,16},{8,24},{16,0},{24,8},{1,17},{9,25},{17,1},{25,9},{2,18},{10... | collective-permute-start | bytes 1179656 | tf_op jit(solution)/shard_map/ppermute | solution.py:457
  39.5 12.2 %collective-permute-start.3 = (bf16[1,2,2,3,128,128]{5,4,3,2,1,0:T(8,128)(2,1)S(1)}, bf16[1,2,2,3,128,128]{5,4,3,2,1,0:T(8,128)(2,1)S(1)}, u32[]{:S(2)}, u32[]{:S(2)}) collective-permute-start(bf16[1,2,2,3,128,128]{5,4,3,2,1,0:T(8,128)(2,1)S(1)} %get-tuple-element.25), channel_id=1, source_target_pairs={{0,1},{1,0},{2,3},{3,2},{4,5},{5,4},{6,7},{7,6},{8,9},{9,8},{10,11... | collective-permute-start | bytes 1179656 | tf_op jit(solution)/shard_map/ppermute | solution.py:396
  51.7 0.0 collective-permute-done.2.found_ref
  51.7 0.6 shard_map.33
  52.3 9.7 %collective-permute-start.4 = (f32[3,48,128]{2,1,0:T(8,128)S(1)}, f32[3,48,128]{2,1,0:T(8,128)S(1)}, u32[]{:S(2)}, u32[]{:S(2)}) collective-permute-start(f32[3,48,128]{2,1,0:T(8,128)S(1)} %get-tuple-element.27), channel_id=1, source_target_pairs={{0,1},{1,0},{2,3},{3,2},{4,5},{5,4},{6,7},{7,6},{8,9},{9,8},{10,11... | collective-permute-start | bytes 221192 | tf_op jit(solution)/shard_map/ppermute | solution.py:396
  62.0 0.7 collective-permute-start.5
  62.7 0.1 pad_add_fusion.place_ref
  62.8 5.1 %collective-permute-done.halo_ref = bf16[3,2,2,3,128,128]{5,4,3,2,1,0:T(8,128)(2,1)} collective-permute-done((bf16[3,2,2,3,128,128]{5,4,3,2,1,0:T(8,128)(2,1)}, bf16[3,2,2,3,128,128]{5,4,3,2,1,0:T(8,128)(2,1)}, u32[]{:S(2)}, u32[]{:S(2)}) %collective-permute-start) | collective-permute-done | bytes 1179680 | tf_op jit(solution)/shard_map/ppermute | solution.py:396
  67.9 3.1 %shard_map.34 = (f32[128,128]{1,0:T(8,128)S(1)}, f32[1,2,2,3,128,128]{5,4,3,2,1,0:T(8,128)S(1)}) custom-call(f32[1,4]{1,0:T(1,128)S(1)} %broadcast_multiply_fusion.weight_ref, f32[4,2,2,3,128,128]{5,4,3,2,1,0:T(8,128)} %get-tuple-element.18.edge_ref.last_ref, bf16[3,2,2,3,128,128]{5,4,3,2,1,0:T(8,128)(2,1)} %collective-permute-done.halo_ref, ...), custom_call_target="tpu_custom_call" | custom-call | flops 1024 | bytes 1024 | tf_op jit(solution)/shard_map/pallas_call | solution.py:234
  71.0 5.2 %collective-permute-done.3.halo_ref = bf16[1,2,2,3,128,128]{5,4,3,2,1,0:T(8,128)(2,1)S(1)} collective-permute-done((bf16[1,2,2,3,128,128]{5,4,3,2,1,0:T(8,128)(2,1)S(1)}, bf16[1,2,2,3,128,128]{5,4,3,2,1,0:T(8,128)(2,1)S(1)}, u32[]{:S(2)}, u32[]{:S(2)}) %collective-permute-start.3) | collective-permute-done | bytes 393248 | tf_op jit(solution)/shard_map/ppermute | solution.py:396
  76.2 1.3 %shard_map.35 = f32[8,48,128]{2,1,0:T(8,128)} custom-call(f32[1,4]{1,0:T(1,128)S(1)} %broadcast_multiply_fusion.weight_ref, f32[1,2,2,3,128,128]{5,4,3,2,1,0:T(8,128)S(1)} %get-tuple-element.24.edge_ref, bf16[1,2,2,3,128,128]{5,4,3,2,1,0:T(8,128)(2,1)S(1)} %collective-permute-done.3.halo_ref, f32[128,128]{1,0:T(8,128)S(1)} %get-tuple-element.26.before_ref), custom_call_target="tpu_custom_call" | custom-call | flops 1024 | bytes 1024 | tf_op jit(solution)/shard_map/pallas_call | solution.py:278
  77.6 4.7 %all-to-all-start.1 = ((f32[8,48,128]{2,1,0:T(8,128)}), f32[8,48,128]{2,1,0:T(8,128)S(1)}, u32[]{:S(2)}, u32[]{:S(2)}) async-start(f32[8,48,128]{2,1,0:T(8,128)} %shard_map.35), calls=%async_computation.1 | async-start | bytes 393216 | tf_op jit(solution)/shard_map/all_to_all | solution.py:402
  82.3 0.0 collective-permute-done.4.near_ref
  82.3 0.0 collective-permute-done.5.far_ref
  82.3 1.4 %shard_map.36.before_ref = f32[16,32,128]{2,1,0:T(8,128)S(1)} custom-call(s32[3]{0:T(128)S(1)} %pad_add_fusion.place_ref, f32[16,48,128]{2,1,0:T(8,128)S(1)} %get-tuple-element.23.refs_0_.base_ref, f32[3,48,128]{2,1,0:T(8,128)S(1)} %collective-permute-done.4.near_ref, f32[3,48,128]{2,1,0:T(8,128)S(1)} %collective-permute-done.5.far_ref), custom_call_target="tpu_custom_call" | custom-call | flops 10000000000 | bytes 1024 | tf_op jit(solution)/shard_map/pallas_call | solution.py:349
  83.7 3.9 %all-to-all-done.1.late_vmem = f32[8,48,128]{2,1,0:T(8,128)S(1)} async-done(((f32[8,48,128]{2,1,0:T(8,128)}), f32[8,48,128]{2,1,0:T(8,128)S(1)}, u32[]{:S(2)}, u32[]{:S(2)}) %all-to-all-start.1) | async-done | bytes 196640 | tf_op jit(solution)/shard_map/all_to_all | solution.py:402
  87.6 1.5 %shard_map.37 = f32[16,32,128]{2,1,0:T(8,128)} custom-call(s32[3]{0:T(128)S(1)} %pad_add_fusion.place_ref, f32[8,48,128]{2,1,0:T(8,128)S(1)} %all-to-all-done.1.late_vmem, f32[16,32,128]{2,1,0:T(8,128)S(1)} %shard_map.36.before_ref), custom_call_target="tpu_custom_call" | custom-call | flops 1024 | bytes 1024 | tf_op jit(solution)/shard_map/pallas_call | solution.py:385
  (1 shorter events, 0.0 us)
Async XLA Ops:
  1.4 29.8 %collective-permute-start.1 = (bf16[4,2,2,3,128,128]{5,4,3,2,1,0:T(8,128)(2,1)S(1)}, bf16[4,2,2,3,128,128]{5,4,3,2,1,0:T(8,128)(2,1)S(1)}, u32[]{:S(2)}, u32[]{:S(2)}) collective-permute-start(bf16[4,2,2,3,128,128]{5,4,3,2,1,0:T(8,128)(2,1)S(1)} %shard_map.28.refs_0_), channel_id=1, source_target_pairs={{1,2},{2,1},{3,4},{4,3},{5,6},{6,5},{9,10},{10,9},{11,12},{12,11},... | collective-permute-start | bytes 4718600 | tf_op jit(solution)/shard_map/ppermute | solution.py:396
  2.2 8.2 %copy-start = (f32[1,4]{1,0:T(1,128)S(1)}, f32[1,4]{1,0:T(1,128)}, u32[]{:S(2)}) copy-start(f32[1,4]{1,0:T(1,128)} %param.3) | copy-start | bytes 52
  4.6 63.3 %collective-permute-start = (bf16[3,2,2,3,128,128]{5,4,3,2,1,0:T(8,128)(2,1)}, bf16[3,2,2,3,128,128]{5,4,3,2,1,0:T(8,128)(2,1)}, u32[]{:S(2)}, u32[]{:S(2)}) collective-permute-start(bf16[3,2,2,3,128,128]{5,4,3,2,1,0:T(8,128)(2,1)} %get-tuple-element.17.refs_0_), channel_id=1, source_target_pairs={{0,1},{1,0},{2,3},{3,2},{4,5},{5,4},{6,7},{7,6},{8,9},{9,8},{10,11... | collective-permute-start | bytes 3538952 | tf_op jit(solution)/shard_map/ppermute | solution.py:396
  37.9 13.7 %collective-permute-start.2 = (f32[1,16,48,128]{3,2,1,0:T(8,128)S(1)}, f32[1,16,48,128]{3,2,1,0:T(8,128)S(1)}, u32[]{:S(2)}, u32[]{:S(2)}) collective-permute-start(f32[1,16,48,128]{3,2,1,0:T(8,128)S(1)} %get-tuple-element.22), channel_id=1, source_target_pairs={{0,16},{8,24},{16,0},{24,8},{1,17},{9,25},{17,1},{25,9},{2,18},{10... | collective-permute-start | bytes 1179656 | tf_op jit(solution)/shard_map/ppermute | solution.py:457
  39.5 36.7 %collective-permute-start.3 = (bf16[1,2,2,3,128,128]{5,4,3,2,1,0:T(8,128)(2,1)S(1)}, bf16[1,2,2,3,128,128]{5,4,3,2,1,0:T(8,128)(2,1)S(1)}, u32[]{:S(2)}, u32[]{:S(2)}) collective-permute-start(bf16[1,2,2,3,128,128]{5,4,3,2,1,0:T(8,128)(2,1)S(1)} %get-tuple-element.25), channel_id=1, source_target_pairs={{0,1},{1,0},{2,3},{3,2},{4,5},{5,4},{6,7},{7,6},{8,9},{9,8},{10,11... | collective-permute-start | bytes 1179656 | tf_op jit(solution)/shard_map/ppermute | solution.py:396
  52.3 30.0 %collective-permute-start.4 = (f32[3,48,128]{2,1,0:T(8,128)S(1)}, f32[3,48,128]{2,1,0:T(8,128)S(1)}, u32[]{:S(2)}, u32[]{:S(2)}) collective-permute-start(f32[3,48,128]{2,1,0:T(8,128)S(1)} %get-tuple-element.27), channel_id=1, source_target_pairs={{0,1},{1,0},{2,3},{3,2},{4,5},{5,4},{6,7},{7,6},{8,9},{9,8},{10,11... | collective-permute-start | bytes 221192 | tf_op jit(solution)/shard_map/ppermute | solution.py:396
  62.0 20.2 %collective-permute-start.5 = (f32[3,48,128]{2,1,0:T(8,128)S(1)}, f32[3,48,128]{2,1,0:T(8,128)S(1)}, u32[]{:S(2)}, u32[]{:S(2)}) collective-permute-start(f32[3,48,128]{2,1,0:T(8,128)S(1)} %get-tuple-element.28), channel_id=1, source_target_pairs={{1,2},{2,1},{3,4},{4,3},{5,6},{6,5},{9,10},{10,9},{11,12},{12,11},... | collective-permute-start | bytes 221192 | tf_op jit(solution)/shard_map/ppermute | solution.py:396
  77.6 10.0 %all-to-all-start.1 = ((f32[8,48,128]{2,1,0:T(8,128)}), f32[8,48,128]{2,1,0:T(8,128)S(1)}, u32[]{:S(2)}, u32[]{:S(2)}) async-start(f32[8,48,128]{2,1,0:T(8,128)} %shard_map.35), calls=%async_computation.1 | async-start | bytes 393216 | tf_op jit(solution)/shard_map/all_to_all | solution.py:402

commit v3 on v2

--- a/solution.py
+++ b/solution.py
@@ -10,8 +10,9 @@
 AXIAL = 0.35
 CROSS = 0.06
 MARGIN = 8
+EDGE = 4
 STEP = 16
-INTERIOR_VMEM = 36 * 1024 * 1024
+INTERIOR_VMEM = 30 * 1024 * 1024
 QUICK = pl.CostEstimate(flops=1024, bytes_accessed=1024, transcendentals=0)
 INTERIOR_FLOPS = 8 * 10**9
 SMOOTH_FLOPS = 10**10
@@ -45,14 +46,18 @@
     )(plane.reshape(1).astype(jnp.int32), hbm(saved_modes), *after)
 
 
-def interior_kernel(after, side_ref, weight_ref, modes_ref, *refs):
-    sens_ref, near_edge_ref, far_edge_ref, wide_ref, lane_ref = refs[after:]
+def interior_kernel(begin, before, after, side_ref, weight_ref, modes_ref, *refs):
+    sens_ref, token_ref, near_edge_ref, far_edge_ref, wide_ref, lane_ref = refs[before + after :]
     slab, rows, lanes = modes_ref.shape[2:]
 
     @pl.when((pl.program_id(0) == 0) & (pl.program_id(1) == 0))
     def _():
-        sens_ref[...] = jnp.zeros_like(sens_ref)
-        wide_ref[...] = jnp.zeros_like(wide_ref)
+        sens_ref[...] = refs[0][...] if before else jnp.zeros_like(sens_ref)
+        token_ref[...] = jnp.zeros_like(token_ref)
+        for plane in (0, slab + 1):
+            wide_ref[:, plane] = jnp.zeros_like(wide_ref[:, plane])
+        for start in (0, MARGIN + rows):
+            wide_ref[:, :, pl.ds(start, MARGIN)] = jnp.zeros_like(wide_ref[:, :, pl.ds(start, MARGIN)])
 
     source = lax.broadcasted_iota(jnp.int32, (lanes, lanes), 0)
     target = lax.broadcasted_iota(jnp.int32, (lanes, lanes), 1)
@@ -61,7 +66,7 @@
     lane = lax.broadcasted_iota(jnp.int32, (STEP, lanes), 1)
     not_last = jnp.where(lane == lanes - 1, 0.0, 1.0)
     not_first = jnp.where(lane == 0, 0.0, 1.0)
-    scale = weight_ref[0, pl.program_id(0)]
+    scale = weight_ref[0, begin + pl.program_id(0)]
 
     def load_plane(plane):
         for kind in range(2):
@@ -137,149 +142,161 @@
                 edge_ref[1, part, pl.ds(start, STEP)] = sign * ov[part]
 
 
-def interior(saved_modes, weights, sides, after):
-    _, modes, kinds, halves, parts, slab, rows, lanes = saved_modes.shape
+def interior(saved_modes, weights, sides, begin, count, before, after):
+    _, _, kinds, halves, parts, slab, rows, lanes = saved_modes.shape
     whole = (slab, rows + 2 * MARGIN, lanes)
-    edges = (modes, halves, kinds, parts, rows, lanes)
+    edges = (count, halves, kinds, parts, rows, lanes)
     fields = kinds * parts
     return pl.pallas_call(
-        functools.partial(interior_kernel, len(after)),
-        grid=(modes, halves),
+        functools.partial(interior_kernel, begin, len(before), len(after)),
+        grid=(count, halves),
         in_specs=[
             pl.BlockSpec(memory_space=pltpu.SMEM),
             pl.BlockSpec(memory_space=pltpu.SMEM),
             pl.BlockSpec(
                 (None, None, kinds, None, parts, slab, rows, lanes),
-                lambda m, c: (0, m, 0, c, 0, 0, 0, 0),
+                lambda m, c: (0, begin + m, 0, c, 0, 0, 0, 0),
             ),
         ]
+        + [pl.BlockSpec(memory_space=pltpu.VMEM)] * len(before)
         + [pl.BlockSpec(memory_space=pl.ANY)] * len(after),
-        out_specs=[pl.BlockSpec(whole, lambda m, c: (0, 0, 0))]
+        out_specs=[
+            pl.BlockSpec(whole, lambda m, c: (0, 0, 0)),
+            pl.BlockSpec((8, lanes), lambda m, c: (0, 0)),
+        ]
         + [pl.BlockSpec((None, None) + edges[2:], lambda m, c: (m, c, 0, 0, 0, 0))] * 2,
-        out_shape=[pltpu.VMEM(whole, jnp.float32), pltpu.HBM(edges, jnp.float32), pltpu.VMEM(edges, jnp.float32)],
+        out_shape=[
+            pltpu.VMEM(whole, jnp.float32),
+            jax.ShapeDtypeStruct((8, lanes), jnp.float32),
+            pltpu.HBM(edges, jnp.float32),
+            pltpu.VMEM(edges, jnp.float32),
+        ],
         scratch_shapes=[
             pltpu.VMEM((fields, slab + 2, rows + 2 * MARGIN, lanes), jnp.float32),
             pltpu.VMEM((fields, slab, rows, lanes), jnp.float32),
         ],
         compiler_params=pltpu.CompilerParams(vmem_limit_bytes=INTERIOR_VMEM),
         cost_estimate=pl.CostEstimate(flops=INTERIOR_FLOPS, bytes_accessed=1024, transcendentals=0),
-    )(sides, weights, saved_modes, *after)
-
-
-def outer_plane(weight_ref, edge_ref, halo_ref, begin, start):
-    modes, halves, _, parts = edge_ref.shape[:4]
+    )(sides, weights, saved_modes, *before, *after)
+
+
+def strain_of(ref, mode):
+    return lambda half, kind, part, start: ref[mode, half, kind, part, pl.ds(start, STEP)]
+
+
+def halo_of(ref, mode):
+    return lambda half, kind, part, start: ref[mode, kind, half, part, pl.ds(start, STEP)]
+
+
+def outer_plane(start, shape, scales, strains, halos):
+    halves, parts = shape
     total = None
-    for mode in range(modes):
+    for scale, strain, halo in zip(scales, strains, halos, strict=True):
         found = None
         for half in range(halves):
             for part in range(parts):
                 u, v = (
-                    edge_ref[mode, half, kind, part, pl.ds(start, STEP)]
-                    + halo_ref[mode, kind, half, part, pl.ds(start, STEP)].astype(jnp.float32)
+                    strain(half, kind, part, start) + halo(half, kind, part, start).astype(jnp.float32)
                     for kind in range(2)
                 )
                 term = u * v
                 if part == 0:
                     term = 2.0 * term
                 found = term if found is None else found + term
-        found = weight_ref[0, begin + mode] * found
+        found = scale * found
         total = found if total is None else total + found
     return total
 
 
-def far_kernel(side_ref, weight_ref, edge_ref, halo_ref, sens_ref, turns_ref, tall_ref):
+def far_kernel(groups, side_ref, weight_ref, edge_ref, *refs):
+    halo_refs = refs[:-3]
+    sens_ref, turns_ref, tall_ref = refs[-3:]
+    scales, strains, halos = [], [], []
+    for (begin, count), halo_ref in zip(groups, halo_refs, strict=True):
+        for mode in range(begin, begin + count):
+            scales.append(weight_ref[0, mode])
+            strains.append(strain_of(edge_ref, mode))
+            halos.append(halo_of(halo_ref, mode - begin))
     slab = sens_ref.shape[0]
-    rows = edge_ref.shape[4]
+    _, halves, _, parts, rows, _ = edge_ref.shape
     count, _, tall, _ = turns_ref.shape
-    band = tall - 2 * MARGIN
+    band = tall - 2 * EDGE
     far = side_ref[0] * (slab - 1)
     tall_ref[...] = sens_ref[far]
     for start in range(0, rows, STEP):
-        tall_ref[pl.ds(MARGIN + start, STEP)] += outer_plane(weight_ref, edge_ref, halo_ref, 0, start)
+        tall_ref[pl.ds(MARGIN + start, STEP)] += outer_plane(start, (halves, parts), scales, strains, halos)
     for piece in range(count):
         index, bits = 0, 1
         while bits < count:
             index = 2 * index + (piece // bits) % 2
             bits *= 2
-        turns_ref[piece] = sens_ref[:, pl.ds(index * band, tall)]
-        turns_ref[piece, far] = tall_ref[pl.ds(index * band, tall)]
-
-
-def finish_far(sides, weights, edges, halo, sens, freqs):
+        start = index * band + MARGIN - EDGE
+        turns_ref[piece] = sens_ref[:, pl.ds(start, tall)]
+        turns_ref[piece, far] = tall_ref[pl.ds(start, tall)]
+
+
+def finish_far(sides, weights, groups, edges, halos, sens, freqs):
     slab, rows, lanes = sens.shape
     band = (rows - 2 * MARGIN) // freqs
     return pl.pallas_call(
-        far_kernel,
-        in_specs=[pl.BlockSpec(memory_space=pltpu.SMEM)] * 2 + [pl.BlockSpec(memory_space=pltpu.VMEM)] * 3,
+        functools.partial(far_kernel, groups),
+        in_specs=[pl.BlockSpec(memory_space=pltpu.SMEM)] * 2
+        + [pl.BlockSpec(memory_space=pltpu.VMEM)] * (len(halos) + 2),
         out_specs=pl.BlockSpec(memory_space=pltpu.VMEM),
-        out_shape=jax.ShapeDtypeStruct((freqs, slab, band + 2 * MARGIN, lanes), jnp.float32),
+        out_shape=jax.ShapeDtypeStruct((freqs, slab, band + 2 * EDGE, lanes), jnp.float32),
         scratch_shapes=[pltpu.VMEM((rows, lanes), jnp.float32)],
         compiler_params=pltpu.CompilerParams(vmem_limit_bytes=SMALL_VMEM),
         cost_estimate=QUICK,
-    )(sides, weights, edges, halo, sens)
-
-
-def near_part_kernel(weight_ref, edge_ref, halo_ref, last_ref, *refs):
-    out_ref, kept_ref, done = refs[-3:]
-    copy = pltpu.make_async_copy(last_ref.at[last_ref.shape[0] - 1], kept_ref.at[0], done)
-    copy.start()
-    for start in range(0, out_ref.shape[0], STEP):
-        out_ref[pl.ds(start, STEP)] = outer_plane(weight_ref, edge_ref, halo_ref, 0, start)
-    copy.wait()
-
-
-def near_part(weights, edges, halo, after):
-    count = halo.shape[0]
-    rows, lanes = edges.shape[4:]
-    return pl.pallas_call(
-        near_part_kernel,
-        grid=(1,),
-        in_specs=[
-            pl.BlockSpec(memory_space=pltpu.SMEM),
-            pl.BlockSpec((count,) + edges.shape[1:], lambda i: (0,) * 6),
-            pl.BlockSpec(halo.shape, lambda i: (0,) * 6),
-        ]
-        + [pl.BlockSpec(memory_space=pl.ANY)] * (1 + len(after)),
-        out_specs=[
-            pl.BlockSpec((rows, lanes), lambda i: (0, 0)),
-            pl.BlockSpec(memory_space=pltpu.VMEM),
-        ],
-        out_shape=[
-            pltpu.VMEM((rows, lanes), jnp.float32),
-            pltpu.VMEM((1,) + edges.shape[1:], jnp.float32),
-        ],
-        scratch_shapes=[pltpu.SemaphoreType.DMA(())],
-        compiler_params=pltpu.CompilerParams(vmem_limit_bytes=SMALL_VMEM),
-        cost_estimate=QUICK,
-    )(weights, edges, halo, edges, *after)
-
-
-def outer_kernel(begin, weight_ref, edge_ref, halo_ref, before_ref, *refs):
-    out_ref, tall_ref, band_ref, done = refs[-4:]
-    rows = edge_ref.shape[4]
+    )(sides, weights, edges, *halos, sens)
+
+
+def fetch_kernel(count, *refs):
+    sources, outs, sems = refs[:count], refs[-1 - count : -1], refs[-1]
+    copies = [pltpu.make_async_copy(sources[i], outs[i], sems.at[i]) for i in range(count)]
+    for copy in copies:
+        copy.start()
+    for copy in copies:
+        copy.wait()
+
+
+def fetch(blocks, after):
+    return pl.pallas_call(
+        functools.partial(fetch_kernel, len(blocks)),
+        in_specs=[pl.BlockSpec(memory_space=pl.ANY)] * (len(blocks) + len(after)),
+        out_specs=[pl.BlockSpec(memory_space=pltpu.VMEM)] * len(blocks),
+        out_shape=[pltpu.VMEM(block.shape, block.dtype) for block in blocks],
+        scratch_shapes=[pltpu.SemaphoreType.DMA((len(blocks),))],
+        compiler_params=pltpu.CompilerParams(vmem_limit_bytes=SMALL_VMEM),
+        cost_estimate=QUICK,
+    )(*[hbm(block) for block in blocks], *after)
+
+
+def near_kernel(weight_ref, edge_ref, halo_ref, out_ref, tall_ref, band_ref, done):
+    modes, halves, _, parts, rows, _ = edge_ref.shape
+    scales = [weight_ref[0, mode] for mode in range(modes)]
+    strains = [strain_of(edge_ref, mode) for mode in range(modes)]
+    halos = [halo_of(halo_ref, mode) for mode in range(modes)]
     pieces, tall, lanes = band_ref.shape
-    band = tall - 2 * MARGIN
+    band = tall - 2 * EDGE
     empty = jnp.zeros((MARGIN, lanes), jnp.float32)
     tall_ref[pl.ds(0, MARGIN)] = empty
     tall_ref[pl.ds(MARGIN + rows, MARGIN)] = empty
     for start in range(0, rows, STEP):
-        found = outer_plane(weight_ref, edge_ref, halo_ref, begin, start)
-        tall_ref[pl.ds(MARGIN + start, STEP)] = before_ref[pl.ds(start, STEP)] + found
+        tall_ref[pl.ds(MARGIN + start, STEP)] = outer_plane(start, (halves, parts), scales, strains, halos)
     for piece in range(pieces):
-        band_ref[piece] = tall_ref[pl.ds(piece // 2 * band, tall)]
+        band_ref[piece] = tall_ref[pl.ds(piece // 2 * band + MARGIN - EDGE, tall)]
     copy = pltpu.make_async_copy(band_ref, out_ref, done)
     copy.start()
     copy.wait()
 
 
-def finish_near(begin, weights, edges, halo, before, pieces, after):
-    rows, lanes = edges.shape[4:]
-    shape = (pieces, rows // (pieces // 2) + 2 * MARGIN, lanes)
-    return pl.pallas_call(
-        functools.partial(outer_kernel, begin),
+def finish_near(weights, edges, halo, pieces):
+    rows, lanes = halo.shape[4:]
+    shape = (pieces, rows // (pieces // 2) + 2 * EDGE, lanes)
+    return pl.pallas_call(
+        near_kernel,
         in_specs=[pl.BlockSpec(memory_space=pltpu.SMEM)]
-        + [pl.BlockSpec(memory_space=pltpu.VMEM)] * 3
-        + [pl.BlockSpec(memory_space=pl.ANY)] * len(after),
+        + [pl.BlockSpec(memory_space=pltpu.VMEM)] * 2,
         out_specs=pl.BlockSpec(memory_space=pltpu.HBM),
         out_shape=pltpu.HBM(shape, jnp.float32),
         scratch_shapes=[
@@ -289,14 +306,14 @@
         ],
         compiler_params=pltpu.CompilerParams(vmem_limit_bytes=SMALL_VMEM),
         cost_estimate=QUICK,
-    )(weights, edges, halo, before, *after)
+    )(weights, edges, halo)
 
 
 class Pass:
     def __init__(self, tall, lanes, first_y, total_y):
         self.tall, self.lanes = tall, lanes
         self.lane = lax.broadcasted_iota(jnp.int32, (tall, lanes), 1)
-        row = lax.broadcasted_iota(jnp.int32, (tall, lanes), 0) + (first_y - MARGIN)
+        row = lax.broadcasted_iota(jnp.int32, (tall, lanes), 0) + (first_y - EDGE)
         self.inside = (row >= 0) & (row < total_y)
 
     def __call__(self, below, center, above):
@@ -341,7 +358,7 @@
     for plane in (2, slab + 3):
         clear(one_ref, plane)
     for plane in range(3, slab + 3):
-        out_ref[plane - 3] = passed(one_ref, plane)[MARGIN : tall - MARGIN]
+        out_ref[plane - 3] = passed(one_ref, plane)[EDGE : tall - EDGE]
 
 
 def smooth(place, base, near, far, total_x, total_y):
@@ -351,7 +368,7 @@
         in_specs=[pl.BlockSpec(memory_space=pltpu.SMEM)]
         + [pl.BlockSpec(memory_space=pltpu.VMEM)] * 3,
         out_specs=pl.BlockSpec(memory_space=pltpu.VMEM),
-        out_shape=pltpu.VMEM((slab, tall - 2 * MARGIN, lanes), jnp.float32),
+        out_shape=pltpu.VMEM((slab, tall - 2 * EDGE, lanes), jnp.float32),
         scratch_shapes=[pltpu.VMEM((slab + 6, tall, lanes), jnp.float32)] * 2,
         compiler_params=pltpu.CompilerParams(vmem_limit_bytes=SMALL_VMEM),
         cost_estimate=pl.CostEstimate(flops=SMOOTH_FLOPS, bytes_accessed=1024, transcendentals=0),
@@ -377,7 +394,7 @@
             for at in range(low, high + 1)
         }
     for at in range(4):
-        out_ref[first + jnp.where(even, 3 - at, at)] += planes[at][MARGIN : tall - MARGIN]
+        out_ref[first + jnp.where(even, 3 - at, at)] += planes[at][EDGE : tall - EDGE]
 
 
 def add_near(place, late, before, total_y):
@@ -421,7 +438,7 @@
         split_kernel,
         in_specs=[pl.BlockSpec(memory_space=pltpu.SMEM), pl.BlockSpec(memory_space=pltpu.VMEM)],
         out_specs=[pl.BlockSpec(memory_space=pltpu.VMEM)] * 2,
-        out_shape=[jax.ShapeDtypeStruct(shape, jnp.float32)] * 2,
+        out_shape=[pltpu.VMEM(shape, jnp.float32)] * 2,
         compiler_params=pltpu.CompilerParams(vmem_limit_bytes=SMALL_VMEM),
         cost_estimate=QUICK,
     )(sides, found)
@@ -444,7 +461,7 @@
         + [pl.BlockSpec(memory_space=pltpu.VMEM)] * 2
         + [pl.BlockSpec(memory_space=pl.ANY)] * len(after),
         out_specs=[pl.BlockSpec(memory_space=pltpu.VMEM)] * 3,
-        out_shape=[jax.ShapeDtypeStruct((count, tall, lanes), jnp.float32) for count in (slab, 3, 3)],
+        out_shape=[pltpu.VMEM((count, tall, lanes), jnp.float32) for count in (slab, 3, 3)],
         compiler_params=pltpu.CompilerParams(vmem_limit_bytes=SMALL_VMEM),
         cost_estimate=QUICK,
     )(sides, keep, found, *after)
@@ -455,7 +472,7 @@
     groups = [[i, i + 1] for i in range(0, count, 2)]
     send, keep = split(sides, lax.all_to_all(turns, "freq", 0, 0, axis_index_groups=groups, tiled=True))
     found = lax.ppermute(send, "freq", [(i, i ^ 2) for i in range(count)])
-    return finish_base(sides, keep, found, [])
+    return *finish_base(sides, keep, found, []), keep
 
 
 def local(saved_modes, mode_gains):
@@ -474,23 +491,23 @@
         found = lax.dynamic_slice(saved_modes, start, (1, count, kinds, halves, parts, 1, rows, lanes))
         return found.reshape((count, kinds, halves, parts, rows, lanes))
 
-    last = modes - 1
     near_plane = jnp.where(odd == 0, slab - 1, 0)
-    (far_out,) = planes(saved_modes, slab - 1 - near_plane, [(0, modes)], [])
-    far_halo = swap(far_out, "space", far_pairs)
-    near_out, last_out = planes(saved_modes, near_plane, [(0, last), (last, 1)], [far_out])
+    half = modes // 2
+    groups = [(0, half), (half, modes - half)]
+    (near_out,) = planes(saved_modes, near_plane, [(0, modes)], [])
     near_halo = swap(near_out, "space", near_pairs)
+    far_outs = planes(saved_modes, slab - 1 - near_plane, groups, [near_out])
+    far_halos = [swap(block, "space", far_pairs) for block in far_outs]
 
     sides = jnp.stack([odd, lax.axis_index("freq")]).astype(jnp.int32)
-    sens, near_edges, far_edges = interior(saved_modes, weights, sides, [near_out])
-    base, near, far = band_sum(sides, finish_far(sides, weights, far_edges, far_halo, sens, freqs))
+    sens, _, near_edges, far_edges = interior(saved_modes, weights, sides, 0, modes, [], far_outs)
+    turns = finish_far(sides, weights, groups, far_edges, far_halos, sens, freqs)
+    base, near, far, keep = band_sum(sides, turns)
     near, far = swap(near, "space", near_pairs), swap(far, "space", far_pairs)
     where = jnp.stack([odd, place * slab, lax.axis_index("freq") * (rows // freqs)]).astype(jnp.int32)
     smoothed = smooth(where, base, near, far, slab * slabs, rows)
 
-    last_halo = swap(last_out, "space", near_pairs)
-    near_late, last_edges = near_part(weights, hbm(near_edges), hbm(near_halo), [base])
-    near_late = finish_near(last, weights, last_edges, last_halo, near_late, 2 * freqs, [])
+    near_late = finish_near(weights, *fetch([near_edges], [keep]), near_halo, 2 * freqs)
     return add_near(where, trade(near_late, near_pairs), smoothed, rows)
 
 

time: 89.5 us -> 87.2 us (0.974)
  starting transfers between devices: 35.3 us -> 29.9 us
  waiting for transfers between devices: 14.2 us -> 16.3 us
  Pallas kernels: 34.3 us -> 35.5 us
    ppermute x1, waiting for transfers between devices: 0.01 us -> 8.57 us  [band_sum(): found = lax.ppermute(send, 'freq', [(i, i ^ 2) for i in range(count)])]
    ppermute x5, waiting for transfers between devices: 10.3 us -> 4.4 us  [swap(): lax.ppermute(block, axis, [p for a, b in pairs for p in ((a, b), (b, a))])]
    ppermute x5, starting transfers between devices: 29 us -> 23.7 us  [swap(): lax.ppermute(block, axis, [p for a, b in pairs for p in ((a, b), (b, a))])]
    pallas_call x4, Pallas kernels: 26.4 us -> 25.3 us  [the longest x1 20 us: interior(): pl.pallas_call(functools.partial(interior_kernel, begin, len(before), len...]
    pallas_call x1, Pallas kernels: 0.59 us -> 1.65 us  [finish_base(): pl.pallas_call(base_kernel, in_specs=[pl.BlockSpec(memory_space=pltpu.SME...]
  transfers between devices with their start and end apart: 7 -> 7, of which waited for: 3 -> 3; matrix products, arithmetic and copies ran while one was open for 0% -> 0% of each run, Pallas kernels for 35% -> 38%
where the time goes in v3:
time: 87.2 us; the launch traced here: 86.6 us
  Pallas kernels  35.5 us (41%)
  starting transfers between devices  29.9 us (34%)
  waiting for transfers between devices  16.3 us (19%)
  blocking collectives  4.79 us (5%)
    ppermute x5, starting transfers between devices, swap(): lax.ppermute(block, axis, [p for a, b in pairs for p in ((a, b), (b, a))])  23.7 us
    pallas_call x1, Pallas kernels, interior(): pl.pallas_call(functools.partial(interior_kernel, begin, len(before), len...  20 us
    ppermute x1, waiting for transfers between devices, band_sum(): found = lax.ppermute(send, 'freq', [(i, i ^ 2) for i in range(count)])  8.57 us
    all_to_all x1, blocking collectives, band_sum(): lax.all_to_all(turns, 'freq', 0, 0, axis_index_groups=groups, tiled=True)  4.79 us
    all_to_all x1, starting transfers between devices, trade(): lax.all_to_all(pieces, ('freq', 'space'), 0, 0, axis_index_groups=groups,...  4.7 us
    ppermute x5, waiting for transfers between devices, swap(): lax.ppermute(block, axis, [p for a, b in pairs for p in ((a, b), (b, a))])  4.4 us
    pallas_call x2, Pallas kernels, planes(): pl.pallas_call(functools.partial(plane_kernel, [first for first, _ in gro...  3.97 us
    all_to_all x1, waiting for transfers between devices, trade(): lax.all_to_all(pieces, ('freq', 'space'), 0, 0, axis_index_groups=groups,...  3.31 us
  transfers between devices with their start and end apart: 7, of which 3 were waited for; matrix products, arithmetic and copies ran while one was open for 0% of the time, Pallas kernels for 38%

profile of v3, /device:TPU:0, one launch (start us, length us, event | category | flops | bytes accessed | tf_op | source)
XLA Modules:
  0.0 86.6 jit_solution(5248353270265847961)
XLA Ops:
  0.0 1.4 %shard_map.28.refs_0_ = bf16[4,2,2,3,128,128]{5,4,3,2,1,0:T(8,128)(2,1)S(1)} custom-call(s32[1]{0:T(128)} %bitcast.5.plane_ref, bf16[1,4,2,2,3,16,128,128]{7,6,5,4,3,2,1,0:T(8,128)(2,1)} %modes_ref.5), custom_call_target="tpu_custom_call" | custom-call | flops 1024 | bytes 1024 | tf_op jit(solution)/shard_map/pallas_call | solution.py:35
  1.4 3.0 %collective-permute-start.2 = (bf16[4,2,2,3,128,128]{5,4,3,2,1,0:T(8,128)(2,1)S(1)}, bf16[4,2,2,3,128,128]{5,4,3,2,1,0:T(8,128)(2,1)S(1)}, u32[]{:S(2)}, u32[]{:S(2)}) collective-permute-start(bf16[4,2,2,3,128,128]{5,4,3,2,1,0:T(8,128)(2,1)S(1)} %shard_map.28.refs_0_), channel_id=1, source_target_pairs={{0,1},{1,0},{2,3},{3,2},{4,5},{5,4},{6,7},{7,6},{8,9},{9,8},{10,11... | collective-permute-start | bytes 4718600 | tf_op jit(solution)/shard_map/ppermute | solution.py:413
  4.5 0.0 copy-start.2
  4.5 2.6 %shard_map.29 = (bf16[2,2,2,3,128,128]{5,4,3,2,1,0:T(8,128)(2,1)}, bf16[2,2,2,3,128,128]{5,4,3,2,1,0:T(8,128)(2,1)}) custom-call(s32[1]{0:T(128)} %bitcast.4.plane_ref, bf16[1,4,2,2,3,16,128,128]{7,6,5,4,3,2,1,0:T(8,128)(2,1)} %modes_ref.5, bf16[4,2,2,3,128,128]{5,4,3,2,1,0:T(8,128)(2,1)S(1)} %shard_map.28.refs_0_), custom_call_target="tpu_custom_call" | custom-call | flops 1024 | bytes 1024 | tf_op jit(solution)/shard_map/pallas_call | solution.py:35
  7.0 1.6 %collective-permute-start = (bf16[2,2,2,3,128,128]{5,4,3,2,1,0:T(8,128)(2,1)}, bf16[2,2,2,3,128,128]{5,4,3,2,1,0:T(8,128)(2,1)}, u32[]{:S(2)}, u32[]{:S(2)}) collective-permute-start(bf16[2,2,2,3,128,128]{5,4,3,2,1,0:T(8,128)(2,1)} %get-tuple-element.15.refs_0_), channel_id=1, source_target_pairs={{1,2},{2,1},{3,4},{4,3},{5,6},{6,5},{9,10},{10,9},{11,12},{12,11},... | collective-permute-start | bytes 2359304 | tf_op jit(solution)/shard_map/ppermute | solution.py:413
  8.6 1.6 %collective-permute-start.1 = (bf16[2,2,2,3,128,128]{5,4,3,2,1,0:T(8,128)(2,1)}, bf16[2,2,2,3,128,128]{5,4,3,2,1,0:T(8,128)(2,1)}, u32[]{:S(2)}, u32[]{:S(2)}) collective-permute-start(bf16[2,2,2,3,128,128]{5,4,3,2,1,0:T(8,128)(2,1)} %get-tuple-element.16.refs_1_), channel_id=1, source_target_pairs={{1,2},{2,1},{3,4},{4,3},{5,6},{6,5},{9,10},{10,9},{11,12},{12,11},... | collective-permute-start | bytes 2359304 | tf_op jit(solution)/shard_map/ppermute | solution.py:413
  10.1 0.0 copy-done.2
  10.2 0.1 pad_add_fusion.1.side_ref
  10.2 20.0 %shard_map.30 = (f32[16,144,128]{2,1,0:T(8,128)S(1)}, f32[8,128]{1,0:T(8,128)}, f32[4,2,2,3,128,128]{5,4,3,2,1,0:T(8,128)}, f32[4,2,2,3,128,128]{5,4,3,2,1,0:T(8,128)S(1)}) custom-call(s32[2]{0:T(128)S(1)} %pad_add_fusion.1.side_ref, f32[1,4]{1,0:T(1,128)S(1)} %broadcast_multiply_fusion.weight_ref, bf16[1,4,2,2,3,16,128,128]{7,6,5,4,3,2,1,0:T(8,128)(2,1)} %modes_ref.5, ...), custom_call_target="tpu_custom_call" | custom-call | flops 8000000000 | bytes 1024 | tf_op jit(solution)/shard_map/pallas_call | solution.py:150
  30.2 0.0 collective-permute-done.refs_0_
  30.2 0.0 collective-permute-done.1.refs_1_
  30.2 1.8 %shard_map.31 = f32[4,16,40,128]{3,2,1,0:T(8,128)S(1)} custom-call(s32[2]{0:T(128)S(1)} %pad_add_fusion.1.side_ref, f32[1,4]{1,0:T(1,128)S(1)} %broadcast_multiply_fusion.weight_ref, f32[4,2,2,3,128,128]{5,4,3,2,1,0:T(8,128)S(1)} %get-tuple-element.18.edge_ref, bf16[2,2,2,3,128,128]{5,4,3,2,1,0:T(8,128)(2,1)} %collective-permute-done.refs_0_, ...), custom_call_target="tpu_custom_call" | custom-call | flops 1024 | bytes 1024 | tf_op jit(solution)/shard_map/pallas_call | solution.py:241
  32.0 4.8 %all_to_all.10.found_ref = f32[4,16,40,128]{3,2,1,0:T(8,128)S(1)} all-to-all(f32[4,16,40,128]{3,2,1,0:T(8,128)S(1)} %shard_map.31), channel_id=1, replica_groups={{0,8},{16,24},{1,9},{17,25},{2,10},{18,26},{3,11},{19,27},{4,12},{20,28..., dimensions={0} | all-to-all | bytes 2621440 | tf_op jit(solution)/shard_map/all_to_all | solution.py:473
  36.8 1.3 %shard_map.32 = (f32[1,16,40,128]{3,2,1,0:T(8,128)}, f32[1,16,40,128]{3,2,1,0:T(8,128)S(1)}) custom-call(s32[2]{0:T(128)S(1)} %pad_add_fusion.1.side_ref, f32[4,16,40,128]{3,2,1,0:T(8,128)S(1)} %all_to_all.10.found_ref), custom_call_target="tpu_custom_call" | custom-call | flops 1024 | bytes 1024 | tf_op jit(solution)/shard_map/pallas_call | solution.py:437
  38.2 1.5 %collective-permute-start.3 = (f32[1,16,40,128]{3,2,1,0:T(8,128)}, f32[1,16,40,128]{3,2,1,0:T(8,128)}, u32[]{:S(2)}, u32[]{:S(2)}) collective-permute-start(f32[1,16,40,128]{3,2,1,0:T(8,128)} %get-tuple-element.21), channel_id=1, source_target_pairs={{0,16},{8,24},{16,0},{24,8},{1,17},{9,25},{17,1},{25,9},{2,18},{10... | collective-permute-start | bytes 983048 | tf_op jit(solution)/shard_map/ppermute | solution.py:474
  39.7 8.6 %collective-permute-done.3.found_ref = f32[1,16,40,128]{3,2,1,0:T(8,128)} collective-permute-done((f32[1,16,40,128]{3,2,1,0:T(8,128)}, f32[1,16,40,128]{3,2,1,0:T(8,128)}, u32[]{:S(2)}, u32[]{:S(2)}) %collective-permute-start.3) | collective-permute-done | bytes 327712 | tf_op jit(solution)/shard_map/ppermute | solution.py:474
  48.2 1.6 %shard_map.35 = (f32[16,40,128]{2,1,0:T(8,128)S(1)}, f32[3,40,128]{2,1,0:T(8,128)}, f32[3,40,128]{2,1,0:T(8,128)S(1)}) custom-call(s32[2]{0:T(128)S(1)} %pad_add_fusion.1.side_ref, f32[1,16,40,128]{3,2,1,0:T(8,128)S(1)} %get-tuple-element.20.refs_1_.keep_ref, f32[1,16,40,128]{3,2,1,0:T(8,128)} %collective-permute-done.3.found_ref), custom_call_target="tpu_custom_call" | custom-call | flops 1024 | bytes 1024 | tf_op jit(solution)/shard_map/pallas_call | solution.py:458
  49.9 0.0 copy-start
  49.9 16.2 %collective-permute-start.4 = (f32[3,40,128]{2,1,0:T(8,128)}, f32[3,40,128]{2,1,0:T(8,128)}, u32[]{:S(2)}, u32[]{:S(2)}) collective-permute-start(f32[3,40,128]{2,1,0:T(8,128)} %get-tuple-element.23), channel_id=1, source_target_pairs={{0,1},{1,0},{2,3},{3,2},{4,5},{5,4},{6,7},{7,6},{8,9},{9,8},{10,11... | collective-permute-start | bytes 184328 | tf_op jit(solution)/shard_map/ppermute | solution.py:413
  66.1 1.3 %collective-permute-start.5 = (f32[3,40,128]{2,1,0:T(8,128)S(1)}, f32[3,40,128]{2,1,0:T(8,128)}, u32[]{:S(2)}, u32[]{:S(2)}) collective-permute-start(f32[3,40,128]{2,1,0:T(8,128)S(1)} %get-tuple-element.24), channel_id=1, source_target_pairs={{1,2},{2,1},{3,4},{4,3},{5,6},{6,5},{9,10},{10,9},{11,12},{12,11},... | collective-permute-start | bytes 184328 | tf_op jit(solution)/shard_map/ppermute | solution.py:413
  67.4 0.1 pad_add_fusion.place_ref
  67.5 1.9 %shard_map.33.edge_ref = f32[4,2,2,3,128,128]{5,4,3,2,1,0:T(8,128)S(1)} custom-call(f32[4,2,2,3,128,128]{5,4,3,2,1,0:T(8,128)} %get-tuple-element.17.refs_0_, f32[1,16,40,128]{3,2,1,0:T(8,128)S(1)} %get-tuple-element.20.refs_1_.keep_ref), custom_call_target="tpu_custom_call" | custom-call | flops 1024 | bytes 1024 | tf_op jit(solution)/shard_map/pallas_call | solution.py:263
  69.4 0.0 copy-done
  69.4 4.4 %collective-permute-done.2.halo_ref = bf16[4,2,2,3,128,128]{5,4,3,2,1,0:T(8,128)(2,1)S(1)} collective-permute-done((bf16[4,2,2,3,128,128]{5,4,3,2,1,0:T(8,128)(2,1)S(1)}, bf16[4,2,2,3,128,128]{5,4,3,2,1,0:T(8,128)(2,1)S(1)}, u32[]{:S(2)}, u32[]{:S(2)}) %collective-permute-start.2) | collective-permute-done | bytes 1572896 | tf_op jit(solution)/shard_map/ppermute | solution.py:413
  73.8 0.0 copy-start.1
  73.8 1.6 %shard_map.34 = f32[8,40,128]{2,1,0:T(8,128)} custom-call(f32[1,4]{1,0:T(1,128)S(1)} %broadcast_multiply_fusion.weight_ref, f32[4,2,2,3,128,128]{5,4,3,2,1,0:T(8,128)S(1)} %shard_map.33.edge_ref, bf16[4,2,2,3,128,128]{5,4,3,2,1,0:T(8,128)(2,1)S(1)} %collective-permute-done.2.halo_ref), custom_call_target="tpu_custom_call" | custom-call | flops 1024 | bytes 1024 | tf_op jit(solution)/shard_map/pallas_call | solution.py:296
  75.4 4.7 %all-to-all-start.1 = ((f32[8,40,128]{2,1,0:T(8,128)}), f32[8,40,128]{2,1,0:T(8,128)S(1)}, u32[]{:S(2)}, u32[]{:S(2)}) async-start(f32[8,40,128]{2,1,0:T(8,128)} %shard_map.34), calls=%async_computation.1 | async-start | bytes 327680 | tf_op jit(solution)/shard_map/all_to_all | solution.py:419
  80.1 0.0 collective-permute-done.4.near_ref
  80.1 0.0 collective-permute-done.5.far_ref
  80.1 0.0 copy-done.1
  80.1 1.7 %shard_map.36.before_ref = f32[16,32,128]{2,1,0:T(8,128)S(1)} custom-call(s32[3]{0:T(128)S(1)} %pad_add_fusion.place_ref, f32[16,40,128]{2,1,0:T(8,128)S(1)} %copy-done.1, f32[3,40,128]{2,1,0:T(8,128)} %collective-permute-done.4.near_ref, f32[3,40,128]{2,1,0:T(8,128)} %collective-permute-done.5.far_ref), custom_call_target="tpu_custom_call" | custom-call | flops 10000000000 | bytes 1024 | tf_op jit(solution)/shard_map/pallas_call | solution.py:366
  81.8 3.3 %all-to-all-done.1.late_vmem = f32[8,40,128]{2,1,0:T(8,128)S(1)} async-done(((f32[8,40,128]{2,1,0:T(8,128)}), f32[8,40,128]{2,1,0:T(8,128)S(1)}, u32[]{:S(2)}, u32[]{:S(2)}) %all-to-all-start.1) | async-done | bytes 163872 | tf_op jit(solution)/shard_map/all_to_all | solution.py:419
  85.1 1.5 %shard_map.37 = f32[16,32,128]{2,1,0:T(8,128)} custom-call(s32[3]{0:T(128)S(1)} %pad_add_fusion.place_ref, f32[8,40,128]{2,1,0:T(8,128)S(1)} %all-to-all-done.1.late_vmem, f32[16,32,128]{2,1,0:T(8,128)S(1)} %shard_map.36.before_ref), custom_call_target="tpu_custom_call" | custom-call | flops 1024 | bytes 1024 | tf_op jit(solution)/shard_map/pallas_call | solution.py:402
  (1 shorter events, 0.0 us)
Async XLA Ops:
  1.4 72.4 %collective-permute-start.2 = (bf16[4,2,2,3,128,128]{5,4,3,2,1,0:T(8,128)(2,1)S(1)}, bf16[4,2,2,3,128,128]{5,4,3,2,1,0:T(8,128)(2,1)S(1)}, u32[]{:S(2)}, u32[]{:S(2)}) collective-permute-start(bf16[4,2,2,3,128,128]{5,4,3,2,1,0:T(8,128)(2,1)S(1)} %shard_map.28.refs_0_), channel_id=1, source_target_pairs={{0,1},{1,0},{2,3},{3,2},{4,5},{5,4},{6,7},{7,6},{8,9},{9,8},{10,11... | collective-permute-start | bytes 4718600 | tf_op jit(solution)/shard_map/ppermute | solution.py:413
  4.5 5.7 %copy-start.2 = (f32[1,4]{1,0:T(1,128)S(1)}, f32[1,4]{1,0:T(1,128)}, u32[]{:S(2)}) copy-start(f32[1,4]{1,0:T(1,128)} %param.3) | copy-start | bytes 52
  7.0 23.2 %collective-permute-start = (bf16[2,2,2,3,128,128]{5,4,3,2,1,0:T(8,128)(2,1)}, bf16[2,2,2,3,128,128]{5,4,3,2,1,0:T(8,128)(2,1)}, u32[]{:S(2)}, u32[]{:S(2)}) collective-permute-start(bf16[2,2,2,3,128,128]{5,4,3,2,1,0:T(8,128)(2,1)} %get-tuple-element.15.refs_0_), channel_id=1, source_target_pairs={{1,2},{2,1},{3,4},{4,3},{5,6},{6,5},{9,10},{10,9},{11,12},{12,11},... | collective-permute-start | bytes 2359304 | tf_op jit(solution)/shard_map/ppermute | solution.py:413
  8.6 21.6 %collective-permute-start.1 = (bf16[2,2,2,3,128,128]{5,4,3,2,1,0:T(8,128)(2,1)}, bf16[2,2,2,3,128,128]{5,4,3,2,1,0:T(8,128)(2,1)}, u32[]{:S(2)}, u32[]{:S(2)}) collective-permute-start(bf16[2,2,2,3,128,128]{5,4,3,2,1,0:T(8,128)(2,1)} %get-tuple-element.16.refs_1_), channel_id=1, source_target_pairs={{1,2},{2,1},{3,4},{4,3},{5,6},{6,5},{9,10},{10,9},{11,12},{12,11},... | collective-permute-start | bytes 2359304 | tf_op jit(solution)/shard_map/ppermute | solution.py:413
  38.2 10.1 %collective-permute-start.3 = (f32[1,16,40,128]{3,2,1,0:T(8,128)}, f32[1,16,40,128]{3,2,1,0:T(8,128)}, u32[]{:S(2)}, u32[]{:S(2)}) collective-permute-start(f32[1,16,40,128]{3,2,1,0:T(8,128)} %get-tuple-element.21), channel_id=1, source_target_pairs={{0,16},{8,24},{16,0},{24,8},{1,17},{9,25},{17,1},{25,9},{2,18},{10... | collective-permute-start | bytes 983048 | tf_op jit(solution)/shard_map/ppermute | solution.py:474
  49.9 19.5 %copy-start = (f32[16,40,128]{2,1,0:T(8,128)}, f32[16,40,128]{2,1,0:T(8,128)S(1)}, u32[]{:S(2)}) copy-start(f32[16,40,128]{2,1,0:T(8,128)S(1)} %get-tuple-element.22.base_ref) | copy-start | bytes 983044
  49.9 30.2 %collective-permute-start.4 = (f32[3,40,128]{2,1,0:T(8,128)}, f32[3,40,128]{2,1,0:T(8,128)}, u32[]{:S(2)}, u32[]{:S(2)}) collective-permute-start(f32[3,40,128]{2,1,0:T(8,128)} %get-tuple-element.23), channel_id=1, source_target_pairs={{0,1},{1,0},{2,3},{3,2},{4,5},{5,4},{6,7},{7,6},{8,9},{9,8},{10,11... | collective-permute-start | bytes 184328 | tf_op jit(solution)/shard_map/ppermute | solution.py:413
  66.1 13.9 %collective-permute-start.5 = (f32[3,40,128]{2,1,0:T(8,128)S(1)}, f32[3,40,128]{2,1,0:T(8,128)}, u32[]{:S(2)}, u32[]{:S(2)}) collective-permute-start(f32[3,40,128]{2,1,0:T(8,128)S(1)} %get-tuple-element.24), channel_id=1, source_target_pairs={{1,2},{2,1},{3,4},{4,3},{5,6},{6,5},{9,10},{10,9},{11,12},{12,11},... | collective-permute-start | bytes 184328 | tf_op jit(solution)/shard_map/ppermute | solution.py:413
  73.8 6.3 %copy-start.1 = (f32[16,40,128]{2,1,0:T(8,128)S(1)}, f32[16,40,128]{2,1,0:T(8,128)}, u32[]{:S(2)}) copy-start(f32[16,40,128]{2,1,0:T(8,128)} %copy-done) | copy-start | bytes 983044
  75.4 9.7 %all-to-all-start.1 = ((f32[8,40,128]{2,1,0:T(8,128)}), f32[8,40,128]{2,1,0:T(8,128)S(1)}, u32[]{:S(2)}, u32[]{:S(2)}) async-start(f32[8,40,128]{2,1,0:T(8,128)} %shard_map.34), calls=%async_computation.1 | async-start | bytes 327680 | tf_op jit(solution)/shard_map/all_to_all | solution.py:419

commit v4 on v3

--- a/solution.py
+++ b/solution.py
@@ -271,42 +271,52 @@
     )(*[hbm(block) for block in blocks], *after)
 
 
-def near_kernel(weight_ref, edge_ref, halo_ref, out_ref, tall_ref, band_ref, done):
+def near_kernel(side_ref, weight_ref, edge_ref, halo_ref, keep_ref, give_ref, tall_ref):
     modes, halves, _, parts, rows, _ = edge_ref.shape
     scales = [weight_ref[0, mode] for mode in range(modes)]
     strains = [strain_of(edge_ref, mode) for mode in range(modes)]
     halos = [halo_of(halo_ref, mode) for mode in range(modes)]
-    pieces, tall, lanes = band_ref.shape
+    _, tall, lanes = keep_ref.shape
     band = tall - 2 * EDGE
-    empty = jnp.zeros((MARGIN, lanes), jnp.float32)
-    tall_ref[pl.ds(0, MARGIN)] = empty
-    tall_ref[pl.ds(MARGIN + rows, MARGIN)] = empty
+    empty = jnp.zeros((2 * EDGE, lanes), jnp.float32)
+    tall_ref[pl.ds(0, 2 * EDGE)] = empty
+    tall_ref[pl.ds(rows, 2 * EDGE)] = empty
     for start in range(0, rows, STEP):
-        tall_ref[pl.ds(MARGIN + start, STEP)] = outer_plane(start, (halves, parts), scales, strains, halos)
-    for piece in range(pieces):
-        band_ref[piece] = tall_ref[pl.ds(piece // 2 * band + MARGIN - EDGE, tall)]
-    copy = pltpu.make_async_copy(band_ref, out_ref, done)
-    copy.start()
-    copy.wait()
-
-
-def finish_near(weights, edges, halo, pieces):
-    rows, lanes = halo.shape[4:]
-    shape = (pieces, rows // (pieces // 2) + 2 * EDGE, lanes)
+        tall_ref[pl.ds(EDGE + start, STEP)] = outer_plane(start, (halves, parts), scales, strains, halos)
+    for turn, ref in enumerate((keep_ref, give_ref, keep_ref, give_ref)):
+        start = pl.multiple_of((side_ref[1] ^ turn) * band, 8)
+        ref[turn // 2] = tall_ref[pl.ds(start, tall)]
+
+
+def finish_near(sides, weights, edges, halo, freqs):
+    rows, lanes = edges.shape[4:]
+    bands = jax.ShapeDtypeStruct((2, rows // freqs + 2 * EDGE, lanes), jnp.float32)
     return pl.pallas_call(
         near_kernel,
-        in_specs=[pl.BlockSpec(memory_space=pltpu.SMEM)]
-        + [pl.BlockSpec(memory_space=pltpu.VMEM)] * 2,
-        out_specs=pl.BlockSpec(memory_space=pltpu.HBM),
-        out_shape=pltpu.HBM(shape, jnp.float32),
-        scratch_shapes=[
-            pltpu.VMEM((rows + 2 * MARGIN, lanes), jnp.float32),
-            pltpu.VMEM(shape, jnp.float32),
-            pltpu.SemaphoreType.DMA(()),
-        ],
-        compiler_params=pltpu.CompilerParams(vmem_limit_bytes=SMALL_VMEM),
-        cost_estimate=QUICK,
-    )(weights, edges, halo)
+        in_specs=[pl.BlockSpec(memory_space=pltpu.SMEM)] * 2 + [pl.BlockSpec(memory_space=pltpu.VMEM)] * 2,
+        out_specs=[pl.BlockSpec(memory_space=pltpu.VMEM)] * 2,
+        out_shape=[bands] * 2,
+        scratch_shapes=[pltpu.VMEM((rows + 2 * EDGE, lanes), jnp.float32)],
+        compiler_params=pltpu.CompilerParams(vmem_limit_bytes=SMALL_VMEM),
+        cost_estimate=QUICK,
+    )(sides, weights, edges, halo)
+
+
+def pair_kernel(keep_ref, found_ref, own_ref, other_ref):
+    own_ref[...] = keep_ref[0] + found_ref[0]
+    other_ref[...] = keep_ref[1] + found_ref[1]
+
+
+def pair_sum(keep, found):
+    band = jax.ShapeDtypeStruct(keep.shape[1:], jnp.float32)
+    return pl.pallas_call(
+        pair_kernel,
+        in_specs=[pl.BlockSpec(memory_space=pltpu.VMEM)] * 2,
+        out_specs=[pl.BlockSpec(memory_space=pltpu.VMEM)] * 2,
+        out_shape=[band] * 2,
+        compiler_params=pltpu.CompilerParams(vmem_limit_bytes=SMALL_VMEM),
+        cost_estimate=QUICK,
+    )(keep, found)
 
 
 class Pass:
@@ -375,18 +385,16 @@
     )(place, base, near, far)
 
 
-def add_near_kernel(total_y, place_ref, late_vmem, before_ref, out_ref):
-    pieces, tall, lanes = late_vmem.shape
-    slab, band = before_ref.shape[:2]
+def add_near_kernel(total_y, place_ref, own_refs, beyond_refs, before_ref, out_ref):
+    tall, lanes = own_refs[0].shape
+    slab = before_ref.shape[0]
     even = place_ref[0] == 0
     first = jnp.where(even, slab - 4, 0)
     out_ref[...] = before_ref[...]
     smoothed = Pass(tall, lanes, place_ref[2], total_y)
-    lower, upper = (
-        functools.reduce(jnp.add, [late_vmem[i] for i in range(which, pieces, 2)]) for which in range(2)
-    )
-    zero = jnp.zeros_like(lower)
-    planes = {-1: jnp.where(even, upper, lower), 0: jnp.where(even, lower, upper)}
+    own, beyond = (refs[0][...] + refs[1][...] for refs in (own_refs, beyond_refs))
+    zero = jnp.zeros_like(own)
+    planes = {-1: beyond, 0: own}
     for reach in (1, 2, 3):
         low, high = max(-1 - reach, reach - 4), min(reach, 3)
         planes = {
@@ -397,26 +405,37 @@
         out_ref[first + jnp.where(even, 3 - at, at)] += planes[at][EDGE : tall - EDGE]
 
 
-def add_near(place, late, before, total_y):
+def add_near(place, own, beyond, before, total_y):
     slab, band, lanes = before.shape
     return pl.pallas_call(
         functools.partial(add_near_kernel, total_y),
-        in_specs=[pl.BlockSpec(memory_space=pltpu.SMEM)] + [pl.BlockSpec(memory_space=pltpu.VMEM)] * 2,
+        in_specs=[pl.BlockSpec(memory_space=pltpu.SMEM)]
+        + [[pl.BlockSpec(memory_space=pltpu.VMEM)] * 2] * 2
+        + [pl.BlockSpec(memory_space=pltpu.VMEM)],
         out_specs=pl.BlockSpec(memory_space=pltpu.VMEM),
         out_shape=jax.ShapeDtypeStruct(before.shape, jnp.float32),
         compiler_params=pltpu.CompilerParams(vmem_limit_bytes=SMALL_VMEM),
         cost_estimate=QUICK,
-    )(place, late, before)
+    )(place, own, beyond, before)
 
 
 def swap(block, axis, pairs):
     return lax.ppermute(block, axis, [p for a, b in pairs for p in ((a, b), (b, a))])
 
 
-def trade(pieces, pairs):
-    slabs = lax.axis_size("space")
-    groups = [[f * slabs + s for f in range(lax.axis_size("freq")) for s in pair] for pair in pairs]
-    return lax.all_to_all(pieces, ("freq", "space"), 0, 0, axis_index_groups=groups, tiled=True)
+def both(freq_pairs, space_pairs, slabs):
+    return [(f * slabs + s, g * slabs + r) for f, g in freq_pairs for s, r in space_pairs]
+
+
+def near_sums(keep, give, near_pairs):
+    freqs, slabs = lax.axis_size("freq"), lax.axis_size("space")
+    own, other = pair_sum(keep, lax.ppermute(give, "freq", [(i, i ^ 1) for i in range(freqs)]))
+    across = [(i, i ^ 2) for i in range(freqs)]
+    swaps = [p for a, b in near_pairs for p in ((a, b), (b, a))]
+    from_own = lax.ppermute(other, "freq", across)
+    beyond = lax.ppermute(own, "space", swaps)
+    from_beyond = lax.ppermute(other, ("freq", "space"), both(across, swaps, slabs))
+    return [own, from_own], [beyond, from_beyond]
 
 
 def hbm(block):
@@ -507,8 +526,8 @@
     where = jnp.stack([odd, place * slab, lax.axis_index("freq") * (rows // freqs)]).astype(jnp.int32)
     smoothed = smooth(where, base, near, far, slab * slabs, rows)
 
-    near_late = finish_near(weights, *fetch([near_edges], [keep]), near_halo, 2 * freqs)
-    return add_near(where, trade(near_late, near_pairs), smoothed, rows)
+    keep, give = finish_near(sides, weights, *fetch([near_edges], [keep]), near_halo, freqs)
+    return add_near(where, *near_sums(keep, give, near_pairs), smoothed, rows)
 
 
 def solution(mesh):

time: 87.2 us -> 85.6 us (0.982)
  starting transfers between devices: 29.9 us -> 28.1 us
  waiting for transfers between devices: 16.3 us -> 17.6 us
  Pallas kernels: 35.5 us -> 34.6 us
    all_to_all x1 -> x0, starting transfers between devices: 4.7 us -> none  [trade(): lax.all_to_all(pieces, ('freq', 'space'), 0, 0, axis_index_groups=groups,...]
    ppermute x0 -> x4, starting transfers between devices: none -> 4.05 us  [the longest x1 2.45 us: near_sums(): lax.ppermute(other, ('freq', 'space'), both(across, swaps, slabs))]
    ppermute x0 -> x4, waiting for transfers between devices: none -> 3.48 us  [the longest x1 2.35 us: near_sums(): beyond = lax.ppermute(own, 'space', swaps)]
    all_to_all x1 -> x0, waiting for transfers between devices: 3.31 us -> none  [trade(): lax.all_to_all(pieces, ('freq', 'space'), 0, 0, axis_index_groups=groups,...]
    ppermute x5, waiting for transfers between devices: 4.4 us -> 7.45 us  [swap(): lax.ppermute(block, axis, [p for a, b in pairs for p in ((a, b), (b, a))])]
    ppermute x1, waiting for transfers between devices: 8.57 us -> 6.67 us  [band_sum(): found = lax.ppermute(send, 'freq', [(i, i ^ 2) for i in range(count)])]
    ppermute x5, starting transfers between devices: 23.7 us -> 22.6 us  [swap(): lax.ppermute(block, axis, [p for a, b in pairs for p in ((a, b), (b, a))])]
  transfers between devices with their start and end apart: 7 -> 10, of which waited for: 3 -> 4; matrix products, arithmetic and copies ran while one was open for 0% -> 0% of each run, Pallas kernels for 38% -> 37%
where the time goes in v4:
time: 85.6 us; the launch traced here: 85.3 us
  Pallas kernels  34.6 us (40%)
  starting transfers between devices  28.1 us (33%)
  waiting for transfers between devices  17.6 us (21%)
  blocking collectives  4.79 us (6%)
    ppermute x5, starting transfers between devices, swap(): lax.ppermute(block, axis, [p for a, b in pairs for p in ((a, b), (b, a))])  22.6 us
    pallas_call x1, Pallas kernels, interior(): pl.pallas_call(functools.partial(interior_kernel, begin, len(before), len...  20.6 us
    ppermute x5, waiting for transfers between devices, swap(): lax.ppermute(block, axis, [p for a, b in pairs for p in ((a, b), (b, a))])  7.45 us
    ppermute x1, waiting for transfers between devices, band_sum(): found = lax.ppermute(send, 'freq', [(i, i ^ 2) for i in range(count)])  6.67 us
    all_to_all x1, blocking collectives, band_sum(): lax.all_to_all(turns, 'freq', 0, 0, axis_index_groups=groups, tiled=True)  4.79 us
    pallas_call x2, Pallas kernels, planes(): pl.pallas_call(functools.partial(plane_kernel, [first for first, _ in gro...  3.97 us
    ppermute x1, starting transfers between devices, near_sums(): lax.ppermute(other, ('freq', 'space'), both(across, swaps, slabs))  2.45 us
    ppermute x1, waiting for transfers between devices, near_sums(): beyond = lax.ppermute(own, 'space', swaps)  2.35 us
  transfers between devices with their start and end apart: 10, of which 4 were waited for; matrix products, arithmetic and copies ran while one was open for 0% of the time, Pallas kernels for 37%

profile of v4, /device:TPU:0, one launch (start us, length us, event | category | flops | bytes accessed | tf_op | source)
XLA Modules:
  0.0 85.3 jit_solution(15524517083442459789)
XLA Ops:
  0.0 1.4 %shard_map.28.refs_0_ = bf16[4,2,2,3,128,128]{5,4,3,2,1,0:T(8,128)(2,1)S(1)} custom-call(s32[1]{0:T(128)} %bitcast.5.plane_ref, bf16[1,4,2,2,3,16,128,128]{7,6,5,4,3,2,1,0:T(8,128)(2,1)} %modes_ref.5), custom_call_target="tpu_custom_call" | custom-call | flops 1024 | bytes 1024 | tf_op jit(solution)/shard_map/pallas_call | solution.py:35
  1.4 3.0 %collective-permute-start.2 = (bf16[4,2,2,3,128,128]{5,4,3,2,1,0:T(8,128)(2,1)S(1)}, bf16[4,2,2,3,128,128]{5,4,3,2,1,0:T(8,128)(2,1)S(1)}, u32[]{:S(2)}, u32[]{:S(2)}) collective-permute-start(bf16[4,2,2,3,128,128]{5,4,3,2,1,0:T(8,128)(2,1)S(1)} %shard_map.28.refs_0_), channel_id=1, source_target_pairs={{0,1},{1,0},{2,3},{3,2},{4,5},{5,4},{6,7},{7,6},{8,9},{9,8},{10,11... | collective-permute-start | bytes 4718600 | tf_op jit(solution)/shard_map/ppermute | solution.py:423
  4.5 0.0 copy-start
  4.5 2.6 %shard_map.29 = (bf16[2,2,2,3,128,128]{5,4,3,2,1,0:T(8,128)(2,1)}, bf16[2,2,2,3,128,128]{5,4,3,2,1,0:T(8,128)(2,1)}) custom-call(s32[1]{0:T(128)} %bitcast.4.plane_ref, bf16[1,4,2,2,3,16,128,128]{7,6,5,4,3,2,1,0:T(8,128)(2,1)} %modes_ref.5, bf16[4,2,2,3,128,128]{5,4,3,2,1,0:T(8,128)(2,1)S(1)} %shard_map.28.refs_0_), custom_call_target="tpu_custom_call" | custom-call | flops 1024 | bytes 1024 | tf_op jit(solution)/shard_map/pallas_call | solution.py:35
  7.0 1.6 %collective-permute-start = (bf16[2,2,2,3,128,128]{5,4,3,2,1,0:T(8,128)(2,1)}, bf16[2,2,2,3,128,128]{5,4,3,2,1,0:T(8,128)(2,1)}, u32[]{:S(2)}, u32[]{:S(2)}) collective-permute-start(bf16[2,2,2,3,128,128]{5,4,3,2,1,0:T(8,128)(2,1)} %get-tuple-element.19.refs_0_), channel_id=1, source_target_pairs={{1,2},{2,1},{3,4},{4,3},{5,6},{6,5},{9,10},{10,9},{11,12},{12,11},... | collective-permute-start | bytes 2359304 | tf_op jit(solution)/shard_map/ppermute | solution.py:423
  8.6 1.6 %collective-permute-start.1 = (bf16[2,2,2,3,128,128]{5,4,3,2,1,0:T(8,128)(2,1)}, bf16[2,2,2,3,128,128]{5,4,3,2,1,0:T(8,128)(2,1)}, u32[]{:S(2)}, u32[]{:S(2)}) collective-permute-start(bf16[2,2,2,3,128,128]{5,4,3,2,1,0:T(8,128)(2,1)} %get-tuple-element.20.refs_1_), channel_id=1, source_target_pairs={{1,2},{2,1},{3,4},{4,3},{5,6},{6,5},{9,10},{10,9},{11,12},{12,11},... | collective-permute-start | bytes 2359304 | tf_op jit(solution)/shard_map/ppermute | solution.py:423
  10.2 0.0 copy-done
  10.2 0.1 pad_add_fusion.1.side_ref
  10.2 20.6 %shard_map.30 = (f32[16,144,128]{2,1,0:T(8,128)S(1)}, f32[8,128]{1,0:T(8,128)}, f32[4,2,2,3,128,128]{5,4,3,2,1,0:T(8,128)}, f32[4,2,2,3,128,128]{5,4,3,2,1,0:T(8,128)S(1)}) custom-call(s32[2]{0:T(128)S(1)} %pad_add_fusion.1.side_ref, f32[1,4]{1,0:T(1,128)S(1)} %broadcast_multiply_fusion.weight_ref, bf16[1,4,2,2,3,16,128,128]{7,6,5,4,3,2,1,0:T(8,128)(2,1)} %modes_ref.5, ...), custom_call_target="tpu_custom_call" | custom-call | flops 8000000000 | bytes 1024 | tf_op jit(solution)/shard_map/pallas_call | solution.py:150
  30.8 0.0 collective-permute-done.refs_0_
  30.8 0.0 collective-permute-done.1.refs_1_
  30.8 1.9 %shard_map.31 = f32[4,16,40,128]{3,2,1,0:T(8,128)S(1)} custom-call(s32[2]{0:T(128)S(1)} %pad_add_fusion.1.side_ref, f32[1,4]{1,0:T(1,128)S(1)} %broadcast_multiply_fusion.weight_ref, f32[4,2,2,3,128,128]{5,4,3,2,1,0:T(8,128)S(1)} %get-tuple-element.22.edge_ref, bf16[2,2,2,3,128,128]{5,4,3,2,1,0:T(8,128)(2,1)} %collective-permute-done.refs_0_, ...), custom_call_target="tpu_custom_call" | custom-call | flops 1024 | bytes 1024 | tf_op jit(solution)/shard_map/pallas_call | solution.py:241
  32.7 4.8 %all_to_all.5.found_ref = f32[4,16,40,128]{3,2,1,0:T(8,128)S(1)} all-to-all(f32[4,16,40,128]{3,2,1,0:T(8,128)S(1)} %shard_map.31), channel_id=1, replica_groups={{0,8},{16,24},{1,9},{17,25},{2,10},{18,26},{3,11},{19,27},{4,12},{20,28..., dimensions={0} | all-to-all | bytes 2621440 | tf_op jit(solution)/shard_map/all_to_all | solution.py:492
  37.5 1.3 %shard_map.32 = (f32[1,16,40,128]{3,2,1,0:T(8,128)}, f32[1,16,40,128]{3,2,1,0:T(8,128)S(1)}) custom-call(s32[2]{0:T(128)S(1)} %pad_add_fusion.1.side_ref, f32[4,16,40,128]{3,2,1,0:T(8,128)S(1)} %all_to_all.5.found_ref), custom_call_target="tpu_custom_call" | custom-call | flops 1024 | bytes 1024 | tf_op jit(solution)/shard_map/pallas_call | solution.py:456
  38.8 1.5 %collective-permute-start.7 = (f32[1,16,40,128]{3,2,1,0:T(8,128)}, f32[1,16,40,128]{3,2,1,0:T(8,128)}, u32[]{:S(2)}, u32[]{:S(2)}) collective-permute-start(f32[1,16,40,128]{3,2,1,0:T(8,128)} %get-tuple-element.29), channel_id=1, source_target_pairs={{0,16},{8,24},{16,0},{24,8},{1,17},{9,25},{17,1},{25,9},{2,18},{10... | collective-permute-start | bytes 983048 | tf_op jit(solution)/shard_map/ppermute | solution.py:493
  40.3 1.9 %shard_map.33.edge_ref = f32[4,2,2,3,128,128]{5,4,3,2,1,0:T(8,128)S(1)} custom-call(f32[4,2,2,3,128,128]{5,4,3,2,1,0:T(8,128)} %get-tuple-element.21.refs_0_, f32[1,16,40,128]{3,2,1,0:T(8,128)S(1)} %get-tuple-element.24.refs_1_.keep_ref), custom_call_target="tpu_custom_call" | custom-call | flops 1024 | bytes 1024 | tf_op jit(solution)/shard_map/pallas_call | solution.py:263
  42.2 6.7 %collective-permute-done.7.found_ref = f32[1,16,40,128]{3,2,1,0:T(8,128)} collective-permute-done((f32[1,16,40,128]{3,2,1,0:T(8,128)}, f32[1,16,40,128]{3,2,1,0:T(8,128)}, u32[]{:S(2)}, u32[]{:S(2)}) %collective-permute-start.7) | collective-permute-done | bytes 327712 | tf_op jit(solution)/shard_map/ppermute | solution.py:493
  48.9 1.0 %shard_map.36 = (f32[16,40,128]{2,1,0:T(8,128)S(1)}, f32[3,40,128]{2,1,0:T(8,128)S(1)}, f32[3,40,128]{2,1,0:T(8,128)S(1)}) custom-call(s32[2]{0:T(128)S(1)} %pad_add_fusion.1.side_ref, f32[1,16,40,128]{3,2,1,0:T(8,128)S(1)} %get-tuple-element.24.refs_1_.keep_ref, f32[1,16,40,128]{3,2,1,0:T(8,128)} %collective-permute-done.7.found_ref), custom_call_target="tpu_custom_call" | custom-call | flops 1024 | bytes 1024 | tf_op jit(solution)/shard_map/pallas_call | solution.py:477
  49.9 15.7 %collective-permute-start.8 = (f32[3,40,128]{2,1,0:T(8,128)S(1)}, f32[3,40,128]{2,1,0:T(8,128)S(1)}, u32[]{:S(2)}, u32[]{:S(2)}) collective-permute-start(f32[3,40,128]{2,1,0:T(8,128)S(1)} %get-tuple-element.31), channel_id=1, source_target_pairs={{0,1},{1,0},{2,3},{3,2},{4,5},{5,4},{6,7},{7,6},{8,9},{9,8},{10,11... | collective-permute-start | bytes 184328 | tf_op jit(solution)/shard_map/ppermute | solution.py:423
  65.7 0.7 collective-permute-start.9
  66.3 7.4 %collective-permute-done.2.halo_ref = bf16[4,2,2,3,128,128]{5,4,3,2,1,0:T(8,128)(2,1)S(1)} collective-permute-done((bf16[4,2,2,3,128,128]{5,4,3,2,1,0:T(8,128)(2,1)S(1)}, bf16[4,2,2,3,128,128]{5,4,3,2,1,0:T(8,128)(2,1)S(1)}, u32[]{:S(2)}, u32[]{:S(2)}) %collective-permute-start.2) | collective-permute-done | bytes 1572896 | tf_op jit(solution)/shard_map/ppermute | solution.py:423
  73.8 1.0 %shard_map.34 = (f32[2,40,128]{2,1,0:T(8,128)S(1)}, f32[2,40,128]{2,1,0:T(8,128)S(1)}) custom-call(s32[2]{0:T(128)S(1)} %pad_add_fusion.1.side_ref, f32[1,4]{1,0:T(1,128)S(1)} %broadcast_multiply_fusion.weight_ref, f32[4,2,2,3,128,128]{5,4,3,2,1,0:T(8,128)S(1)} %shard_map.33.edge_ref, bf16[4,2,2,3,128,128]{5,4,3,2,1,0:T(8,128)(2,1)S(1)} %collective-permute-done.2.halo_ref), custom_call_target="tpu_custom_call" | custom-call | flops 1024 | bytes 1024 | tf_op jit(solution)/shard_map/pallas_call | solution.py:294
  74.8 0.1 collective-permute-start.3
  74.8 0.1 pad_add_fusion.place_ref
  74.9 1.1 %collective-permute-done.3.found_ref = f32[2,40,128]{2,1,0:T(8,128)S(1)} collective-permute-done((f32[2,40,128]{2,1,0:T(8,128)S(1)}, f32[2,40,128]{2,1,0:T(8,128)S(1)}, u32[]{:S(2)}, u32[]{:S(2)}) %collective-permute-start.3) | collective-permute-done | bytes 40992 | tf_op jit(solution)/shard_map/ppermute | solution.py:432
  76.0 1.5 %collective-permute-start.4 = (f32[40,128]{1,0:T(8,128)S(1)}, f32[40,128]{1,0:T(8,128)S(1)}, u32[]{:S(2)}, u32[]{:S(2)}) collective-permute-start(f32[40,128]{1,0:T(8,128)S(1)} %get-tuple-element.28), channel_id=1, source_target_pairs={{0,16},{8,24},{16,0},{24,8},{1,17},{9,25},{17,1},{25,9},{2,18},{10... | collective-permute-start | bytes 61448 | tf_op jit(solution)/shard_map/ppermute | solution.py:435
  77.5 2.5 %collective-permute-start.6 = (f32[40,128]{1,0:T(8,128)S(1)}, f32[40,128]{1,0:T(8,128)S(1)}, u32[]{:S(2)}, u32[]{:S(2)}) collective-permute-start(f32[40,128]{1,0:T(8,128)S(1)} %get-tuple-element.28), channel_id=1, source_target_pairs={{0,17},{1,16},{2,19},{3,18},{4,21},{5,20},{6,23},{7,22},{8,25},{9,... | collective-permute-start | bytes 61448 | tf_op jit(solution)/shard_map/ppermute | solution.py:437
  80.0 0.0 collective-permute-start.5
  80.0 0.0 collective-permute-done.8.near_ref
  80.0 0.0 collective-permute-done.9.far_ref
  80.0 1.4 %shard_map.37.before_ref = f32[16,32,128]{2,1,0:T(8,128)S(1)} custom-call(s32[3]{0:T(128)S(1)} %pad_add_fusion.place_ref, f32[16,40,128]{2,1,0:T(8,128)S(1)} %get-tuple-element.30.base_ref, f32[3,40,128]{2,1,0:T(8,128)S(1)} %collective-permute-done.8.near_ref, f32[3,40,128]{2,1,0:T(8,128)S(1)} %collective-permute-done.9.far_ref), custom_call_target="tpu_custom_call" | custom-call | flops 10000000000 | bytes 1024 | tf_op jit(solution)/shard_map/pallas_call | solution.py:376
  81.4 0.0 collective-permute-done.4.own_refs_1_
  81.4 2.4 %collective-permute-done.5.beyond_refs_0_ = f32[40,128]{1,0:T(8,128)S(1)} collective-permute-done((f32[40,128]{1,0:T(8,128)S(1)}, f32[40,128]{1,0:T(8,128)S(1)}, u32[]{:S(2)}, u32[]{:S(2)}) %collective-permute-start.5) | collective-permute-done | bytes 20512 | tf_op jit(solution)/shard_map/ppermute | solution.py:436
  83.8 0.0 collective-permute-done.6.beyond_refs_1_
  83.8 1.5 %shard_map.38 = f32[16,32,128]{2,1,0:T(8,128)} custom-call(s32[3]{0:T(128)S(1)} %pad_add_fusion.place_ref, f32[40,128]{1,0:T(8,128)S(1)} %get-tuple-element.27.own_refs_0_, f32[40,128]{1,0:T(8,128)S(1)} %collective-permute-done.4.own_refs_1_, f32[40,128]{1,0:T(8,128)S(1)} %collective-permute-done.5.beyond_refs_0_, ...), custom_call_target="tpu_custom_call" | custom-call | flops 1024 | bytes 1024 | tf_op jit(solution)/shard_map/pallas_call | solution.py:410
  (2 shorter events, 0.0 us)
Async XLA Ops:
  1.4 72.4 %collective-permute-start.2 = (bf16[4,2,2,3,128,128]{5,4,3,2,1,0:T(8,128)(2,1)S(1)}, bf16[4,2,2,3,128,128]{5,4,3,2,1,0:T(8,128)(2,1)S(1)}, u32[]{:S(2)}, u32[]{:S(2)}) collective-permute-start(bf16[4,2,2,3,128,128]{5,4,3,2,1,0:T(8,128)(2,1)S(1)} %shard_map.28.refs_0_), channel_id=1, source_target_pairs={{0,1},{1,0},{2,3},{3,2},{4,5},{5,4},{6,7},{7,6},{8,9},{9,8},{10,11... | collective-permute-start | bytes 4718600 | tf_op jit(solution)/shard_map/ppermute | solution.py:423
  4.5 5.7 %copy-start = (f32[1,4]{1,0:T(1,128)S(1)}, f32[1,4]{1,0:T(1,128)}, u32[]{:S(2)}) copy-start(f32[1,4]{1,0:T(1,128)} %param.3) | copy-start | bytes 52
  7.0 23.8 %collective-permute-start = (bf16[2,2,2,3,128,128]{5,4,3,2,1,0:T(8,128)(2,1)}, bf16[2,2,2,3,128,128]{5,4,3,2,1,0:T(8,128)(2,1)}, u32[]{:S(2)}, u32[]{:S(2)}) collective-permute-start(bf16[2,2,2,3,128,128]{5,4,3,2,1,0:T(8,128)(2,1)} %get-tuple-element.19.refs_0_), channel_id=1, source_target_pairs={{1,2},{2,1},{3,4},{4,3},{5,6},{6,5},{9,10},{10,9},{11,12},{12,11},... | collective-permute-start | bytes 2359304 | tf_op jit(solution)/shard_map/ppermute | solution.py:423
  8.6 22.2 %collective-permute-start.1 = (bf16[2,2,2,3,128,128]{5,4,3,2,1,0:T(8,128)(2,1)}, bf16[2,2,2,3,128,128]{5,4,3,2,1,0:T(8,128)(2,1)}, u32[]{:S(2)}, u32[]{:S(2)}) collective-permute-start(bf16[2,2,2,3,128,128]{5,4,3,2,1,0:T(8,128)(2,1)} %get-tuple-element.20.refs_1_), channel_id=1, source_target_pairs={{1,2},{2,1},{3,4},{4,3},{5,6},{6,5},{9,10},{10,9},{11,12},{12,11},... | collective-permute-start | bytes 2359304 | tf_op jit(solution)/shard_map/ppermute | solution.py:423
  38.8 10.1 %collective-permute-start.7 = (f32[1,16,40,128]{3,2,1,0:T(8,128)}, f32[1,16,40,128]{3,2,1,0:T(8,128)}, u32[]{:S(2)}, u32[]{:S(2)}) collective-permute-start(f32[1,16,40,128]{3,2,1,0:T(8,128)} %get-tuple-element.29), channel_id=1, source_target_pairs={{0,16},{8,24},{16,0},{24,8},{1,17},{9,25},{17,1},{25,9},{2,18},{10... | collective-permute-start | bytes 983048 | tf_op jit(solution)/shard_map/ppermute | solution.py:493
  49.9 30.1 %collective-permute-start.8 = (f32[3,40,128]{2,1,0:T(8,128)S(1)}, f32[3,40,128]{2,1,0:T(8,128)S(1)}, u32[]{:S(2)}, u32[]{:S(2)}) collective-permute-start(f32[3,40,128]{2,1,0:T(8,128)S(1)} %get-tuple-element.31), channel_id=1, source_target_pairs={{0,1},{1,0},{2,3},{3,2},{4,5},{5,4},{6,7},{7,6},{8,9},{9,8},{10,11... | collective-permute-start | bytes 184328 | tf_op jit(solution)/shard_map/ppermute | solution.py:423
  65.7 14.3 %collective-permute-start.9 = (f32[3,40,128]{2,1,0:T(8,128)S(1)}, f32[3,40,128]{2,1,0:T(8,128)S(1)}, u32[]{:S(2)}, u32[]{:S(2)}) collective-permute-start(f32[3,40,128]{2,1,0:T(8,128)S(1)} %get-tuple-element.32), channel_id=1, source_target_pairs={{1,2},{2,1},{3,4},{4,3},{5,6},{6,5},{9,10},{10,9},{11,12},{12,11},... | collective-permute-start | bytes 184328 | tf_op jit(solution)/shard_map/ppermute | solution.py:423
  74.8 1.3 %collective-permute-start.3 = (f32[2,40,128]{2,1,0:T(8,128)S(1)}, f32[2,40,128]{2,1,0:T(8,128)S(1)}, u32[]{:S(2)}, u32[]{:S(2)}) collective-permute-start(f32[2,40,128]{2,1,0:T(8,128)S(1)} %get-tuple-element.26), channel_id=1, source_target_pairs={{0,8},{8,0},{16,24},{24,16},{1,9},{9,1},{17,25},{25,17},{2,10},{10... | collective-permute-start | bytes 122888 | tf_op jit(solution)/shard_map/ppermute | solution.py:432
  76.0 5.4 %collective-permute-start.4 = (f32[40,128]{1,0:T(8,128)S(1)}, f32[40,128]{1,0:T(8,128)S(1)}, u32[]{:S(2)}, u32[]{:S(2)}) collective-permute-start(f32[40,128]{1,0:T(8,128)S(1)} %get-tuple-element.28), channel_id=1, source_target_pairs={{0,16},{8,24},{16,0},{24,8},{1,17},{9,25},{17,1},{25,9},{2,18},{10... | collective-permute-start | bytes 61448 | tf_op jit(solution)/shard_map/ppermute | solution.py:435
  77.5 6.2 %collective-permute-start.6 = (f32[40,128]{1,0:T(8,128)S(1)}, f32[40,128]{1,0:T(8,128)S(1)}, u32[]{:S(2)}, u32[]{:S(2)}) collective-permute-start(f32[40,128]{1,0:T(8,128)S(1)} %get-tuple-element.28), channel_id=1, source_target_pairs={{0,17},{1,16},{2,19},{3,18},{4,21},{5,20},{6,23},{7,22},{8,25},{9,... | collective-permute-start | bytes 61448 | tf_op jit(solution)/shard_map/ppermute | solution.py:437
  80.0 3.8 %collective-permute-start.5 = (f32[40,128]{1,0:T(8,128)S(1)}, f32[40,128]{1,0:T(8,128)S(1)}, u32[]{:S(2)}, u32[]{:S(2)}) collective-permute-start(f32[40,128]{1,0:T(8,128)S(1)} %get-tuple-element.27.own_refs_0_), channel_id=1, source_target_pairs={{0,1},{1,0},{2,3},{3,2},{4,5},{5,4},{6,7},{7,6},{8,9},{9,8},{10,11... | collective-permute-start | bytes 61448 | tf_op jit(solution)/shard_map/ppermute | solution.py:436

commit v5 on v4

--- a/solution.py
+++ b/solution.py
@@ -271,11 +271,12 @@
     )(*[hbm(block) for block in blocks], *after)
 
 
-def near_kernel(side_ref, weight_ref, edge_ref, halo_ref, keep_ref, give_ref, tall_ref):
+def near_kernel(count, side_ref, weight_ref, edge_ref, *refs):
+    halo_refs, (keep_ref, give_ref, tall_ref) = refs[:count], refs[count:]
     modes, halves, _, parts, rows, _ = edge_ref.shape
     scales = [weight_ref[0, mode] for mode in range(modes)]
     strains = [strain_of(edge_ref, mode) for mode in range(modes)]
-    halos = [halo_of(halo_ref, mode) for mode in range(modes)]
+    halos = [halo_of(ref, mode) for ref in halo_refs for mode in range(ref.shape[0])]
     _, tall, lanes = keep_ref.shape
     band = tall - 2 * EDGE
     empty = jnp.zeros((2 * EDGE, lanes), jnp.float32)
@@ -288,18 +289,19 @@
         ref[turn // 2] = tall_ref[pl.ds(start, tall)]
 
 
-def finish_near(sides, weights, edges, halo, freqs):
+def finish_near(sides, weights, edges, halos, freqs):
     rows, lanes = edges.shape[4:]
     bands = jax.ShapeDtypeStruct((2, rows // freqs + 2 * EDGE, lanes), jnp.float32)
     return pl.pallas_call(
-        near_kernel,
-        in_specs=[pl.BlockSpec(memory_space=pltpu.SMEM)] * 2 + [pl.BlockSpec(memory_space=pltpu.VMEM)] * 2,
+        functools.partial(near_kernel, len(halos)),
+        in_specs=[pl.BlockSpec(memory_space=pltpu.SMEM)] * 2
+        + [pl.BlockSpec(memory_space=pltpu.VMEM)] * (1 + len(halos)),
         out_specs=[pl.BlockSpec(memory_space=pltpu.VMEM)] * 2,
         out_shape=[bands] * 2,
         scratch_shapes=[pltpu.VMEM((rows + 2 * EDGE, lanes), jnp.float32)],
         compiler_params=pltpu.CompilerParams(vmem_limit_bytes=SMALL_VMEM),
         cost_estimate=QUICK,
-    )(sides, weights, edges, halo)
+    )(sides, weights, edges, *halos)
 
 
 def pair_kernel(keep_ref, found_ref, own_ref, other_ref):
@@ -513,8 +515,9 @@
     near_plane = jnp.where(odd == 0, slab - 1, 0)
     half = modes // 2
     groups = [(0, half), (half, modes - half)]
-    (near_out,) = planes(saved_modes, near_plane, [(0, modes)], [])
-    near_halo = swap(near_out, "space", near_pairs)
+    (first_out,) = planes(saved_modes, near_plane, [(0, 1)], [])
+    (near_out,) = planes(saved_modes, near_plane, [(1, modes - 1)], [first_out])
+    near_halos = [swap(block, "space", near_pairs) for block in (first_out, near_out)]
     far_outs = planes(saved_modes, slab - 1 - near_plane, groups, [near_out])
     far_halos = [swap(block, "space", far_pairs) for block in far_outs]
 
@@ -526,7 +529,7 @@
     where = jnp.stack([odd, place * slab, lax.axis_index("freq") * (rows // freqs)]).astype(jnp.int32)
     smoothed = smooth(where, base, near, far, slab * slabs, rows)
 
-    keep, give = finish_near(sides, weights, *fetch([near_edges], [keep]), near_halo, freqs)
+    keep, give = finish_near(sides, weights, *fetch([near_edges], [keep]), near_halos, freqs)
     return add_near(where, *near_sums(keep, give, near_pairs), smoothed, rows)
 
 

time: 85.6 us -> 85.3 us (level)
  waiting for transfers between devices: 17.6 us -> 14.6 us
  starting transfers between devices: 28.1 us -> 29.7 us
    ppermute x5 -> x6, waiting for transfers between devices: 7.45 us -> 4.74 us  [swap(): lax.ppermute(block, axis, [p for a, b in pairs for p in ((a, b), (b, a))])]
    ppermute x5 -> x6, starting transfers between devices: 22.6 us -> 23.7 us  [swap(): lax.ppermute(block, axis, [p for a, b in pairs for p in ((a, b), (b, a))])]
    pallas_call x2 -> x3, Pallas kernels: 3.97 us -> 4.83 us  [planes(): pl.pallas_call(functools.partial(plane_kernel, [first for first, _ in gro...]
  transfers between devices with their start and end apart: 10 -> 11, of which waited for: 4 -> 4; matrix products, arithmetic and copies ran while one was open for 0% -> 0% of each run, Pallas kernels for 37% -> 39%
where the time goes in v5:
time: 85.3 us; the launch traced here: 84.9 us
  Pallas kernels  35.4 us (42%)
  starting transfers between devices  29.7 us (35%)
  waiting for transfers between devices  14.6 us (17%)
  blocking collectives  4.79 us (6%)
    ppermute x6, starting transfers between devices, swap(): lax.ppermute(block, axis, [p for a, b in pairs for p in ((a, b), (b, a))])  23.7 us
    pallas_call x1, Pallas kernels, interior(): pl.pallas_call(functools.partial(interior_kernel, begin, len(before), len...  20.6 us
    ppermute x1, waiting for transfers between devices, band_sum(): found = lax.ppermute(send, 'freq', [(i, i ^ 2) for i in range(count)])  6.42 us
    pallas_call x3, Pallas kernels, planes(): pl.pallas_call(functools.partial(plane_kernel, [first for first, _ in gro...  4.83 us
    all_to_all x1, blocking collectives, band_sum(): lax.all_to_all(turns, 'freq', 0, 0, axis_index_groups=groups, tiled=True)  4.79 us
    ppermute x6, waiting for transfers between devices, swap(): lax.ppermute(block, axis, [p for a, b in pairs for p in ((a, b), (b, a))])  4.74 us
    ppermute x1, starting transfers between devices, near_sums(): lax.ppermute(other, ('freq', 'space'), both(across, swaps, slabs))  2.45 us
    ppermute x1, waiting for transfers between devices, near_sums(): beyond = lax.ppermute(own, 'space', swaps)  2.35 us
  transfers between devices with their start and end apart: 11, of which 4 were waited for; matrix products, arithmetic and copies ran while one was open for 0% of the time, Pallas kernels for 39%

profile of v5, /device:TPU:0, one launch (start us, length us, event | category | flops | bytes accessed | tf_op | source)
XLA Modules:
  0.0 84.9 jit_solution(7531937410641841881)
XLA Ops:
  0.0 1.0 %shard_map.28.refs_0_ = bf16[1,2,2,3,128,128]{5,4,3,2,1,0:T(8,128)(2,1)S(1)} custom-call(s32[1]{0:T(128)} %bitcast.5.plane_ref, bf16[1,4,2,2,3,16,128,128]{7,6,5,4,3,2,1,0:T(8,128)(2,1)} %modes_ref.7), custom_call_target="tpu_custom_call" | custom-call | flops 1024 | bytes 1024 | tf_op jit(solution)/shard_map/pallas_call | solution.py:35
  1.0 3.0 %collective-permute-start.2 = (bf16[1,2,2,3,128,128]{5,4,3,2,1,0:T(8,128)(2,1)S(1)}, bf16[1,2,2,3,128,128]{5,4,3,2,1,0:T(8,128)(2,1)S(1)}, u32[]{:S(2)}, u32[]{:S(2)}) collective-permute-start(bf16[1,2,2,3,128,128]{5,4,3,2,1,0:T(8,128)(2,1)S(1)} %shard_map.28.refs_0_), channel_id=1, source_target_pairs={{0,1},{1,0},{2,3},{3,2},{4,5},{5,4},{6,7},{7,6},{8,9},{9,8},{10,11... | collective-permute-start | bytes 1179656 | tf_op jit(solution)/shard_map/ppermute | solution.py:425
  4.0 1.3 %shard_map.29.refs_0_ = bf16[3,2,2,3,128,128]{5,4,3,2,1,0:T(8,128)(2,1)S(1)} custom-call(s32[1]{0:T(128)} %bitcast.5.plane_ref, bf16[1,4,2,2,3,16,128,128]{7,6,5,4,3,2,1,0:T(8,128)(2,1)} %modes_ref.7, bf16[1,2,2,3,128,128]{5,4,3,2,1,0:T(8,128)(2,1)S(1)} %shard_map.28.refs_0_), custom_call_target="tpu_custom_call" | custom-call | flops 1024 | bytes 1024 | tf_op jit(solution)/shard_map/pallas_call | solution.py:35
  5.3 0.1 collective-permute-start.3
  5.4 0.0 copy-start
  5.4 2.6 %shard_map.30 = (bf16[2,2,2,3,128,128]{5,4,3,2,1,0:T(8,128)(2,1)}, bf16[2,2,2,3,128,128]{5,4,3,2,1,0:T(8,128)(2,1)}) custom-call(s32[1]{0:T(128)} %bitcast.4.plane_ref, bf16[1,4,2,2,3,16,128,128]{7,6,5,4,3,2,1,0:T(8,128)(2,1)} %modes_ref.7, bf16[3,2,2,3,128,128]{5,4,3,2,1,0:T(8,128)(2,1)S(1)} %shard_map.29.refs_0_), custom_call_target="tpu_custom_call" | custom-call | flops 1024 | bytes 1024 | tf_op jit(solution)/shard_map/pallas_call | solution.py:35
  8.0 1.6 %collective-permute-start = (bf16[2,2,2,3,128,128]{5,4,3,2,1,0:T(8,128)(2,1)}, bf16[2,2,2,3,128,128]{5,4,3,2,1,0:T(8,128)(2,1)}, u32[]{:S(2)}, u32[]{:S(2)}) collective-permute-start(bf16[2,2,2,3,128,128]{5,4,3,2,1,0:T(8,128)(2,1)} %get-tuple-element.19.refs_0_), channel_id=1, source_target_pairs={{1,2},{2,1},{3,4},{4,3},{5,6},{6,5},{9,10},{10,9},{11,12},{12,11},... | collective-permute-start | bytes 2359304 | tf_op jit(solution)/shard_map/ppermute | solution.py:425
  9.6 1.5 %collective-permute-start.1 = (bf16[2,2,2,3,128,128]{5,4,3,2,1,0:T(8,128)(2,1)}, bf16[2,2,2,3,128,128]{5,4,3,2,1,0:T(8,128)(2,1)}, u32[]{:S(2)}, u32[]{:S(2)}) collective-permute-start(bf16[2,2,2,3,128,128]{5,4,3,2,1,0:T(8,128)(2,1)} %get-tuple-element.20.refs_1_), channel_id=1, source_target_pairs={{1,2},{2,1},{3,4},{4,3},{5,6},{6,5},{9,10},{10,9},{11,12},{12,11},... | collective-permute-start | bytes 2359304 | tf_op jit(solution)/shard_map/ppermute | solution.py:425
  11.1 0.0 copy-done
  11.1 0.1 pad_add_fusion.1.side_ref
  11.2 20.6 %shard_map.31 = (f32[16,144,128]{2,1,0:T(8,128)S(1)}, f32[8,128]{1,0:T(8,128)}, f32[4,2,2,3,128,128]{5,4,3,2,1,0:T(8,128)}, f32[4,2,2,3,128,128]{5,4,3,2,1,0:T(8,128)S(1)}) custom-call(s32[2]{0:T(128)S(1)} %pad_add_fusion.1.side_ref, f32[1,4]{1,0:T(1,128)S(1)} %broadcast_multiply_fusion.weight_ref, bf16[1,4,2,2,3,16,128,128]{7,6,5,4,3,2,1,0:T(8,128)(2,1)} %modes_ref.7, ...), custom_call_target="tpu_custom_call" | custom-call | flops 8000000000 | bytes 1024 | tf_op jit(solution)/shard_map/pallas_call | solution.py:150
  31.8 0.0 collective-permute-done.refs_0_
  31.8 0.0 collective-permute-done.1.refs_1_
  31.8 1.9 %shard_map.32 = f32[4,16,40,128]{3,2,1,0:T(8,128)S(1)} custom-call(s32[2]{0:T(128)S(1)} %pad_add_fusion.1.side_ref, f32[1,4]{1,0:T(1,128)S(1)} %broadcast_multiply_fusion.weight_ref, f32[4,2,2,3,128,128]{5,4,3,2,1,0:T(8,128)S(1)} %get-tuple-element.22.edge_ref, bf16[2,2,2,3,128,128]{5,4,3,2,1,0:T(8,128)(2,1)} %collective-permute-done.refs_0_, ...), custom_call_target="tpu_custom_call" | custom-call | flops 1024 | bytes 1024 | tf_op jit(solution)/shard_map/pallas_call | solution.py:241
  33.7 4.8 %all_to_all.5.found_ref = f32[4,16,40,128]{3,2,1,0:T(8,128)S(1)} all-to-all(f32[4,16,40,128]{3,2,1,0:T(8,128)S(1)} %shard_map.32), channel_id=1, replica_groups={{0,8},{16,24},{1,9},{17,25},{2,10},{18,26},{3,11},{19,27},{4,12},{20,28..., dimensions={0} | all-to-all | bytes 2621440 | tf_op jit(solution)/shard_map/all_to_all | solution.py:494
  38.5 1.4 %shard_map.33 = (f32[1,16,40,128]{3,2,1,0:T(8,128)}, f32[1,16,40,128]{3,2,1,0:T(8,128)S(1)}) custom-call(s32[2]{0:T(128)S(1)} %pad_add_fusion.1.side_ref, f32[4,16,40,128]{3,2,1,0:T(8,128)S(1)} %all_to_all.5.found_ref), custom_call_target="tpu_custom_call" | custom-call | flops 1024 | bytes 1024 | tf_op jit(solution)/shard_map/pallas_call | solution.py:458
  39.8 2.0 %collective-permute-start.8 = (f32[1,16,40,128]{3,2,1,0:T(8,128)}, f32[1,16,40,128]{3,2,1,0:T(8,128)}, u32[]{:S(2)}, u32[]{:S(2)}) collective-permute-start(f32[1,16,40,128]{3,2,1,0:T(8,128)} %get-tuple-element.29), channel_id=1, source_target_pairs={{0,16},{8,24},{16,0},{24,8},{1,17},{9,25},{17,1},{25,9},{2,18},{10... | collective-permute-start | bytes 983048 | tf_op jit(solution)/shard_map/ppermute | solution.py:495
  41.8 1.9 %shard_map.34.edge_ref = f32[4,2,2,3,128,128]{5,4,3,2,1,0:T(8,128)S(1)} custom-call(f32[4,2,2,3,128,128]{5,4,3,2,1,0:T(8,128)} %get-tuple-element.21.refs_0_, f32[1,16,40,128]{3,2,1,0:T(8,128)S(1)} %get-tuple-element.24.refs_1_.keep_ref), custom_call_target="tpu_custom_call" | custom-call | flops 1024 | bytes 1024 | tf_op jit(solution)/shard_map/pallas_call | solution.py:263
  43.7 6.4 %collective-permute-done.8.found_ref = f32[1,16,40,128]{3,2,1,0:T(8,128)} collective-permute-done((f32[1,16,40,128]{3,2,1,0:T(8,128)}, f32[1,16,40,128]{3,2,1,0:T(8,128)}, u32[]{:S(2)}, u32[]{:S(2)}) %collective-permute-start.8) | collective-permute-done | bytes 327712 | tf_op jit(solution)/shard_map/ppermute | solution.py:495
  50.1 1.0 %shard_map.37 = (f32[16,40,128]{2,1,0:T(8,128)S(1)}, f32[3,40,128]{2,1,0:T(8,128)S(1)}, f32[3,40,128]{2,1,0:T(8,128)S(1)}) custom-call(s32[2]{0:T(128)S(1)} %pad_add_fusion.1.side_ref, f32[1,16,40,128]{3,2,1,0:T(8,128)S(1)} %get-tuple-element.24.refs_1_.keep_ref, f32[1,16,40,128]{3,2,1,0:T(8,128)} %collective-permute-done.8.found_ref), custom_call_target="tpu_custom_call" | custom-call | flops 1024 | bytes 1024 | tf_op jit(solution)/shard_map/pallas_call | solution.py:479
  51.1 16.8 %collective-permute-start.9 = (f32[3,40,128]{2,1,0:T(8,128)S(1)}, f32[3,40,128]{2,1,0:T(8,128)S(1)}, u32[]{:S(2)}, u32[]{:S(2)}) collective-permute-start(f32[3,40,128]{2,1,0:T(8,128)S(1)} %get-tuple-element.31), channel_id=1, source_target_pairs={{0,1},{1,0},{2,3},{3,2},{4,5},{5,4},{6,7},{7,6},{8,9},{9,8},{10,11... | collective-permute-start | bytes 184328 | tf_op jit(solution)/shard_map/ppermute | solution.py:425
  68.0 0.7 collective-permute-start.10
  68.6 0.0 collective-permute-done.2.refs_0_
  68.6 4.7 %collective-permute-done.3.refs_1_ = bf16[3,2,2,3,128,128]{5,4,3,2,1,0:T(8,128)(2,1)S(1)} collective-permute-done((bf16[3,2,2,3,128,128]{5,4,3,2,1,0:T(8,128)(2,1)S(1)}, bf16[3,2,2,3,128,128]{5,4,3,2,1,0:T(8,128)(2,1)S(1)}, u32[]{:S(2)}, u32[]{:S(2)}) %collective-permute-start.3) | collective-permute-done | bytes 1179680 | tf_op jit(solution)/shard_map/ppermute | solution.py:425
  73.4 1.0 %shard_map.35 = (f32[2,40,128]{2,1,0:T(8,128)S(1)}, f32[2,40,128]{2,1,0:T(8,128)S(1)}) custom-call(s32[2]{0:T(128)S(1)} %pad_add_fusion.1.side_ref, f32[1,4]{1,0:T(1,128)S(1)} %broadcast_multiply_fusion.weight_ref, f32[4,2,2,3,128,128]{5,4,3,2,1,0:T(8,128)S(1)} %shard_map.34.edge_ref, bf16[1,2,2,3,128,128]{5,4,3,2,1,0:T(8,128)(2,1)S(1)} %collective-permute-done.2.refs_0_, ...), custom_call_target="tpu_custom_call" | custom-call | flops 1024 | bytes 1024 | tf_op jit(solution)/shard_map/pallas_call | solution.py:295
  74.3 0.1 collective-permute-start.4
  74.4 0.1 pad_add_fusion.place_ref
  74.5 1.1 %collective-permute-done.4.found_ref = f32[2,40,128]{2,1,0:T(8,128)S(1)} collective-permute-done((f32[2,40,128]{2,1,0:T(8,128)S(1)}, f32[2,40,128]{2,1,0:T(8,128)S(1)}, u32[]{:S(2)}, u32[]{:S(2)}) %collective-permute-start.4) | collective-permute-done | bytes 40992 | tf_op jit(solution)/shard_map/ppermute | solution.py:434
  75.6 1.5 %collective-permute-start.5 = (f32[40,128]{1,0:T(8,128)S(1)}, f32[40,128]{1,0:T(8,128)S(1)}, u32[]{:S(2)}, u32[]{:S(2)}) collective-permute-start(f32[40,128]{1,0:T(8,128)S(1)} %get-tuple-element.28), channel_id=1, source_target_pairs={{0,16},{8,24},{16,0},{24,8},{1,17},{9,25},{17,1},{25,9},{2,18},{10... | collective-permute-start | bytes 61448 | tf_op jit(solution)/shard_map/ppermute | solution.py:437
  77.1 2.5 %collective-permute-start.7 = (f32[40,128]{1,0:T(8,128)S(1)}, f32[40,128]{1,0:T(8,128)S(1)}, u32[]{:S(2)}, u32[]{:S(2)}) collective-permute-start(f32[40,128]{1,0:T(8,128)S(1)} %get-tuple-element.28), channel_id=1, source_target_pairs={{0,17},{1,16},{2,19},{3,18},{4,21},{5,20},{6,23},{7,22},{8,25},{9,... | collective-permute-start | bytes 61448 | tf_op jit(solution)/shard_map/ppermute | solution.py:439
  79.6 0.0 collective-permute-start.6
  79.6 0.0 collective-permute-done.9.near_ref
  79.6 0.0 collective-permute-done.10.far_ref
  79.6 1.4 %shard_map.38.before_ref = f32[16,32,128]{2,1,0:T(8,128)S(1)} custom-call(s32[3]{0:T(128)S(1)} %pad_add_fusion.place_ref, f32[16,40,128]{2,1,0:T(8,128)S(1)} %get-tuple-element.30.base_ref, f32[3,40,128]{2,1,0:T(8,128)S(1)} %collective-permute-done.9.near_ref, f32[3,40,128]{2,1,0:T(8,128)S(1)} %collective-permute-done.10.far_ref), custom_call_target="tpu_custom_call" | custom-call | flops 10000000000 | bytes 1024 | tf_op jit(solution)/shard_map/pallas_call | solution.py:378
  81.0 0.0 collective-permute-done.5.own_refs_1_
  81.0 2.4 %collective-permute-done.6.beyond_refs_0_ = f32[40,128]{1,0:T(8,128)S(1)} collective-permute-done((f32[40,128]{1,0:T(8,128)S(1)}, f32[40,128]{1,0:T(8,128)S(1)}, u32[]{:S(2)}, u32[]{:S(2)}) %collective-permute-start.6) | collective-permute-done | bytes 20512 | tf_op jit(solution)/shard_map/ppermute | solution.py:438
  83.4 0.0 collective-permute-done.7.beyond_refs_1_
  83.4 1.5 %shard_map.39 = f32[16,32,128]{2,1,0:T(8,128)} custom-call(s32[3]{0:T(128)S(1)} %pad_add_fusion.place_ref, f32[40,128]{1,0:T(8,128)S(1)} %get-tuple-element.27.own_refs_0_, f32[40,128]{1,0:T(8,128)S(1)} %collective-permute-done.5.own_refs_1_, f32[40,128]{1,0:T(8,128)S(1)} %collective-permute-done.6.beyond_refs_0_, ...), custom_call_target="tpu_custom_call" | custom-call | flops 1024 | bytes 1024 | tf_op jit(solution)/shard_map/pallas_call | solution.py:412
  (2 shorter events, 0.0 us)
Async XLA Ops:
  1.0 67.6 %collective-permute-start.2 = (bf16[1,2,2,3,128,128]{5,4,3,2,1,0:T(8,128)(2,1)S(1)}, bf16[1,2,2,3,128,128]{5,4,3,2,1,0:T(8,128)(2,1)S(1)}, u32[]{:S(2)}, u32[]{:S(2)}) collective-permute-start(bf16[1,2,2,3,128,128]{5,4,3,2,1,0:T(8,128)(2,1)S(1)} %shard_map.28.refs_0_), channel_id=1, source_target_pairs={{0,1},{1,0},{2,3},{3,2},{4,5},{5,4},{6,7},{7,6},{8,9},{9,8},{10,11... | collective-permute-start | bytes 1179656 | tf_op jit(solution)/shard_map/ppermute | solution.py:425
  5.3 68.0 %collective-permute-start.3 = (bf16[3,2,2,3,128,128]{5,4,3,2,1,0:T(8,128)(2,1)S(1)}, bf16[3,2,2,3,128,128]{5,4,3,2,1,0:T(8,128)(2,1)S(1)}, u32[]{:S(2)}, u32[]{:S(2)}) collective-permute-start(bf16[3,2,2,3,128,128]{5,4,3,2,1,0:T(8,128)(2,1)S(1)} %shard_map.29.refs_0_), channel_id=1, source_target_pairs={{0,1},{1,0},{2,3},{3,2},{4,5},{5,4},{6,7},{7,6},{8,9},{9,8},{10,11... | collective-permute-start | bytes 3538952 | tf_op jit(solution)/shard_map/ppermute | solution.py:425
  5.4 5.7 %copy-start = (f32[1,4]{1,0:T(1,128)S(1)}, f32[1,4]{1,0:T(1,128)}, u32[]{:S(2)}) copy-start(f32[1,4]{1,0:T(1,128)} %param.3) | copy-start | bytes 52
  8.0 23.8 %collective-permute-start = (bf16[2,2,2,3,128,128]{5,4,3,2,1,0:T(8,128)(2,1)}, bf16[2,2,2,3,128,128]{5,4,3,2,1,0:T(8,128)(2,1)}, u32[]{:S(2)}, u32[]{:S(2)}) collective-permute-start(bf16[2,2,2,3,128,128]{5,4,3,2,1,0:T(8,128)(2,1)} %get-tuple-element.19.refs_0_), channel_id=1, source_target_pairs={{1,2},{2,1},{3,4},{4,3},{5,6},{6,5},{9,10},{10,9},{11,12},{12,11},... | collective-permute-start | bytes 2359304 | tf_op jit(solution)/shard_map/ppermute | solution.py:425
  9.6 22.2 %collective-permute-start.1 = (bf16[2,2,2,3,128,128]{5,4,3,2,1,0:T(8,128)(2,1)}, bf16[2,2,2,3,128,128]{5,4,3,2,1,0:T(8,128)(2,1)}, u32[]{:S(2)}, u32[]{:S(2)}) collective-permute-start(bf16[2,2,2,3,128,128]{5,4,3,2,1,0:T(8,128)(2,1)} %get-tuple-element.20.refs_1_), channel_id=1, source_target_pairs={{1,2},{2,1},{3,4},{4,3},{5,6},{6,5},{9,10},{10,9},{11,12},{12,11},... | collective-permute-start | bytes 2359304 | tf_op jit(solution)/shard_map/ppermute | solution.py:425
  39.8 10.3 %collective-permute-start.8 = (f32[1,16,40,128]{3,2,1,0:T(8,128)}, f32[1,16,40,128]{3,2,1,0:T(8,128)}, u32[]{:S(2)}, u32[]{:S(2)}) collective-permute-start(f32[1,16,40,128]{3,2,1,0:T(8,128)} %get-tuple-element.29), channel_id=1, source_target_pairs={{0,16},{8,24},{16,0},{24,8},{1,17},{9,25},{17,1},{25,9},{2,18},{10... | collective-permute-start | bytes 983048 | tf_op jit(solution)/shard_map/ppermute | solution.py:495
  51.1 28.5 %collective-permute-start.9 = (f32[3,40,128]{2,1,0:T(8,128)S(1)}, f32[3,40,128]{2,1,0:T(8,128)S(1)}, u32[]{:S(2)}, u32[]{:S(2)}) collective-permute-start(f32[3,40,128]{2,1,0:T(8,128)S(1)} %get-tuple-element.31), channel_id=1, source_target_pairs={{0,1},{1,0},{2,3},{3,2},{4,5},{5,4},{6,7},{7,6},{8,9},{9,8},{10,11... | collective-permute-start | bytes 184328 | tf_op jit(solution)/shard_map/ppermute | solution.py:425
  68.0 11.6 %collective-permute-start.10 = (f32[3,40,128]{2,1,0:T(8,128)S(1)}, f32[3,40,128]{2,1,0:T(8,128)S(1)}, u32[]{:S(2)}, u32[]{:S(2)}) collective-permute-start(f32[3,40,128]{2,1,0:T(8,128)S(1)} %get-tuple-element.32), channel_id=1, source_target_pairs={{1,2},{2,1},{3,4},{4,3},{5,6},{6,5},{9,10},{10,9},{11,12},{12,11},... | collective-permute-start | bytes 184328 | tf_op jit(solution)/shard_map/ppermute | solution.py:425
  74.3 1.3 %collective-permute-start.4 = (f32[2,40,128]{2,1,0:T(8,128)S(1)}, f32[2,40,128]{2,1,0:T(8,128)S(1)}, u32[]{:S(2)}, u32[]{:S(2)}) collective-permute-start(f32[2,40,128]{2,1,0:T(8,128)S(1)} %get-tuple-element.26), channel_id=1, source_target_pairs={{0,8},{8,0},{16,24},{24,16},{1,9},{9,1},{17,25},{25,17},{2,10},{10... | collective-permute-start | bytes 122888 | tf_op jit(solution)/shard_map/ppermute | solution.py:434
  75.6 5.4 %collective-permute-start.5 = (f32[40,128]{1,0:T(8,128)S(1)}, f32[40,128]{1,0:T(8,128)S(1)}, u32[]{:S(2)}, u32[]{:S(2)}) collective-permute-start(f32[40,128]{1,0:T(8,128)S(1)} %get-tuple-element.28), channel_id=1, source_target_pairs={{0,16},{8,24},{16,0},{24,8},{1,17},{9,25},{17,1},{25,9},{2,18},{10... | collective-permute-start | bytes 61448 | tf_op jit(solution)/shard_map/ppermute | solution.py:437
  77.1 6.2 %collective-permute-start.7 = (f32[40,128]{1,0:T(8,128)S(1)}, f32[40,128]{1,0:T(8,128)S(1)}, u32[]{:S(2)}, u32[]{:S(2)}) collective-permute-start(f32[40,128]{1,0:T(8,128)S(1)} %get-tuple-element.28), channel_id=1, source_target_pairs={{0,17},{1,16},{2,19},{3,18},{4,21},{5,20},{6,23},{7,22},{8,25},{9,... | collective-permute-start | bytes 61448 | tf_op jit(solution)/shard_map/ppermute | solution.py:439
  79.6 3.8 %collective-permute-start.6 = (f32[40,128]{1,0:T(8,128)S(1)}, f32[40,128]{1,0:T(8,128)S(1)}, u32[]{:S(2)}, u32[]{:S(2)}) collective-permute-start(f32[40,128]{1,0:T(8,128)S(1)} %get-tuple-element.27.own_refs_0_), channel_id=1, source_target_pairs={{0,1},{1,0},{2,3},{3,2},{4,5},{5,4},{6,7},{7,6},{8,9},{9,8},{10,11... | collective-permute-start | bytes 61448 | tf_op jit(solution)/shard_map/ppermute | solution.py:438

commit v6 on v5

--- a/solution.py
+++ b/solution.py
@@ -513,7 +513,7 @@
         return found.reshape((count, kinds, halves, parts, rows, lanes))
 
     near_plane = jnp.where(odd == 0, slab - 1, 0)
-    half = modes // 2
+    half = modes // 4 or 1
     groups = [(0, half), (half, modes - half)]
     (first_out,) = planes(saved_modes, near_plane, [(0, 1)], [])
     (near_out,) = planes(saved_modes, near_plane, [(1, modes - 1)], [first_out])

time: 85.3 us -> 95.1 us (1.11)
  waiting for transfers between devices: 14.6 us -> 35.6 us
  starting transfers between devices: 29.7 us -> 18.6 us
    ppermute x6, waiting for transfers between devices: 4.74 us -> 33.2 us  [swap(): lax.ppermute(block, axis, [p for a, b in pairs for p in ((a, b), (b, a))])]
    ppermute x6, starting transfers between devices: 23.7 us -> 11.2 us  [swap(): lax.ppermute(block, axis, [p for a, b in pairs for p in ((a, b), (b, a))])]
    ppermute x1, waiting for transfers between devices: 6.42 us -> 0.01 us  [band_sum(): found = lax.ppermute(send, 'freq', [(i, i ^ 2) for i in range(count)])]
    ppermute x1, starting transfers between devices: 2.45 us -> 4.25 us  [near_sums(): lax.ppermute(other, ('freq', 'space'), both(across, swaps, slabs))]
    ppermute x1, waiting for transfers between devices: 1.13 us -> 0.01 us  [near_sums(): lax.ppermute(give, 'freq', [(i, i ^ 1) for i in range(freqs)])]
  transfers between devices with their start and end apart: 11 -> 11, of which waited for: 4 -> 3; matrix products, arithmetic and copies ran while one was open for 0% -> 0% of each run, Pallas kernels for 39% -> 31%
where the time goes in v6:
time: 95.1 us; the launch traced here: 94.7 us
  waiting for transfers between devices  35.6 us (37%)
  Pallas kernels  35.5 us (37%)
  starting transfers between devices  18.6 us (20%)
  blocking collectives  4.79 us (5%)
    ppermute x6, waiting for transfers between devices, swap(): lax.ppermute(block, axis, [p for a, b in pairs for p in ((a, b), (b, a))])  33.2 us
    pallas_call x1, Pallas kernels, interior(): pl.pallas_call(functools.partial(interior_kernel, begin, len(before), len...  20.6 us
    ppermute x6, starting transfers between devices, swap(): lax.ppermute(block, axis, [p for a, b in pairs for p in ((a, b), (b, a))])  11.2 us
    pallas_call x3, Pallas kernels, planes(): pl.pallas_call(functools.partial(plane_kernel, [first for first, _ in gro...  4.86 us
    all_to_all x1, blocking collectives, band_sum(): lax.all_to_all(turns, 'freq', 0, 0, axis_index_groups=groups, tiled=True)  4.79 us
    ppermute x1, starting transfers between devices, near_sums(): lax.ppermute(other, ('freq', 'space'), both(across, swaps, slabs))  4.25 us
    ppermute x1, waiting for transfers between devices, near_sums(): beyond = lax.ppermute(own, 'space', swaps)  2.35 us
    pallas_call x1, Pallas kernels, finish_far(): pl.pallas_call(functools.partial(far_kernel, groups), in_specs=[pl.BlockS...  1.92 us
  transfers between devices with their start and end apart: 11, of which 3 were waited for; matrix products, arithmetic and copies ran while one was open for 0% of the time, Pallas kernels for 31%

profile of v6, /device:TPU:0, one launch (start us, length us, event | category | flops | bytes accessed | tf_op | source)
XLA Modules:
  0.0 94.7 jit_solution(12069470587490176542)
XLA Ops:
  0.0 1.0 %shard_map.28.refs_0_ = bf16[1,2,2,3,128,128]{5,4,3,2,1,0:T(8,128)(2,1)S(1)} custom-call(s32[1]{0:T(128)} %bitcast.5.plane_ref, bf16[1,4,2,2,3,16,128,128]{7,6,5,4,3,2,1,0:T(8,128)(2,1)} %modes_ref.7), custom_call_target="tpu_custom_call" | custom-call | flops 1024 | bytes 1024 | tf_op jit(solution)/shard_map/pallas_call | solution.py:35
  1.0 1.3 %shard_map.29.refs_0_ = bf16[3,2,2,3,128,128]{5,4,3,2,1,0:T(8,128)(2,1)S(1)} custom-call(s32[1]{0:T(128)} %bitcast.5.plane_ref, bf16[1,4,2,2,3,16,128,128]{7,6,5,4,3,2,1,0:T(8,128)(2,1)} %modes_ref.7, bf16[1,2,2,3,128,128]{5,4,3,2,1,0:T(8,128)(2,1)S(1)} %shard_map.28.refs_0_), custom_call_target="tpu_custom_call" | custom-call | flops 1024 | bytes 1024 | tf_op jit(solution)/shard_map/pallas_call | solution.py:35
  2.3 0.0 copy-start
  2.3 2.6 %shard_map.30 = (bf16[1,2,2,3,128,128]{5,4,3,2,1,0:T(8,128)(2,1)}, bf16[3,2,2,3,128,128]{5,4,3,2,1,0:T(8,128)(2,1)}) custom-call(s32[1]{0:T(128)} %bitcast.4.plane_ref, bf16[1,4,2,2,3,16,128,128]{7,6,5,4,3,2,1,0:T(8,128)(2,1)} %modes_ref.7, bf16[3,2,2,3,128,128]{5,4,3,2,1,0:T(8,128)(2,1)S(1)} %shard_map.29.refs_0_), custom_call_target="tpu_custom_call" | custom-call | flops 1024 | bytes 1024 | tf_op jit(solution)/shard_map/pallas_call | solution.py:35
  4.9 1.7 %collective-permute-start.1 = (bf16[3,2,2,3,128,128]{5,4,3,2,1,0:T(8,128)(2,1)}, bf16[3,2,2,3,128,128]{5,4,3,2,1,0:T(8,128)(2,1)}, u32[]{:S(2)}, u32[]{:S(2)}) collective-permute-start(bf16[3,2,2,3,128,128]{5,4,3,2,1,0:T(8,128)(2,1)} %get-tuple-element.20.refs_1_), channel_id=1, source_target_pairs={{1,2},{2,1},{3,4},{4,3},{5,6},{6,5},{9,10},{10,9},{11,12},{12,11},... | collective-permute-start | bytes 3538952 | tf_op jit(solution)/shard_map/ppermute | solution.py:425
  6.6 4.7 %collective-permute-start.2 = (bf16[1,2,2,3,128,128]{5,4,3,2,1,0:T(8,128)(2,1)S(1)}, bf16[1,2,2,3,128,128]{5,4,3,2,1,0:T(8,128)(2,1)S(1)}, u32[]{:S(2)}, u32[]{:S(2)}) collective-permute-start(bf16[1,2,2,3,128,128]{5,4,3,2,1,0:T(8,128)(2,1)S(1)} %shard_map.28.refs_0_), channel_id=1, source_target_pairs={{0,1},{1,0},{2,3},{3,2},{4,5},{5,4},{6,7},{7,6},{8,9},{9,8},{10,11... | collective-permute-start | bytes 1179656 | tf_op jit(solution)/shard_map/ppermute | solution.py:425
  11.4 0.1 collective-permute-start.3
  11.4 1.4 %collective-permute-start = (bf16[1,2,2,3,128,128]{5,4,3,2,1,0:T(8,128)(2,1)}, bf16[1,2,2,3,128,128]{5,4,3,2,1,0:T(8,128)(2,1)}, u32[]{:S(2)}, u32[]{:S(2)}) collective-permute-start(bf16[1,2,2,3,128,128]{5,4,3,2,1,0:T(8,128)(2,1)} %get-tuple-element.19.refs_0_), channel_id=1, source_target_pairs={{1,2},{2,1},{3,4},{4,3},{5,6},{6,5},{9,10},{10,9},{11,12},{12,11},... | collective-permute-start | bytes 1179656 | tf_op jit(solution)/shard_map/ppermute | solution.py:425
  12.9 0.0 copy-done
  12.9 0.1 pad_add_fusion.1.side_ref
  12.9 20.6 %shard_map.31 = (f32[16,144,128]{2,1,0:T(8,128)S(1)}, f32[8,128]{1,0:T(8,128)}, f32[4,2,2,3,128,128]{5,4,3,2,1,0:T(8,128)}, f32[4,2,2,3,128,128]{5,4,3,2,1,0:T(8,128)S(1)}) custom-call(s32[2]{0:T(128)S(1)} %pad_add_fusion.1.side_ref, f32[1,4]{1,0:T(1,128)S(1)} %broadcast_multiply_fusion.weight_ref, bf16[1,4,2,2,3,16,128,128]{7,6,5,4,3,2,1,0:T(8,128)(2,1)} %modes_ref.7, ...), custom_call_target="tpu_custom_call" | custom-call | flops 8000000000 | bytes 1024 | tf_op jit(solution)/shard_map/pallas_call | solution.py:150
  33.5 0.0 collective-permute-done.refs_0_
  33.5 0.0 collective-permute-done.1.refs_1_
  33.5 1.9 %shard_map.32 = f32[4,16,40,128]{3,2,1,0:T(8,128)S(1)} custom-call(s32[2]{0:T(128)S(1)} %pad_add_fusion.1.side_ref, f32[1,4]{1,0:T(1,128)S(1)} %broadcast_multiply_fusion.weight_ref, f32[4,2,2,3,128,128]{5,4,3,2,1,0:T(8,128)S(1)} %get-tuple-element.22.edge_ref, bf16[1,2,2,3,128,128]{5,4,3,2,1,0:T(8,128)(2,1)} %collective-permute-done.refs_0_, ...), custom_call_target="tpu_custom_call" | custom-call | flops 1024 | bytes 1024 | tf_op jit(solution)/shard_map/pallas_call | solution.py:241
  35.4 4.8 %all_to_all.5.found_ref = f32[4,16,40,128]{3,2,1,0:T(8,128)S(1)} all-to-all(f32[4,16,40,128]{3,2,1,0:T(8,128)S(1)} %shard_map.32), channel_id=1, replica_groups={{0,8},{16,24},{1,9},{17,25},{2,10},{18,26},{3,11},{19,27},{4,12},{20,28..., dimensions={0} | all-to-all | bytes 2621440 | tf_op jit(solution)/shard_map/all_to_all | solution.py:494
  40.2 1.4 %shard_map.33 = (f32[1,16,40,128]{3,2,1,0:T(8,128)}, f32[1,16,40,128]{3,2,1,0:T(8,128)S(1)}) custom-call(s32[2]{0:T(128)S(1)} %pad_add_fusion.1.side_ref, f32[4,16,40,128]{3,2,1,0:T(8,128)S(1)} %all_to_all.5.found_ref), custom_call_target="tpu_custom_call" | custom-call | flops 1024 | bytes 1024 | tf_op jit(solution)/shard_map/pallas_call | solution.py:458
  41.6 1.5 %collective-permute-start.8 = (f32[1,16,40,128]{3,2,1,0:T(8,128)}, f32[1,16,40,128]{3,2,1,0:T(8,128)}, u32[]{:S(2)}, u32[]{:S(2)}) collective-permute-start(f32[1,16,40,128]{3,2,1,0:T(8,128)} %get-tuple-element.29), channel_id=1, source_target_pairs={{0,16},{8,24},{16,0},{24,8},{1,17},{9,25},{17,1},{25,9},{2,18},{10... | collective-permute-start | bytes 983048 | tf_op jit(solution)/shard_map/ppermute | solution.py:495
  43.1 1.9 %shard_map.34.edge_ref = f32[4,2,2,3,128,128]{5,4,3,2,1,0:T(8,128)S(1)} custom-call(f32[4,2,2,3,128,128]{5,4,3,2,1,0:T(8,128)} %get-tuple-element.21.refs_0_, f32[1,16,40,128]{3,2,1,0:T(8,128)S(1)} %get-tuple-element.24.refs_1_.keep_ref), custom_call_target="tpu_custom_call" | custom-call | flops 1024 | bytes 1024 | tf_op jit(solution)/shard_map/pallas_call | solution.py:263
  45.0 8.0 %collective-permute-done.2.refs_0_ = bf16[1,2,2,3,128,128]{5,4,3,2,1,0:T(8,128)(2,1)S(1)} collective-permute-done((bf16[1,2,2,3,128,128]{5,4,3,2,1,0:T(8,128)(2,1)S(1)}, bf16[1,2,2,3,128,128]{5,4,3,2,1,0:T(8,128)(2,1)S(1)}, u32[]{:S(2)}, u32[]{:S(2)}) %collective-permute-start.2) | collective-permute-done | bytes 393248 | tf_op jit(solution)/shard_map/ppermute | solution.py:425
  53.0 25.2 %collective-permute-done.3.refs_1_ = bf16[3,2,2,3,128,128]{5,4,3,2,1,0:T(8,128)(2,1)S(1)} collective-permute-done((bf16[3,2,2,3,128,128]{5,4,3,2,1,0:T(8,128)(2,1)S(1)}, bf16[3,2,2,3,128,128]{5,4,3,2,1,0:T(8,128)(2,1)S(1)}, u32[]{:S(2)}, u32[]{:S(2)}) %collective-permute-start.3) | collective-permute-done | bytes 1179680 | tf_op jit(solution)/shard_map/ppermute | solution.py:425
  78.2 1.0 %shard_map.35 = (f32[2,40,128]{2,1,0:T(8,128)S(1)}, f32[2,40,128]{2,1,0:T(8,128)S(1)}) custom-call(s32[2]{0:T(128)S(1)} %pad_add_fusion.1.side_ref, f32[1,4]{1,0:T(1,128)S(1)} %broadcast_multiply_fusion.weight_ref, f32[4,2,2,3,128,128]{5,4,3,2,1,0:T(8,128)S(1)} %shard_map.34.edge_ref, bf16[1,2,2,3,128,128]{5,4,3,2,1,0:T(8,128)(2,1)S(1)} %collective-permute-done.2.refs_0_, ...), custom_call_target="tpu_custom_call" | custom-call | flops 1024 | bytes 1024 | tf_op jit(solution)/shard_map/pallas_call | solution.py:295
  79.2 0.1 collective-permute-start.4
  79.3 0.0 collective-permute-done.8.found_ref
  79.3 1.0 %shard_map.37 = (f32[16,40,128]{2,1,0:T(8,128)S(1)}, f32[3,40,128]{2,1,0:T(8,128)S(1)}, f32[3,40,128]{2,1,0:T(8,128)S(1)}) custom-call(s32[2]{0:T(128)S(1)} %pad_add_fusion.1.side_ref, f32[1,16,40,128]{3,2,1,0:T(8,128)S(1)} %get-tuple-element.24.refs_1_.keep_ref, f32[1,16,40,128]{3,2,1,0:T(8,128)} %collective-permute-done.8.found_ref), custom_call_target="tpu_custom_call" | custom-call | flops 1024 | bytes 1024 | tf_op jit(solution)/shard_map/pallas_call | solution.py:479
  80.3 2.5 %collective-permute-start.9 = (f32[3,40,128]{2,1,0:T(8,128)S(1)}, f32[3,40,128]{2,1,0:T(8,128)S(1)}, u32[]{:S(2)}, u32[]{:S(2)}) collective-permute-start(f32[3,40,128]{2,1,0:T(8,128)S(1)} %get-tuple-element.31), channel_id=1, source_target_pairs={{0,1},{1,0},{2,3},{3,2},{4,5},{5,4},{6,7},{7,6},{8,9},{9,8},{10,11... | collective-permute-start | bytes 184328 | tf_op jit(solution)/shard_map/ppermute | solution.py:425
  82.9 0.7 collective-permute-start.10
  83.5 0.1 pad_add_fusion.place_ref
  83.6 0.0 collective-permute-done.4.found_ref
  83.6 1.6 %collective-permute-start.5 = (f32[40,128]{1,0:T(8,128)S(1)}, f32[40,128]{1,0:T(8,128)S(1)}, u32[]{:S(2)}, u32[]{:S(2)}) collective-permute-start(f32[40,128]{1,0:T(8,128)S(1)} %get-tuple-element.28), channel_id=1, source_target_pairs={{0,16},{8,24},{16,0},{24,8},{1,17},{9,25},{17,1},{25,9},{2,18},{10... | collective-permute-start | bytes 61448 | tf_op jit(solution)/shard_map/ppermute | solution.py:437
  85.2 4.3 %collective-permute-start.7 = (f32[40,128]{1,0:T(8,128)S(1)}, f32[40,128]{1,0:T(8,128)S(1)}, u32[]{:S(2)}, u32[]{:S(2)}) collective-permute-start(f32[40,128]{1,0:T(8,128)S(1)} %get-tuple-element.28), channel_id=1, source_target_pairs={{0,17},{1,16},{2,19},{3,18},{4,21},{5,20},{6,23},{7,22},{8,25},{9,... | collective-permute-start | bytes 61448 | tf_op jit(solution)/shard_map/ppermute | solution.py:439
  89.4 0.0 collective-permute-start.6
  89.5 0.0 collective-permute-done.9.near_ref
  89.5 0.0 collective-permute-done.10.far_ref
  89.5 1.4 %shard_map.38.before_ref = f32[16,32,128]{2,1,0:T(8,128)S(1)} custom-call(s32[3]{0:T(128)S(1)} %pad_add_fusion.place_ref, f32[16,40,128]{2,1,0:T(8,128)S(1)} %get-tuple-element.30.base_ref, f32[3,40,128]{2,1,0:T(8,128)S(1)} %collective-permute-done.9.near_ref, f32[3,40,128]{2,1,0:T(8,128)S(1)} %collective-permute-done.10.far_ref), custom_call_target="tpu_custom_call" | custom-call | flops 10000000000 | bytes 1024 | tf_op jit(solution)/shard_map/pallas_call | solution.py:378
  90.8 0.0 collective-permute-done.5.own_refs_1_
  90.9 2.4 %collective-permute-done.6.beyond_refs_0_ = f32[40,128]{1,0:T(8,128)S(1)} collective-permute-done((f32[40,128]{1,0:T(8,128)S(1)}, f32[40,128]{1,0:T(8,128)S(1)}, u32[]{:S(2)}, u32[]{:S(2)}) %collective-permute-start.6) | collective-permute-done | bytes 20512 | tf_op jit(solution)/shard_map/ppermute | solution.py:438
  93.2 0.0 collective-permute-done.7.beyond_refs_1_
  93.2 1.5 %shard_map.39 = f32[16,32,128]{2,1,0:T(8,128)} custom-call(s32[3]{0:T(128)S(1)} %pad_add_fusion.place_ref, f32[40,128]{1,0:T(8,128)S(1)} %get-tuple-element.27.own_refs_0_, f32[40,128]{1,0:T(8,128)S(1)} %collective-permute-done.5.own_refs_1_, f32[40,128]{1,0:T(8,128)S(1)} %collective-permute-done.6.beyond_refs_0_, ...), custom_call_target="tpu_custom_call" | custom-call | flops 1024 | bytes 1024 | tf_op jit(solution)/shard_map/pallas_call | solution.py:412
  (2 shorter events, 0.0 us)
Async XLA Ops:
  2.3 10.6 %copy-start = (f32[1,4]{1,0:T(1,128)S(1)}, f32[1,4]{1,0:T(1,128)}, u32[]{:S(2)}) copy-start(f32[1,4]{1,0:T(1,128)} %param.3) | copy-start | bytes 52
  4.9 28.6 %collective-permute-start.1 = (bf16[3,2,2,3,128,128]{5,4,3,2,1,0:T(8,128)(2,1)}, bf16[3,2,2,3,128,128]{5,4,3,2,1,0:T(8,128)(2,1)}, u32[]{:S(2)}, u32[]{:S(2)}) collective-permute-start(bf16[3,2,2,3,128,128]{5,4,3,2,1,0:T(8,128)(2,1)} %get-tuple-element.20.refs_1_), channel_id=1, source_target_pairs={{1,2},{2,1},{3,4},{4,3},{5,6},{6,5},{9,10},{10,9},{11,12},{12,11},... | collective-permute-start | bytes 3538952 | tf_op jit(solution)/shard_map/ppermute | solution.py:425
  6.6 46.4 %collective-permute-start.2 = (bf16[1,2,2,3,128,128]{5,4,3,2,1,0:T(8,128)(2,1)S(1)}, bf16[1,2,2,3,128,128]{5,4,3,2,1,0:T(8,128)(2,1)S(1)}, u32[]{:S(2)}, u32[]{:S(2)}) collective-permute-start(bf16[1,2,2,3,128,128]{5,4,3,2,1,0:T(8,128)(2,1)S(1)} %shard_map.28.refs_0_), channel_id=1, source_target_pairs={{0,1},{1,0},{2,3},{3,2},{4,5},{5,4},{6,7},{7,6},{8,9},{9,8},{10,11... | collective-permute-start | bytes 1179656 | tf_op jit(solution)/shard_map/ppermute | solution.py:425
  11.4 66.9 %collective-permute-start.3 = (bf16[3,2,2,3,128,128]{5,4,3,2,1,0:T(8,128)(2,1)S(1)}, bf16[3,2,2,3,128,128]{5,4,3,2,1,0:T(8,128)(2,1)S(1)}, u32[]{:S(2)}, u32[]{:S(2)}) collective-permute-start(bf16[3,2,2,3,128,128]{5,4,3,2,1,0:T(8,128)(2,1)S(1)} %shard_map.29.refs_0_), channel_id=1, source_target_pairs={{0,1},{1,0},{2,3},{3,2},{4,5},{5,4},{6,7},{7,6},{8,9},{9,8},{10,11... | collective-permute-start | bytes 3538952 | tf_op jit(solution)/shard_map/ppermute | solution.py:425
  11.4 22.1 %collective-permute-start = (bf16[1,2,2,3,128,128]{5,4,3,2,1,0:T(8,128)(2,1)}, bf16[1,2,2,3,128,128]{5,4,3,2,1,0:T(8,128)(2,1)}, u32[]{:S(2)}, u32[]{:S(2)}) collective-permute-start(bf16[1,2,2,3,128,128]{5,4,3,2,1,0:T(8,128)(2,1)} %get-tuple-element.19.refs_0_), channel_id=1, source_target_pairs={{1,2},{2,1},{3,4},{4,3},{5,6},{6,5},{9,10},{10,9},{11,12},{12,11},... | collective-permute-start | bytes 1179656 | tf_op jit(solution)/shard_map/ppermute | solution.py:425
  41.6 37.7 %collective-permute-start.8 = (f32[1,16,40,128]{3,2,1,0:T(8,128)}, f32[1,16,40,128]{3,2,1,0:T(8,128)}, u32[]{:S(2)}, u32[]{:S(2)}) collective-permute-start(f32[1,16,40,128]{3,2,1,0:T(8,128)} %get-tuple-element.29), channel_id=1, source_target_pairs={{0,16},{8,24},{16,0},{24,8},{1,17},{9,25},{17,1},{25,9},{2,18},{10... | collective-permute-start | bytes 983048 | tf_op jit(solution)/shard_map/ppermute | solution.py:495
  79.2 4.4 %collective-permute-start.4 = (f32[2,40,128]{2,1,0:T(8,128)S(1)}, f32[2,40,128]{2,1,0:T(8,128)S(1)}, u32[]{:S(2)}, u32[]{:S(2)}) collective-permute-start(f32[2,40,128]{2,1,0:T(8,128)S(1)} %get-tuple-element.26), channel_id=1, source_target_pairs={{0,8},{8,0},{16,24},{24,16},{1,9},{9,1},{17,25},{25,17},{2,10},{10... | collective-permute-start | bytes 122888 | tf_op jit(solution)/shard_map/ppermute | solution.py:434
  80.3 9.1 %collective-permute-start.9 = (f32[3,40,128]{2,1,0:T(8,128)S(1)}, f32[3,40,128]{2,1,0:T(8,128)S(1)}, u32[]{:S(2)}, u32[]{:S(2)}) collective-permute-start(f32[3,40,128]{2,1,0:T(8,128)S(1)} %get-tuple-element.31), channel_id=1, source_target_pairs={{0,1},{1,0},{2,3},{3,2},{4,5},{5,4},{6,7},{7,6},{8,9},{9,8},{10,11... | collective-permute-start | bytes 184328 | tf_op jit(solution)/shard_map/ppermute | solution.py:425
  82.9 6.6 %collective-permute-start.10 = (f32[3,40,128]{2,1,0:T(8,128)S(1)}, f32[3,40,128]{2,1,0:T(8,128)S(1)}, u32[]{:S(2)}, u32[]{:S(2)}) collective-permute-start(f32[3,40,128]{2,1,0:T(8,128)S(1)} %get-tuple-element.32), channel_id=1, source_target_pairs={{1,2},{2,1},{3,4},{4,3},{5,6},{6,5},{9,10},{10,9},{11,12},{12,11},... | collective-permute-start | bytes 184328 | tf_op jit(solution)/shard_map/ppermute | solution.py:425
  83.6 7.2 %collective-permute-start.5 = (f32[40,128]{1,0:T(8,128)S(1)}, f32[40,128]{1,0:T(8,128)S(1)}, u32[]{:S(2)}, u32[]{:S(2)}) collective-permute-start(f32[40,128]{1,0:T(8,128)S(1)} %get-tuple-element.28), channel_id=1, source_target_pairs={{0,16},{8,24},{16,0},{24,8},{1,17},{9,25},{17,1},{25,9},{2,18},{10... | collective-permute-start | bytes 61448 | tf_op jit(solution)/shard_map/ppermute | solution.py:437
  85.2 8.0 %collective-permute-start.7 = (f32[40,128]{1,0:T(8,128)S(1)}, f32[40,128]{1,0:T(8,128)S(1)}, u32[]{:S(2)}, u32[]{:S(2)}) collective-permute-start(f32[40,128]{1,0:T(8,128)S(1)} %get-tuple-element.28), channel_id=1, source_target_pairs={{0,17},{1,16},{2,19},{3,18},{4,21},{5,20},{6,23},{7,22},{8,25},{9,... | collective-permute-start | bytes 61448 | tf_op jit(solution)/shard_map/ppermute | solution.py:439
  89.4 3.8 %collective-permute-start.6 = (f32[40,128]{1,0:T(8,128)S(1)}, f32[40,128]{1,0:T(8,128)S(1)}, u32[]{:S(2)}, u32[]{:S(2)}) collective-permute-start(f32[40,128]{1,0:T(8,128)S(1)} %get-tuple-element.27.own_refs_0_), channel_id=1, source_target_pairs={{0,1},{1,0},{2,3},{3,2},{4,5},{5,4},{6,7},{7,6},{8,9},{9,8},{10,11... | collective-permute-start | bytes 61448 | tf_op jit(solution)/shard_map/ppermute | solution.py:438
